TPU v7x, 32 devices: a whole 2x2x4 slice. The times are simulated.
32 devices in a mesh: bin: 8 (over y, x, core), shard: 4 (over z).
Axes of the slice: x: 2, y: 2, z: 4, core: 2. Of those that a mesh axis runs over, the one named last changes fastest.
Arguments:
- block_input: bfloat16 [16384, 1152], P(('bin', 'shard')), may hold values from -6 to 6
- label_embed: float32 [64, 1152], P('bin'), may hold values from -6 to 6
- time_index: int32 [64], P('bin'), may hold values from 0 to 999
- segment_ids: int32 [16384], P('bin'), may hold values from 0 to 7, as said below
- ada_weight: bfloat16 [1152, 6912], replicated, may hold values from -0.1875 to 0.1875
- ada_bias: float32 [6912], replicated, may hold values from -2 to 2
- qkv_weight: bfloat16 [1152, 3456], P('bin', 'shard'), may hold values from -0.1875 to 0.1875
- qv_bias: float32 [2304], replicated, may hold values from -2 to 2
- proj_weight: bfloat16 [1152, 1152], P('bin', 'shard'), may hold values from -0.75 to 0.75
- proj_bias: float32 [1152], replicated, may hold values from -2 to 2
- up_weight: bfloat16 [1152, 4608], P('bin', 'shard'), may hold values from -0.1875 to 0.1875
- up_bias: float32 [4608], replicated, may hold values from -2 to 2
- down_weight: bfloat16 [4608, 1152], P('bin', 'shard'), may hold values from -0.09375 to 0.09375
- down_bias: float32 [1152], replicated, may hold values from -2 to 2
- bin_weight: float32 [8], P('bin'), may hold values from 0.3 to 3
- out_cotangent: bfloat16 [16384, 1152], P(('bin', 'shard')), may hold values from -6 to 6
Outputs:
- block_output: float32 [16384, 1152], P(('bin', 'shard'))
- grad_input: float32 [16384, 1152], P(('bin', 'shard'))
- grad_label: float32 [64, 1152], P('bin')
- grad_ada_weight: float32 [1152, 6912], P(None, ('bin', 'shard'))
- grad_ada_bias: float32 [6912], P(('bin', 'shard'))
- grad_qkv_weight: float32 [1152, 3456], P('bin', 'shard')
- grad_qv_bias: float32 [2304], replicated
- grad_proj_weight: float32 [1152, 1152], P('bin', 'shard')
- grad_proj_bias: float32 [1152], replicated
- grad_up_weight: float32 [1152, 4608], P('bin', 'shard')
- grad_up_bias: float32 [4608], replicated
- grad_down_weight: float32 [4608, 1152], P('bin', 'shard')
- grad_down_bias: float32 [1152], replicated
Inputs may be any that keep to these rules, and one draw needn't show every extreme that they name: `segment_ids`: within each bin's group of 2048 tokens the ids number its images from 0 in order of their tokens; every image is 256 or 1024 consecutive tokens, and both sizes occur in every draw. Slots at or above a group's image count are unused.
All inputs are finite; a program needn't handle non-finite values.
Results may differ from a plain program's by a relative error of at most 0.017.
Values may be sent and summed in bfloat16 or wider, within the bound.
No kernel may reach another device: no remote copies, remote signals or barrier semaphores. Data moves between devices by JAX's collectives and lax.ppermute only.
A program may use at most 384 MiB of HBM per device.

v0:
```python
import math

import jax
import jax.numpy as jnp
from jax import lax
from jax.sharding import PartitionSpec as P

HEADS = 16
HEAD_DIM = 72


def time_embed(time_index, width):
    half_width = width // 2
    freqs = jnp.exp(-math.log(10000.0) * jnp.arange(half_width, dtype=jnp.float32) / half_width)
    angles = time_index.astype(jnp.float32)[:, None] * freqs[None, :]
    return jnp.concatenate([jnp.cos(angles), jnp.sin(angles)], axis=1)


def layer_norm(value):
    center = value - jnp.mean(value, axis=1, keepdims=True)
    inverse = lax.rsqrt(jnp.mean(center * center, axis=1, keepdims=True) + 1e-06)
    return (center * inverse, inverse)


def norm_back(normed, inverse, grad_normed):
    mean_grad = jnp.mean(grad_normed, axis=1, keepdims=True)
    mean_cross = jnp.mean(grad_normed * normed, axis=1, keepdims=True)
    return inverse * (grad_normed - mean_grad - normed * mean_cross)


def matmul(left, right):
    return jnp.dot(left, right, preferred_element_type=jnp.float32)


def contract_rows(left, right):
    return lax.dot_general(
        left, right, (((0,), (0,)), ((), ())), preferred_element_type=jnp.float32
    )


def contract_cols(left, right):
    return lax.dot_general(
        left, right, (((1,), (1,)), ((), ())), preferred_element_type=jnp.float32
    )


def head_blocks(matrix):
    group_heads = 4
    return matrix.reshape(matrix.shape[0], HEADS // group_heads, group_heads, HEAD_DIM).transpose(
        1, 0, 2, 3
    )


def merge_heads(blocks):
    return blocks.transpose(1, 0, 2, 3).reshape(blocks.shape[1], -1)


def block_scores(query, keys, same):
    scores = jnp.einsum("qhd,khd->hqk", query, keys, preferred_element_type=jnp.float32)
    scores = scores * (1.0 / math.sqrt(HEAD_DIM))
    return jnp.where(same[None], scores, -1e30)


def attend_forward(query_low, keys_all, values_all, same):

    def one_block(operands):
        query, keys, values = operands
        scores = block_scores(query, keys, same)
        top = jnp.max(scores, axis=2, keepdims=True)
        expo = jnp.exp(scores - top)
        total = jnp.sum(expo, axis=2, keepdims=True)
        probs = (expo / total).astype(jnp.bfloat16)
        output = jnp.einsum("hqk,khd->qhd", probs, values, preferred_element_type=jnp.float32)
        return (output, (top + jnp.log(total))[:, :, 0])

    outputs, log_total = lax.map(
        one_block, (head_blocks(query_low), head_blocks(keys_all), head_blocks(values_all))
    )
    return (merge_heads(outputs), log_total)


def attend_backward(query_low, keys_all, values_all, same, log_total, grad_heads):
    scale = 1.0 / math.sqrt(HEAD_DIM)

    def one_block(operands):
        query, keys, values, log_block, grad_block = operands
        scores = block_scores(query, keys, same)
        probs = jnp.exp(scores - log_block[:, :, None])
        grad_probs = jnp.einsum(
            "qhd,khd->hqk", grad_block, values, preferred_element_type=jnp.float32
        )
        delta = jnp.sum(grad_probs * probs, axis=2, keepdims=True)
        grad_scores = (probs * (grad_probs - delta)).astype(jnp.bfloat16)
        grad_query = (
            jnp.einsum("hqk,khd->qhd", grad_scores, keys, preferred_element_type=jnp.float32)
            * scale
        )
        grad_keys = (
            jnp.einsum("hqk,qhd->khd", grad_scores, query, preferred_element_type=jnp.float32)
            * scale
        )
        grad_values = jnp.einsum(
            "hqk,qhd->khd",
            probs.astype(jnp.bfloat16),
            grad_block,
            preferred_element_type=jnp.float32,
        )
        return (grad_query, grad_keys, grad_values)

    grad_query, grad_keys, grad_values = lax.map(
        one_block,
        (
            head_blocks(query_low),
            head_blocks(keys_all),
            head_blocks(values_all),
            log_total,
            head_blocks(grad_heads),
        ),
    )
    return (merge_heads(grad_query), merge_heads(grad_keys), merge_heads(grad_values))


def collect_weights(local_weights):
    wider = (
        lax.all_gather(local_weights[0], "shard", axis=1, tiled=True),
        lax.all_gather(local_weights[1], "shard", axis=1, tiled=True),
        lax.all_gather(local_weights[2], "shard", axis=1, tiled=True),
        lax.all_gather(local_weights[3], "shard", axis=1, tiled=True),
    )
    return (
        lax.all_gather(wider[0], "bin", axis=0, tiled=True),
        lax.all_gather(wider[1], "bin", axis=0, tiled=True),
        lax.all_gather(wider[2], "bin", axis=0, tiled=True),
        lax.all_gather(wider[3], "bin", axis=0, tiled=True),
    )


def forward_pass(full_weights, tokens, per_token, biases, segment_ids, own_segments):
    qkv_full, proj_full, up_full, down_full = full_weights
    qv_bias, proj_bias, up_bias, down_bias = biases
    width = tokens.shape[1]
    shift_a, scale_a, gate_a, shift_m, scale_m, gate_m = jnp.split(per_token, 6, axis=1)
    normed, inverse = layer_norm(tokens)
    attn_in = (normed * (1.0 + scale_a) + shift_a).astype(jnp.bfloat16)
    qkv_bias = jnp.concatenate([qv_bias[:width], jnp.zeros((width,), jnp.float32), qv_bias[width:]])
    qkv_low = (matmul(attn_in, qkv_full) + qkv_bias).astype(jnp.bfloat16)
    query_low = qkv_low[:, :width]
    keys_all, values_all = (
        lax.all_gather(qkv_low[:, width : 2 * width], "shard", axis=0, tiled=True),
        lax.all_gather(qkv_low[:, 2 * width :], "shard", axis=0, tiled=True),
    )
    same = own_segments[:, None] == segment_ids[None, :]
    heads_out, log_total = attend_forward(query_low, keys_all, values_all, same)
    heads_low = heads_out.astype(jnp.bfloat16)
    attn_out = matmul(heads_low, proj_full) + proj_bias
    middle = tokens + gate_a * attn_out
    normed_mlp, inverse_mlp = layer_norm(middle)
    mlp_in = (normed_mlp * (1.0 + scale_m) + shift_m).astype(jnp.bfloat16)
    pre_act = matmul(mlp_in, up_full) + up_bias
    act_low = jax.nn.gelu(pre_act, approximate=True).astype(jnp.bfloat16)
    mlp_out = matmul(act_low, down_full) + down_bias
    result = middle + gate_m * mlp_out
    saved = (
        normed,
        inverse,
        attn_in,
        query_low,
        keys_all,
        values_all,
        log_total,
        heads_low,
        attn_out,
        normed_mlp,
        inverse_mlp,
        mlp_in,
        pre_act,
        act_low,
        mlp_out,
        same,
    )
    return (result, saved)


def per_device(
    block_input,
    label_embed,
    time_index,
    segment_ids,
    ada_weight,
    ada_bias,
    qkv_weight,
    qv_bias,
    proj_weight,
    proj_bias,
    up_weight,
    up_bias,
    down_weight,
    down_bias,
    bin_weight,
    out_cotangent,
):
    tokens = block_input.astype(jnp.float32)
    width = tokens.shape[1]
    tok_count = tokens.shape[0]
    slots = label_embed.shape[0]
    own_segments = lax.dynamic_slice_in_dim(
        segment_ids, lax.axis_index("shard") * tok_count, tok_count
    )
    onehot = (own_segments[:, None] == jnp.arange(slots, dtype=jnp.int32)[None, :]).astype(
        jnp.float32
    )
    cond = label_embed + time_embed(time_index, width)
    cond_low = jax.nn.silu(cond).astype(jnp.bfloat16)
    modul = matmul(cond_low, ada_weight) + ada_bias
    per_token = jnp.dot(
        onehot, modul, precision=lax.Precision.HIGHEST, preferred_element_type=jnp.float32
    )
    biases = (qv_bias, proj_bias, up_bias, down_bias)
    local_weights = (qkv_weight, proj_weight, up_weight, down_weight)
    full_weights = collect_weights(local_weights)
    result, saved = forward_pass(full_weights, tokens, per_token, biases, segment_ids, own_segments)
    grad_out = out_cotangent.astype(jnp.float32) * bin_weight[0]
    local_again, tokens_again, per_token_again, grad_out = lax.optimization_barrier(
        (local_weights, tokens, per_token, grad_out)
    )
    full_weights = collect_weights(local_again)
    saved = forward_pass(
        full_weights, tokens_again, per_token_again, biases, segment_ids, own_segments
    )[1]
    (
        normed,
        inverse,
        attn_in,
        query_low,
        keys_all,
        values_all,
        log_total,
        heads_low,
        attn_out,
        normed_mlp,
        inverse_mlp,
        mlp_in,
        pre_act,
        act_low,
        mlp_out,
        same,
    ) = saved
    qkv_full, proj_full, up_full, down_full = full_weights
    shift_a, scale_a, gate_a, shift_m, scale_m, gate_m = jnp.split(per_token, 6, axis=1)
    grad_mlp = (grad_out * gate_m).astype(jnp.bfloat16)
    grad_down_w = contract_rows(act_low, grad_mlp)
    grad_down_b = jnp.sum(grad_mlp.astype(jnp.float32), axis=0)
    grad_act = contract_cols(grad_mlp, down_full)
    gelu_back = jax.vjp(lambda value: jax.nn.gelu(value, approximate=True), pre_act)[1]
    grad_pre = gelu_back(grad_act)[0].astype(jnp.bfloat16)
    grad_up_w = contract_rows(mlp_in, grad_pre)
    grad_up_b = jnp.sum(grad_pre.astype(jnp.float32), axis=0)
    grad_in_mlp = contract_cols(grad_pre, up_full)
    grad_mid = grad_out + norm_back(normed_mlp, inverse_mlp, grad_in_mlp * (1.0 + scale_m))
    grad_attn = (grad_mid * gate_a).astype(jnp.bfloat16)
    grad_proj_w = contract_rows(heads_low, grad_attn)
    grad_proj_b = jnp.sum(grad_attn.astype(jnp.float32), axis=0)
    grad_heads = contract_cols(grad_attn, proj_full).astype(jnp.bfloat16)
    grad_query, grad_keys_all, grad_values_all = attend_backward(
        query_low, keys_all, values_all, same, log_total, grad_heads
    )
    grad_keys, grad_values = (
        lax.psum_scatter(
            grad_keys_all.astype(jnp.bfloat16), "shard", scatter_dimension=0, tiled=True
        ).astype(jnp.float32),
        lax.psum_scatter(
            grad_values_all.astype(jnp.bfloat16), "shard", scatter_dimension=0, tiled=True
        ).astype(jnp.float32),
    )
    grad_qkv = jnp.concatenate(
        [
            grad_query.astype(jnp.bfloat16),
            grad_keys.astype(jnp.bfloat16),
            grad_values.astype(jnp.bfloat16),
        ],
        axis=1,
    )
    grad_qkv_w = contract_rows(attn_in, grad_qkv)
    grad_qkv_wide = grad_qkv.astype(jnp.float32)
    grad_qv_b = jnp.concatenate(
        [jnp.sum(grad_qkv_wide[:, :width], axis=0), jnp.sum(grad_qkv_wide[:, 2 * width :], axis=0)]
    )
    grad_in_attn = contract_cols(grad_qkv, qkv_full)
    grad_input = grad_mid + norm_back(normed, inverse, grad_in_attn * (1.0 + scale_a))
    grad_tok_mod = jnp.concatenate(
        [
            grad_in_attn,
            grad_in_attn * normed,
            grad_mid * attn_out,
            grad_in_mlp,
            grad_in_mlp * normed_mlp,
            grad_out * mlp_out,
        ],
        axis=1,
    )
    grad_mod_part = lax.dot_general(
        onehot,
        grad_tok_mod,
        (((0,), (0,)), ((), ())),
        precision=lax.Precision.HIGHEST,
        preferred_element_type=jnp.float32,
    )
    grad_mod = lax.psum(grad_mod_part.astype(jnp.bfloat16), "shard")
    grad_cond_act = contract_cols(grad_mod, ada_weight)
    silu_back = jax.vjp(jax.nn.silu, cond)[1]
    grad_label = silu_back(grad_cond_act)[0]
    bins_count = lax.axis_size("bin")
    shard_count = lax.axis_size("shard")
    own_width = grad_mod.shape[1] // (bins_count * shard_count)
    mod_view = grad_mod.reshape(slots, bins_count, shard_count, own_width)
    own_columns = lax.dynamic_index_in_dim(
        mod_view, lax.axis_index("shard"), axis=2, keepdims=False
    )
    own_columns = own_columns.reshape(slots, bins_count * own_width)
    cond_rows = jnp.concatenate([cond_low, jnp.ones((slots, 1), jnp.bfloat16)], axis=1)
    ada_terms = contract_rows(cond_rows, own_columns).reshape(width + 1, bins_count, own_width)
    ada_sums = lax.psum_scatter(ada_terms, "bin", scatter_dimension=1, tiled=True)[:, 0, :]
    grad_ada_w = ada_sums[:width]
    grad_ada_b = ada_sums[width]
    weight_grads = (grad_qkv_w, grad_proj_w, grad_up_w, grad_down_w)
    shorter = (
        lax.psum_scatter(weight_grads[0], "bin", scatter_dimension=0, tiled=True),
        lax.psum_scatter(weight_grads[1], "bin", scatter_dimension=0, tiled=True),
        lax.psum_scatter(weight_grads[2], "bin", scatter_dimension=0, tiled=True),
        lax.psum_scatter(weight_grads[3], "bin", scatter_dimension=0, tiled=True),
    )
    grads_local = (
        lax.psum_scatter(
            shorter[0].astype(jnp.bfloat16), "shard", scatter_dimension=1, tiled=True
        ).astype(jnp.float32),
        lax.psum_scatter(
            shorter[1].astype(jnp.bfloat16), "shard", scatter_dimension=1, tiled=True
        ).astype(jnp.float32),
        lax.psum_scatter(
            shorter[2].astype(jnp.bfloat16), "shard", scatter_dimension=1, tiled=True
        ).astype(jnp.float32),
        lax.psum_scatter(
            shorter[3].astype(jnp.bfloat16), "shard", scatter_dimension=1, tiled=True
        ).astype(jnp.float32),
    )
    bias_sums = lax.psum((grad_qv_b, grad_proj_b, grad_up_b, grad_down_b), ("bin", "shard"))
    return (
        result,
        grad_input,
        grad_label,
        grad_ada_w,
        grad_ada_b,
        grads_local[0],
        bias_sums[0],
        grads_local[1],
        bias_sums[1],
        grads_local[2],
        bias_sums[2],
        grads_local[3],
        bias_sums[3],
    )


def solution(mesh):
    placed = (
        P(("bin", "shard"), None),
        P("bin", None),
        P("bin"),
        P("bin"),
        P(),
        P(),
        P("bin", "shard"),
        P(),
        P("bin", "shard"),
        P(),
        P("bin", "shard"),
        P(),
        P("bin", "shard"),
        P(),
        P("bin"),
        P(("bin", "shard"), None),
    )
    return jax.shard_map(
        per_device,
        mesh=mesh,
        in_specs=placed,
        out_specs=(
            P(("bin", "shard"), None),
            P(("bin", "shard"), None),
            P("bin", None),
            P(None, ("bin", "shard")),
            P(("bin", "shard")),
            P("bin", "shard"),
            P(),
            P("bin", "shard"),
            P(),
            P("bin", "shard"),
            P(),
            P("bin", "shard"),
            P(),
        ),
        check_vma=False,
    )
```

profile of v0, /device:TPU:8, one launch (start us, length us, event | category | flops | bytes accessed | tf_op | source)
XLA Modules:
  0.0 2135.8 jit_solution(2418818417426220248)
XLA Ops:
  19.5 8.9 fusion.134
  30.0 21.3 all-gather.2
  58.6 48.9 %all-gather.37.cloned.1.call-done = bf16[1152,3456]{1,0:T(8,128)(2,1)} async-done(((bf16[144,3456]{1,0:T(8,128)(2,1)}), bf16[1152,3456]{1,0:T(8,128)(2,1)}) %all-gather.37.cloned.1.call-update) | async-done | bytes 7962640 | tf_op jit(solution)/shard_map/all_gather | solution.py:131
  107.5 8.3 add_convert_fusion
  118.4 19.5 all-gather.3
  139.3 9.3 all-gather.49.cloned.1.call-done
  148.6 35.7 %all-gather.45.cloned.1.call-done = bf16[576,1152]{0,1:T(8,128)(2,1)} async-done(((bf16[576,288]{0,1:T(8,128)(2,1)}), bf16[576,1152]{0,1:T(8,128)(2,1)}) %all-gather.45.cloned.1.call-update) | async-done | bytes 1327120 | tf_op jit(solution)/shard_map/all_gather | solution.py:128
  187.0 32.5 %all-gather = bf16[4,864,144]{1,2,0:T(8,128)(2,1)S(1)} all-gather(bf16[1,864,144]{1,2,0:T(8,128)(2,1)S(1)} %bitcast.272), channel_id=1, replica_groups=mesh['bin'=8,'shard'=4] {'shard'}, dimensions={0}, use_global_device_ids=true | all-gather | bytes 1244160 | tf_op jit(solution)/shard_map/all_gather | solution.py:125
  227.0 57.1 %all-gather.39.cloned.1.call-done = bf16[2048,1152]{1,0:T(8,128)(2,1)} async-done(((bf16[512,1152]{1,0:T(8,128)(2,1)}), bf16[2048,1152]{1,0:T(8,128)(2,1)}) %all-gather.39.cloned.1.call-update) | async-done | bytes 4718608 | tf_op jit(solution)/shard_map/all_gather | solution.py:150
  290.8 81.4 %all-gather.41.cloned.1.call-done = bf16[2048,1152]{1,0:T(8,128)(2,1)} async-done(((bf16[512,1152]{1,0:T(8,128)(2,1)}), bf16[2048,1152]{1,0:T(8,128)(2,1)}) %all-gather.41.cloned.1.call-update) | async-done | bytes 4718608 | tf_op jit(solution)/shard_map/all_gather | solution.py:149
  380.1 70.7 %while.40 = (s32[]{:T(128)}, bf16[4,512,4,72]{1,3,2,0:T(8,128)(2,1)}, f32[4,4,512]{2,1,0:T(4,128)}, bf16[4,2048,4,72]{1,3,2,0:T(8,128)(2,1)}, bf16[4,512,4,72]{1...) while((s32[]{:T(128)}, ...), condition=%wide.region_13.14_spmd.clone, body=%wide.region_10.13_spmd.clone.sunk | while | flops 1259337728 | bytes 57848412 | solution.py:76
  462.2 9.7 all-gather.51.cloned.1.call-done
  471.8 13.1 fusion.171
  485.0 52.6 %all-gather.47.cloned.1.call-done = bf16[4608,1152]{1,0:T(8,128)(2,1)} async-done(((bf16[576,1152]{1,0:T(8,128)(2,1)}), bf16[4608,1152]{1,0:T(8,128)(2,1)}) %all-gather.47.cloned.1.call-update) | async-done | bytes 10616848 | tf_op jit(solution)/shard_map/all_gather | solution.py:134
  537.5 17.5 convert_reduce_fusion
  555.0 12.2 fusion.153
  579.7 236.6 %while.41 = (s32[]{:T(128)}, bf16[4,512,4,72]{1,3,2,0:T(8,128)(2,1)}, bf16[4,2048,4,72]{1,3,2,0:T(8,128)(2,1)}, bf16[4,2048,4,72]{1,3,2,0:T(8,128)(2,1)}, bf16[4...) while((s32[]{:T(128)}, ...), condition=%wide.region_20.21_spmd.clone, body=%wide.region_18.20_spmd.clone.sunk | while | flops 3084597248 | bytes 190455024 | solution.py:110
  579.9 9.4 fusion.245
  590.7 13.0 multiply_reduce_fusion.8
  603.7 15.8 multiply_convert_fusion.10
  639.0 9.4 fusion.245
  649.8 12.9 multiply_reduce_fusion.8
  662.7 15.8 multiply_convert_fusion.10
  698.1 9.4 fusion.245
  708.9 12.9 multiply_reduce_fusion.8
  721.8 15.8 multiply_convert_fusion.10
  757.1 9.4 fusion.245
  767.8 12.9 multiply_reduce_fusion.8
  780.7 15.8 multiply_convert_fusion.10
  825.3 11.7 add_convert_fusion.1
  837.1 65.3 %reduce-scatter.20.cloned.1.call-done = bf16[512,1152]{0,1:T(8,128)(2,1)} async-done(((bf16[2048,1152]{0,1:T(8,128)(2,1)}), bf16[512,1152]{0,1:T(8,128)(2,1)}) %reduce-scatter.20.cloned.1.call-update) | async-done | bytes 1179664 | tf_op jit(solution)/shard_map/reduce_scatter | solution.py:268
  902.4 88.1 %reduce-scatter.22.cloned.1.call-done = bf16[512,1152]{0,1:T(8,128)(2,1)} async-done(((bf16[2048,1152]{0,1:T(8,128)(2,1)}), bf16[512,1152]{0,1:T(8,128)(2,1)}) %reduce-scatter.22.cloned.1.call-update) | async-done | bytes 1179664 | tf_op jit(solution)/shard_map/reduce_scatter | solution.py:271
  990.5 11.9 fusion.154
  1014.5 13.9 fusion.113
  1028.4 8.6 convolution_convert_fusion
  1041.6 12.2 fusion.173
  1054.7 14.4 all-gather.1
  1070.5 14.6 fusion.155
  1088.6 33.5 %reduce-scatter.28.cloned.1.call-done = f32[144,1152]{1,0:T(8,128)} async-done(((f32[1152,1152]{1,0:T(8,128)}), f32[144,1152]{1,0:T(8,128)}) %reduce-scatter.28.cloned.1.call-update) | async-done | bytes 663568 | tf_op jit(solution)/shard_map/reduce_scatter | solution.py:328
  1124.4 10.1 fusion.151
  1134.6 24.8 %all-reduce.4.cloned.1.call-done = bf16[8,6912]{1,0:T(8,128)(2,1)} async-done(((bf16[8,6912]{1,0:T(8,128)(2,1)}), bf16[8,6912]{1,0:T(8,128)(2,1)}) %all-reduce.4.cloned.1.call-update) | async-done | bytes 110608 | tf_op jit(solution)/shard_map/psum | solution.py:308
  1167.5 79.8 %all-gather.23.cloned.1.call-done = bf16[2048,1152]{1,0:T(8,128)(2,1)} async-done(((bf16[512,1152]{1,0:T(8,128)(2,1)}), bf16[2048,1152]{1,0:T(8,128)(2,1)}) %all-gather.23.cloned.1.call-update) | async-done | bytes 4718608 | tf_op jit(solution)/shard_map/all_gather | solution.py:150
  1254.0 83.2 %all-gather.25.cloned.1.call-done = bf16[2048,1152]{1,0:T(8,128)(2,1)} async-done(((bf16[512,1152]{1,0:T(8,128)(2,1)}), bf16[2048,1152]{1,0:T(8,128)(2,1)}) %all-gather.25.cloned.1.call-update) | async-done | bytes 4718608 | tf_op jit(solution)/shard_map/all_gather | solution.py:149
  1343.9 135.2 %reduce-scatter.30.cloned.1.call-done = f32[144,4608]{1,0:T(8,128)} async-done(((f32[1152,4608]{1,0:T(8,128)}), f32[144,4608]{1,0:T(8,128)}) %reduce-scatter.30.cloned.1.call-update) | async-done | bytes 2654224 | tf_op jit(solution)/shard_map/reduce_scatter | solution.py:329
  1483.5 89.5 %while.39 = (s32[]{:T(128)}, bf16[4,512,4,72]{1,3,2,0:T(8,128)(2,1)S(1)}, bf16[4,2048,4,72]{1,3,2,0:T(8,128)(2,1)}, bf16[4,512,4,72]{1,3,2,0:T(8,128)(2,1)}, bf1...) while((s32[]{:T(128)}, ...), condition=%wide.region_5.6_spmd.clone, body=%wide.region_2.5_spmd.clone.sunk | while | flops 1234176000 | bytes 38924372 | solution.py:76
  1484.4 11.2 fusion.231
  1495.5 9.0 fusion.232
  1505.2 11.2 fusion.231
  1516.4 9.7 fusion.232
  1526.8 14.3 fusion.231
  1541.1 10.5 fusion.232
  1552.3 11.2 fusion.231
  1563.5 9.5 fusion.232
  1579.6 72.8 %reduce-scatter.32.cloned.1.call-done = f32[576,1152]{1,0:T(8,128)} async-done(((f32[4608,1152]{1,0:T(8,128)}), f32[576,1152]{1,0:T(8,128)}) %reduce-scatter.32.cloned.1.call-update) | async-done | bytes 2654224 | tf_op jit(solution)/shard_map/reduce_scatter | solution.py:330
  1658.3 59.9 %all-gather.35.cloned.1.call-done = bf16[4608,1152]{1,0:T(8,128)(2,1)} async-done(((bf16[576,1152]{1,0:T(8,128)(2,1)}), bf16[4608,1152]{1,0:T(8,128)(2,1)}) %all-gather.35.cloned.1.call-update) | async-done | bytes 10616848 | tf_op jit(solution)/shard_map/all_gather | solution.py:134
  1718.2 65.7 %all-gather.31.cloned.1.call-done = bf16[1152,4608]{1,0:T(8,128)(2,1)} async-done(((bf16[144,4608]{1,0:T(8,128)(2,1)}), bf16[1152,4608]{1,0:T(8,128)(2,1)}) %all-gather.31.cloned.1.call-update) | async-done | bytes 10616848 | tf_op jit(solution)/shard_map/all_gather | solution.py:133
  1783.9 23.3 %fusion.117 = f32[512,1152]{1,0:T(8,128)} fusion(f32[512,1152]{1,0:T(8,128)S(1)} %copy-done.16, bf16[4608,1152]{1,0:T(8,128)(2,1)} %all-gather.35.cloned.1.call-done, f32[512,6912]{1,0:T(8,128)} %fusion.134, bf16[1152,4608]{1,0:T(8,128)(2,1)} %all-gather.31.cloned.1.call-done, f32[4608]{0:T(1024)S(1)} %copy-done.63, f32[1152]{0:T(1024)S(1)} %copy-done.65, ...), kind=kOutput, calls=%fused_computation.126 | convolution fusion | flops 10900537344 | bytes 35422208 | tf_op jit(solution)/shard_map/dot_general | solution.py:32
  1808.9 114.6 %reduce-scatter.26.cloned.1.call-done = f32[144,3456]{1,0:T(8,128)} async-done(((f32[1152,3456]{1,0:T(8,128)}), f32[144,3456]{1,0:T(8,128)}) %reduce-scatter.26.cloned.1.call-update) | async-done | bytes 1990672 | tf_op jit(solution)/shard_map/reduce_scatter | solution.py:327
  1930.1 40.7 %all-reduce.1 = (f32[2304]{0:T(1024)}, f32[1152]{0:T(1024)}, f32[4608]{0:T(1024)}, f32[1152]{0:T(1024)}) all-reduce(f32[2304]{0:T(1024)S(1)} %pad_maximum_fusion.2, f32[1152]{0:T(1024)S(1)} %copy-done.53, f32[4608]{0:T(1024)S(1)} %copy-done.56, f32[1152]{0:T(1024)S(1)} %copy-done.52), channel_id=1, replica_groups=mesh['bin'=8,'shard'=4] {'bin','shard'}, use_global_device_ids=true, to_apply=%region_31.32 | all-reduce | flops 9216 | bytes 73728 | tf_op jit(solution)/shard_map/psum | solution.py:346
  1970.8 10.6 fusion.138
  1981.4 20.4 reduce-scatter.24.cloned.1.call-done
  2005.6 45.4 %reduce-scatter.38.cloned.1.call-done = bf16[1152,144]{1,0:T(8,128)(2,1)} async-done(((bf16[4608,144]{1,0:T(8,128)(2,1)}), bf16[1152,144]{1,0:T(8,128)(2,1)}) %reduce-scatter.38.cloned.1.call-update) | async-done | bytes 331792
  2053.2 32.7 %reduce-scatter.40.cloned.1.call-done = bf16[288,576]{1,0:T(8,128)(2,1)} async-done(((bf16[1152,576]{1,0:T(8,128)(2,1)}), bf16[288,576]{1,0:T(8,128)(2,1)}) %reduce-scatter.40.cloned.1.call-update) | async-done | bytes 331792
  2088.1 38.3 %reduce-scatter.34.cloned.1.call-done = bf16[864,144]{1,0:T(8,128)(2,1)} async-done(((bf16[3456,144]{1,0:T(8,128)(2,1)}), bf16[864,144]{1,0:T(8,128)(2,1)}) %reduce-scatter.34.cloned.1.call-update) | async-done | bytes 248848
  (365 shorter events, 319.6 us)
Async XLA Ops:
  7.2 100.3 %all-gather.37.cloned.1.call-start = ((), (), s32[]{:S(2)}) async-start(), calls=%async_computation.19 | async-start | bytes 8957952 | tf_op jit(solution)/shard_map/all_gather | solution.py:131
  10.0 45.6 %copy-start = (f32[512,1152]{1,0:T(8,128)}, f32[512,1152]{1,0:T(8,128)S(1)}, u32[]{:S(2)}) copy-start(f32[512,1152]{1,0:T(8,128)S(1)} %convert_element_type.149) | copy-start | bytes 7077892
  53.5 95.1 %all-gather.49.cloned.1.call-start = ((), (), s32[]{:S(2)}) async-start(), calls=%async_computation.25 | async-start | bytes 1658880 | tf_op jit(solution)/shard_map/all_gather | solution.py:127
  54.2 130.1 %all-gather.45.cloned.1.call-start = ((), (), s32[]{:S(2)}) async-start(), calls=%async_computation.23 | async-start | bytes 1843200 | tf_op jit(solution)/shard_map/all_gather | solution.py:128
  54.9 229.2 %all-gather.39.cloned.1.call-start = ((), (), s32[]{:S(2)}) async-start(), calls=%async_computation.20 | async-start | bytes 5898240 | tf_op jit(solution)/shard_map/all_gather | solution.py:150
  58.5 57.3 %copy-start.21 = (bf16[512,1152]{1,0:T(8,128)(2,1)}, bf16[512,1152]{1,0:T(8,128)(2,1)S(1)}, u32[]{:S(2)}) copy-start(bf16[512,1152]{1,0:T(8,128)(2,1)S(1)} %add_convert_fusion.3) | copy-start | bytes 3538948
  58.6 48.9 %copy-start.59 = (f32[3456]{0:T(1024)}, f32[3456]{0:T(1024)S(1)}, u32[]{:S(2)}) copy-start(f32[3456]{0:T(1024)S(1)} %pad_maximum_fusion.1) | copy-start | bytes 41476
  117.8 254.4 %all-gather.41.cloned.1.call-start = ((), (), s32[]{:S(2)}) async-start(), calls=%async_computation.21 | async-start | bytes 5898240 | tf_op jit(solution)/shard_map/all_gather | solution.py:149
  118.4 332.4 %all-gather.43.cloned.1.call-start = ((), (), s32[]{:S(2)}) async-start(), calls=%async_computation.22 | async-start | bytes 2985984 | tf_op jit(solution)/shard_map/all_gather | solution.py:132
  138.0 49.0 %copy-start.31 = (bf16[144,864]{1,0:T(8,128)(2,1)S(1)}, bf16[144,864]{1,0:T(8,128)(2,1)}, u32[]{:S(2)}) copy-start(bf16[144,864]{1,0:T(8,128)(2,1)} %param.28) | copy-start | bytes 746500
  139.2 332.6 %all-gather.51.cloned.1.call-start = ((), (), s32[]{:S(2)}) async-start(), calls=%async_computation.26 | async-start | bytes 11943936 | tf_op jit(solution)/shard_map/all_gather | solution.py:133
  148.6 389.0 %all-gather.47.cloned.1.call-start = ((), (), s32[]{:S(2)}) async-start(), calls=%async_computation.24 | async-start | bytes 11943936 | tf_op jit(solution)/shard_map/all_gather | solution.py:134
  186.9 34.8 %copy-start.8 = (f32[512,1152]{1,0:T(8,128)S(1)}, f32[512,1152]{1,0:T(8,128)}, u32[]{:S(2)}) copy-start(f32[512,1152]{1,0:T(8,128)} %convert_multiply_fusion) | copy-start | bytes 7077892
  186.9 638.4 %all-gather.21.cloned.1.call-start = ((), (), s32[]{:S(2)}) async-start(), calls=%async_computation.11 | async-start | bytes 8957952 | tf_op jit(solution)/shard_map/all_gather | solution.py:131
  221.6 680.8 %reduce-scatter.20.cloned.1.call-start = ((), (), s32[]{:S(2)}) async-start(), calls=%async_computation.27 | async-start | bytes 5898240 | tf_op jit(solution)/shard_map/reduce_scatter | solution.py:268
  380.1 70.7 %copy-start.1 = (f32[512,1152]{1,0:T(8,128)S(1)}, f32[512,1152]{1,0:T(8,128)}, u32[]{:S(2)}) copy-start(f32[512,1152]{1,0:T(8,128)} %copy-done) | copy-start | bytes 7077892
  457.2 110.1 %copy-start.44 = (f32[512]{0:T(512)}, f32[512]{0:T(512)S(1)}, u32[]{:S(2)}) copy-start(f32[512]{0:T(512)S(1)} %broadcast_multiply_fusion.4) | copy-start | bytes 6148
  462.1 22.8 %copy-start.17 = (bf16[512,1152]{1,0:T(8,128)(2,1)}, bf16[512,1152]{1,0:T(8,128)(2,1)S(1)}, u32[]{:S(2)}) copy-start(bf16[512,1152]{1,0:T(8,128)(2,1)S(1)} %add_convert_fusion.2) | copy-start | bytes 3538948
  462.1 75.4 %copy-start.28 = (bf16[512,1152]{1,0:T(8,128)(2,1)S(1)}, bf16[512,1152]{1,0:T(8,128)(2,1)}, u32[]{:S(2)}) copy-start(bf16[512,1152]{1,0:T(8,128)(2,1)} %get-tuple-element.336) | copy-start | bytes 3538948
  603.7 29.4 %slice-start = ((s8[16777216]{0:T(1024)(128)(4,1)}), s8[4194304]{0:T(1024)(128)(4,1)S(1)}, s32[]{:S(2)}) async-start(s8[16777216]{0:T(1024)(128)(4,1)} %bitcast.251), calls=%async_computation.39 | async-start | bytes 8388608 | tf_op jit(solution)/shard_map/while
  603.7 29.4 %slice-start.1 = ((s8[16777216]{0:T(1024)(128)(4,1)}), s8[4194304]{0:T(1024)(128)(4,1)S(1)}, s32[]{:S(2)}) async-start(s8[16777216]{0:T(1024)(128)(4,1)} %bitcast.251), calls=%async_computation.40 | async-start | bytes 8388608 | tf_op jit(solution)/shard_map/while
  603.7 29.4 %slice-start.2 = ((s8[16777216]{0:T(1024)(128)(4,1)}), s8[4194304]{0:T(1024)(128)(4,1)S(1)}, s32[]{:S(2)}) async-start(s8[16777216]{0:T(1024)(128)(4,1)} %bitcast.251), calls=%async_computation.41 | async-start | bytes 8388608 | tf_op jit(solution)/shard_map/while
  662.7 29.5 %slice-start = ((s8[16777216]{0:T(1024)(128)(4,1)}), s8[4194304]{0:T(1024)(128)(4,1)S(1)}, s32[]{:S(2)}) async-start(s8[16777216]{0:T(1024)(128)(4,1)} %bitcast.251), calls=%async_computation.39 | async-start | bytes 8388608 | tf_op jit(solution)/shard_map/while
  662.7 29.5 %slice-start.1 = ((s8[16777216]{0:T(1024)(128)(4,1)}), s8[4194304]{0:T(1024)(128)(4,1)S(1)}, s32[]{:S(2)}) async-start(s8[16777216]{0:T(1024)(128)(4,1)} %bitcast.251), calls=%async_computation.40 | async-start | bytes 8388608 | tf_op jit(solution)/shard_map/while
  662.7 29.5 %slice-start.2 = ((s8[16777216]{0:T(1024)(128)(4,1)}), s8[4194304]{0:T(1024)(128)(4,1)S(1)}, s32[]{:S(2)}) async-start(s8[16777216]{0:T(1024)(128)(4,1)} %bitcast.251), calls=%async_computation.41 | async-start | bytes 8388608 | tf_op jit(solution)/shard_map/while
  721.8 29.4 %slice-start = ((s8[16777216]{0:T(1024)(128)(4,1)}), s8[4194304]{0:T(1024)(128)(4,1)S(1)}, s32[]{:S(2)}) async-start(s8[16777216]{0:T(1024)(128)(4,1)} %bitcast.251), calls=%async_computation.39 | async-start | bytes 8388608 | tf_op jit(solution)/shard_map/while
  721.8 29.4 %slice-start.1 = ((s8[16777216]{0:T(1024)(128)(4,1)}), s8[4194304]{0:T(1024)(128)(4,1)S(1)}, s32[]{:S(2)}) async-start(s8[16777216]{0:T(1024)(128)(4,1)} %bitcast.251), calls=%async_computation.40 | async-start | bytes 8388608 | tf_op jit(solution)/shard_map/while
  721.8 29.4 %slice-start.2 = ((s8[16777216]{0:T(1024)(128)(4,1)}), s8[4194304]{0:T(1024)(128)(4,1)S(1)}, s32[]{:S(2)}) async-start(s8[16777216]{0:T(1024)(128)(4,1)} %bitcast.251), calls=%async_computation.41 | async-start | bytes 8388608 | tf_op jit(solution)/shard_map/while
  780.7 29.5 %slice-start = ((s8[16777216]{0:T(1024)(128)(4,1)}), s8[4194304]{0:T(1024)(128)(4,1)S(1)}, s32[]{:S(2)}) async-start(s8[16777216]{0:T(1024)(128)(4,1)} %bitcast.251), calls=%async_computation.39 | async-start | bytes 8388608 | tf_op jit(solution)/shard_map/while
  780.7 29.5 %slice-start.1 = ((s8[16777216]{0:T(1024)(128)(4,1)}), s8[4194304]{0:T(1024)(128)(4,1)S(1)}, s32[]{:S(2)}) async-start(s8[16777216]{0:T(1024)(128)(4,1)} %bitcast.251), calls=%async_computation.40 | async-start | bytes 8388608 | tf_op jit(solution)/shard_map/while
  780.7 29.5 %slice-start.2 = ((s8[16777216]{0:T(1024)(128)(4,1)}), s8[4194304]{0:T(1024)(128)(4,1)S(1)}, s32[]{:S(2)}) async-start(s8[16777216]{0:T(1024)(128)(4,1)} %bitcast.251), calls=%async_computation.41 | async-start | bytes 8388608 | tf_op jit(solution)/shard_map/while
  816.3 174.2 %reduce-scatter.22.cloned.1.call-start = ((), (), s32[]{:S(2)}) async-start(), calls=%async_computation.28 | async-start | bytes 5898240 | tf_op jit(solution)/shard_map/reduce_scatter | solution.py:271
  817.1 268.1 %all-gather.33.cloned.1.call-start = ((), (), s32[]{:S(2)}) async-start(), calls=%async_computation.17 | async-start | bytes 1843200 | tf_op jit(solution)/shard_map/all_gather | solution.py:128
  817.6 270.3 %all-gather.29.cloned.1.call-start = ((), (), s32[]{:S(2)}) async-start(), calls=%async_computation.15 | async-start | bytes 1658880 | tf_op jit(solution)/shard_map/all_gather | solution.py:127
  818.4 303.8 %reduce-scatter.28.cloned.1.call-start = ((), (), s32[]{:S(2)}) async-start(), calls=%async_computation.32 | async-start | bytes 5971968 | tf_op jit(solution)/shard_map/reduce_scatter | solution.py:328
  825.2 165.2 %copy-start.2 = (f32[512,1152]{1,0:T(8,128)S(1)}, f32[512,1152]{1,0:T(8,128)}, u32[]{:S(2)}) copy-start(f32[512,1152]{1,0:T(8,128)} %copy-done) | copy-start | bytes 7077892
  825.3 165.2 %copy-start.47 = (f32[512]{0:T(512)S(1)}, f32[512]{0:T(512)}, u32[]{:S(2)}) copy-start(f32[512]{0:T(512)} %copy-done.46) | copy-start | bytes 6148
  825.3 334.1 %all-reduce.4.cloned.1.call-start = ((), (), s32[]{:S(2)}) async-start(), calls=%async_computation.29 | async-start | bytes 221184 | tf_op jit(solution)/shard_map/psum | solution.py:308
  1037.1 210.2 %all-gather.23.cloned.1.call-start = ((), (), s32[]{:S(2)}) async-start(), calls=%async_computation.12 | async-start | bytes 5898240 | tf_op jit(solution)/shard_map/all_gather | solution.py:150
  1040.9 296.2 %all-gather.25.cloned.1.call-start = ((), (), s32[]{:S(2)}) async-start(), calls=%async_computation.13 | async-start | bytes 5898240 | tf_op jit(solution)/shard_map/all_gather | solution.py:149
  1041.5 437.5 %reduce-scatter.30.cloned.1.call-start = ((), (), s32[]{:S(2)}) async-start(), calls=%async_computation.33 | async-start | bytes 23887872 | tf_op jit(solution)/shard_map/reduce_scatter | solution.py:329
  1053.8 519.2 %all-gather.27.cloned.1.call-start = ((), (), s32[]{:S(2)}) async-start(), calls=%async_computation.14 | async-start | bytes 2985984 | tf_op jit(solution)/shard_map/all_gather | solution.py:132
  1070.4 582.1 %reduce-scatter.32.cloned.1.call-start = ((), (), s32[]{:S(2)}) async-start(), calls=%async_computation.34 | async-start | bytes 23887872 | tf_op jit(solution)/shard_map/reduce_scatter | solution.py:330
  1085.0 39.4 %copy-start.22 = (bf16[512,1152]{1,0:T(8,128)(2,1)S(1)}, bf16[512,1152]{1,0:T(8,128)(2,1)}, u32[]{:S(2)}) copy-start(bf16[512,1152]{1,0:T(8,128)(2,1)} %copy-done.21) | copy-start | bytes 3538948
  1085.0 633.1 %all-gather.35.cloned.1.call-start = ((), (), s32[]{:S(2)}) async-start(), calls=%async_computation.18 | async-start | bytes 11943936 | tf_op jit(solution)/shard_map/all_gather | solution.py:134
  1087.8 696.1 %all-gather.31.cloned.1.call-start = ((), (), s32[]{:S(2)}) async-start(), calls=%async_computation.16 | async-start | bytes 11943936 | tf_op jit(solution)/shard_map/all_gather | solution.py:133
  1088.6 718.6 %reduce-scatter.36.cloned.1.call-start = ((), (), s32[]{:S(2)}) async-start(), calls=%async_computation.36 | async-start | bytes 737280
  1124.4 799.2 %reduce-scatter.26.cloned.1.call-start = ((), (), s32[]{:S(2)}) async-start(), calls=%async_computation.31 | async-start | bytes 17915904 | tf_op jit(solution)/shard_map/reduce_scatter | solution.py:327
  1134.5 26.6 %copy-start.37 = (bf16[8,1152]{1,0:T(8,128)(2,1)S(1)}, bf16[8,1152]{1,0:T(8,128)(2,1)}, u32[]{:S(2)}) copy-start(bf16[8,1152]{1,0:T(8,128)(2,1)} %copy-done.36) | copy-start | bytes 55300
  1134.5 867.2 %reduce-scatter.24.cloned.1.call-start = ((), (), s32[]{:S(2)}) async-start(), calls=%async_computation.30 | async-start | bytes 9953280 | tf_op jit(solution)/shard_map/reduce_scatter | solution.py:322
  1165.9 885.1 %reduce-scatter.38.cloned.1.call-start = ((), (), s32[]{:S(2)}) async-start(), calls=%async_computation.37 | async-start | bytes 2949120
  1483.3 602.5 %reduce-scatter.40.cloned.1.call-start = ((), (), s32[]{:S(2)}) async-start(), calls=%async_computation.38 | async-start | bytes 1843200
  1483.5 89.6 %copy-start.13 = (bf16[512,1152]{1,0:T(8,128)(2,1)S(1)}, bf16[512,1152]{1,0:T(8,128)(2,1)}, u32[]{:S(2)}) copy-start(bf16[512,1152]{1,0:T(8,128)(2,1)} %param.22) | copy-start | bytes 3538948
  1483.5 89.6 %copy-start.35 = (f32[1152]{0:T(1024)S(1)}, f32[1152]{0:T(1024)}, u32[]{:S(2)}) copy-start(f32[1152]{0:T(1024)} %param.31) | copy-start | bytes 13828
  1579.6 204.3 %copy-start.16 = (f32[512,1152]{1,0:T(8,128)S(1)}, f32[512,1152]{1,0:T(8,128)}, u32[]{:S(2)}) copy-start(f32[512,1152]{1,0:T(8,128)} %copy-done.15) | copy-start | bytes 7077892
  1579.6 204.3 %copy-start.63 = (f32[4608]{0:T(1024)S(1)}, f32[4608]{0:T(1024)}, u32[]{:S(2)}) copy-start(f32[4608]{0:T(1024)} %param.33) | copy-start | bytes 55300
  1579.6 204.3 %copy-start.65 = (f32[1152]{0:T(1024)S(1)}, f32[1152]{0:T(1024)}, u32[]{:S(2)}) copy-start(f32[1152]{0:T(1024)} %param.35) | copy-start | bytes 13828
  1658.0 468.4 %reduce-scatter.34.cloned.1.call-start = ((), (), s32[]{:S(2)}) async-start(), calls=%async_computation.35 | async-start | bytes 2211840
  1808.9 118.3 %copy-start.26 = (bf16[512,1152]{0,1:T(8,128)(2,1)S(1)}, bf16[512,1152]{0,1:T(8,128)(2,1)}, u32[]{:S(2)}) copy-start(bf16[512,1152]{0,1:T(8,128)(2,1)} %reduce-scatter.20.cloned.1.call-done) | copy-start | bytes 3538948
  1808.9 118.3 %copy-start.27 = (bf16[512,1152]{0,1:T(8,128)(2,1)S(1)}, bf16[512,1152]{0,1:T(8,128)(2,1)}, u32[]{:S(2)}) copy-start(bf16[512,1152]{0,1:T(8,128)(2,1)} %reduce-scatter.22.cloned.1.call-done) | copy-start | bytes 3538948
  1929.4 41.4 %copy-start.32 = (bf16[8,6912]{1,0:T(8,128)(2,1)S(1)}, bf16[8,6912]{1,0:T(8,128)(2,1)}, u32[]{:S(2)}) copy-start(bf16[8,6912]{1,0:T(8,128)(2,1)} %all-reduce.4.cloned.1.call-done) | copy-start | bytes 331780
  1929.4 41.4 %copy-start.39 = (f32[8,576]{1,0:T(8,128)S(1)}, f32[8,576]{1,0:T(8,128)}, u32[]{:S(2)}) copy-start(f32[8,576]{1,0:T(8,128)} %copy-done.38) | copy-start | bytes 55300
  1929.4 41.4 %copy-start.41 = (f32[8,576]{1,0:T(8,128)S(1)}, f32[8,576]{1,0:T(8,128)}, u32[]{:S(2)}) copy-start(f32[8,576]{1,0:T(8,128)} %copy-done.40) | copy-start | bytes 55300
  1929.4 41.4 %copy-start.43 = (f32[8,1152]{1,0:T(8,128)S(1)}, f32[8,1152]{1,0:T(8,128)}, u32[]{:S(2)}) copy-start(f32[8,1152]{1,0:T(8,128)} %param.23) | copy-start | bytes 110596
  (46 other events, 264.1 us)
Sparse Core Ops, SparseCore 0:
  53.6 53.8 all-gather.36
  109.0 39.4 all-gather.48
  150.1 34.1 all-gather.44
  185.7 98.3 all-gather.38
  285.5 86.6 all-gather.40
  374.5 31.4 all-gather.42
  407.9 63.8 all-gather.50
  473.7 63.7 all-gather.46
  540.0 52.5 all-gather.20
  816.4 85.9 reduce-scatter.19
  904.7 85.7 reduce-scatter.21
  991.9 35.0 all-gather.32
  1028.6 32.9 all-gather.28
  1064.8 57.2 reduce-scatter.27
  1125.0 34.3 all-reduce.3
  1160.8 86.4 all-gather.22
  1249.2 87.8 all-gather.24
  1340.6 138.3 reduce-scatter.29
  1481.5 30.2 all-gather.26
  1515.2 137.1 reduce-scatter.31
  1654.3 63.7 all-gather.34
  1720.1 63.8 all-gather.30
  1786.8 19.2 reduce-scatter.35
  1809.5 113.9 reduce-scatter.25
  1927.5 74.2 reduce-scatter.23
  2004.1 46.8 reduce-scatter.37
  2053.3 32.5 reduce-scatter.39
  2088.2 38.1 reduce-scatter.33
where the time goes:
time: 2150 us; the launch traced here: 2140 us
  waiting for transfers between devices  1260 us (59%)
  matrix products  511 us (24%)
  other arithmetic  134 us (6%)
  blocking collectives  128 us (6%)
  local copies, waits for them, and re-layouts  84.5 us (4%)
    all_gather x2, waiting for transfers between devices, forward_pass(): lax.all_gather(qkv_low[:, width:2 * width], 'shard', axis=0, tiled=True)  165 us
    all_gather x2, waiting for transfers between devices, forward_pass(): lax.all_gather(qkv_low[:, 2 * width:], 'shard', axis=0, tiled=True)  137 us
    reduce_scatter x1, waiting for transfers between devices, per_device(): lax.psum_scatter(weight_grads[2], 'bin', scatter_dimension=0, tiled=True)  135 us
    unnamed x32, waiting for transfers between devices  122 us
    reduce_scatter x1, waiting for transfers between devices, per_device(): lax.psum_scatter(weight_grads[0], 'bin', scatter_dimension=0, tiled=True)  115 us
    all_gather x2, waiting for transfers between devices, collect_weights(): lax.all_gather(wider[3], 'bin', axis=0, tiled=True)  112 us
    dot_general x8, matrix products, matmul(): return jnp.dot(left, right, preferred_element_type=jnp.float32)  89.2 us
    reduce_scatter x1, waiting for transfers between devices, per_device(): lax.psum_scatter(grad_values_all.astype(jnp.bfloat16), 'shard', scatter_d...  88.1 us
  transfers between devices with their start and end apart: 28, of which 22 were waited for; matrix products, arithmetic and copies ran while one was open for 33% of the time, Pallas kernels for 0%

commit v1 on v0

v1 whole, which is shorter than its diff:
```python
import functools
import math

import jax
import jax.numpy as jnp
from jax import lax
from jax.experimental import pallas as pl
from jax.experimental.pallas import tpu as pltpu
from jax.sharding import PartitionSpec as P

HEADS = 16
HEAD_DIM = 72
UNIT = 256
LOG2E = 1.0 / math.log(2.0)
SCALE2 = LOG2E / math.sqrt(HEAD_DIM)
WIN = 256


def dot_nt(a, b):
    return lax.dot_general(a, b, (((1,), (1,)), ((), ())), preferred_element_type=jnp.float32)


def dot_nn(a, b):
    return lax.dot_general(a, b, (((1,), (0,)), ((), ())), preferred_element_type=jnp.float32)


def dot_tn(a, b):
    return lax.dot_general(a, b, (((0,), (0,)), ((), ())), preferred_element_type=jnp.float32)


def head_window(head, width):
    first = jnp.minimum(lax.div(head * HEAD_DIM, 128), width // 128 - 2)
    return pl.multiple_of(first * 128, 128)


def head_mask(head, base, rows):
    lane = lax.broadcasted_iota(jnp.int32, (rows, WIN), 1) + base
    return (lane >= head * HEAD_DIM) & (lane < (head + 1) * HEAD_DIM)


def attend_kernel(meta, q, k, v, kh, vh, out, lse):
    width = q.shape[1]
    lse[...] = jnp.zeros_like(lse)

    def one_head(head, carry):
        base = head_window(head, width)
        win = pl.ds(base, WIN)

        def attend(row, count, parts):
            rows = pl.ds(row, count)
            mask = head_mask(head, base, count)
            query = jnp.where(mask, q[rows, win], jnp.zeros((), jnp.bfloat16))
            scores = [dot_nt(query, kr[pl.ds(at, n), win]) for kr, vr, at, n in parts]
            top = functools.reduce(
                jnp.maximum, [jnp.max(s, axis=1, keepdims=True) for s in scores]
            )
            expo = [jnp.exp2((s - top) * SCALE2) for s in scores]
            total = sum(jnp.sum(e, axis=1, keepdims=True) for e in expo)
            summed = sum(
                dot_nn(e.astype(jnp.bfloat16), vr[pl.ds(at, n), win])
                for e, (kr, vr, at, n) in zip(expo, parts)
            )
            value = (summed / total).astype(jnp.bfloat16)
            out[rows, win] = jnp.where(mask, value, out[rows, win])
            lane = lax.broadcasted_iota(jnp.int32, (count, 128), 1)
            lse[rows, :] = jnp.where(lane == head, top * SCALE2 + jnp.log2(total), lse[rows, :])

        def alone(row):
            attend(row, UNIT, [(k, v, row, UNIT)])

        @pl.when(meta[0] == 0)
        def _():
            alone(0)
            alone(UNIT)

        @pl.when(meta[0] == 1)
        def _():
            own = pl.multiple_of(meta[1] * UNIT, UNIT)
            other = pl.multiple_of(UNIT - meta[1] * UNIT, UNIT)
            attend(own, UNIT, [(k, v, own, UNIT), (kh, vh, 0, 3 * UNIT)])
            alone(other)

        @pl.when(meta[0] == 2)
        def _():
            attend(0, UNIT, [(k, v, 0, 2 * UNIT), (kh, vh, 0, 2 * UNIT)])
            attend(UNIT, UNIT, [(k, v, 0, 2 * UNIT), (kh, vh, 0, 2 * UNIT)])

        return carry

    lax.fori_loop(0, HEADS, one_head, 0)


def attend(meta, q, k, v, kh, vh):
    rows, width = q.shape
    return pl.pallas_call(
        attend_kernel,
        out_shape=(
            jax.ShapeDtypeStruct((rows, width), jnp.bfloat16),
            jax.ShapeDtypeStruct((rows, 128), jnp.float32),
        ),
        in_specs=[pl.BlockSpec(memory_space=pltpu.SMEM)]
        + [pl.BlockSpec(memory_space=pltpu.VMEM)] * 5,
        out_specs=[pl.BlockSpec(memory_space=pltpu.VMEM)] * 2,
        compiler_params=pltpu.CompilerParams(vmem_limit_bytes=48 << 20),
        cost_estimate=pl.CostEstimate(
            flops=16 * 2 * 2 * 512 * 1024 * 256, bytes_accessed=10 << 20, transcendentals=16 * 512 * 1024
        ),
        name="attend",
    )(meta, q, k, v, kh, vh)


def own_back_kernel(meta, q, g, stats, k, v, kh, vh, grad_q, grad_k, grad_v):
    width = q.shape[1]
    grad_q[...] = jnp.zeros_like(grad_q)
    grad_k[...] = jnp.zeros_like(grad_k)
    grad_v[...] = jnp.zeros_like(grad_v)
    scale = 1.0 / math.sqrt(HEAD_DIM)

    def one_head(head, carry):
        base = head_window(head, width)
        win = pl.ds(base, WIN)

        def back(row, count, parts):
            rows = pl.ds(row, count)
            mask = head_mask(head, base, count)
            zero = jnp.zeros((), jnp.bfloat16)
            query = jnp.where(mask, q[rows, win], zero)
            grad = jnp.where(mask, g[rows, win], zero)
            lse = stats[pl.ds(head, 1), rows]
            delta = stats[pl.ds(head + HEADS, 1), rows]
            total = jnp.zeros((count, WIN), jnp.float32)
            for kr, vr, at, n, own in parts:
                keys = kr[pl.ds(at, n), win]
                probs = jnp.exp2(dot_nt(keys, query) * SCALE2 - lse)
                grad_probs = dot_nt(vr[pl.ds(at, n), win], grad)
                grad_scores = (probs * (grad_probs - delta)).astype(jnp.bfloat16)
                total += dot_tn(grad_scores, keys)
                if own:
                    grad_k[pl.ds(at, n), win] += dot_nn(grad_scores, query)
                    grad_v[pl.ds(at, n), win] += dot_nn(probs.astype(jnp.bfloat16), grad)
            grad_q[rows, win] = jnp.where(
                mask, (total * scale).astype(jnp.bfloat16), grad_q[rows, win]
            )

        def alone(row):
            back(row, UNIT, [(k, v, row, UNIT, True)])

        @pl.when(meta[0] == 0)
        def _():
            alone(0)
            alone(UNIT)

        @pl.when(meta[0] == 1)
        def _():
            own = pl.multiple_of(meta[1] * UNIT, UNIT)
            other = pl.multiple_of(UNIT - meta[1] * UNIT, UNIT)
            back(own, UNIT, [(k, v, own, UNIT, True), (kh, vh, 0, 3 * UNIT, False)])
            alone(other)

        @pl.when(meta[0] == 2)
        def _():
            back(0, 2 * UNIT, [(k, v, 0, 2 * UNIT, True), (kh, vh, 0, 2 * UNIT, False)])

        return carry

    lax.fori_loop(0, HEADS, one_head, 0)


def own_back(meta, q, g, stats, k, v, kh, vh):
    rows, width = q.shape
    return pl.pallas_call(
        own_back_kernel,
        out_shape=(
            jax.ShapeDtypeStruct((rows, width), jnp.bfloat16),
            jax.ShapeDtypeStruct((rows, width), jnp.float32),
            jax.ShapeDtypeStruct((rows, width), jnp.float32),
        ),
        in_specs=[pl.BlockSpec(memory_space=pltpu.SMEM)]
        + [pl.BlockSpec(memory_space=pltpu.VMEM)] * 7,
        out_specs=[pl.BlockSpec(memory_space=pltpu.VMEM)] * 3,
        compiler_params=pltpu.CompilerParams(vmem_limit_bytes=56 << 20),
        cost_estimate=pl.CostEstimate(
            flops=16 * 2 * 4 * 512 * 1024 * 256, bytes_accessed=20 << 20, transcendentals=16 * 512 * 1024
        ),
        name="own_back",
    )(meta, q, g, stats, k, v, kh, vh)


def halo_back_kernel(meta, qh, gh, stats, k, v, part_k, part_v, grad_k, grad_v, acc_k, acc_v):
    width = k.shape[1]
    acc_k[...] = part_k[...]
    acc_v[...] = part_v[...]
    scale = 1.0 / math.sqrt(HEAD_DIM)

    def one_head(head, carry):
        base = head_window(head, width)
        win = pl.ds(base, WIN)

        def back(count, row, own_count):
            mask = head_mask(head, base, count)
            zero = jnp.zeros((), jnp.bfloat16)
            query = jnp.where(mask, qh[0:count, win], zero)
            grad = jnp.where(mask, gh[0:count, win], zero)
            lse = stats[pl.ds(head, 1), 0:count]
            delta = stats[pl.ds(head + HEADS, 1), 0:count]
            own = pl.ds(row, own_count)
            probs = jnp.exp2(dot_nt(k[own, win], query) * SCALE2 - lse)
            grad_probs = dot_nt(v[own, win], grad)
            grad_scores = (probs * (grad_probs - delta)).astype(jnp.bfloat16)
            acc_k[own, win] += dot_nn(grad_scores, query)
            acc_v[own, win] += dot_nn(probs.astype(jnp.bfloat16), grad)

        @pl.when(meta[0] == 1)
        def _():
            back(3 * UNIT, pl.multiple_of(meta[1] * UNIT, UNIT), UNIT)

        @pl.when(meta[0] == 2)
        def _():
            back(2 * UNIT, 0, 2 * UNIT)

        return carry

    @pl.when(meta[0] != 0)
    def _():
        lax.fori_loop(0, HEADS, one_head, 0)

    grad_k[...] = (acc_k[...] * scale).astype(jnp.bfloat16)
    grad_v[...] = acc_v[...].astype(jnp.bfloat16)


def halo_back(meta, qh, gh, stats, k, v, part_k, part_v):
    rows, width = k.shape
    return pl.pallas_call(
        halo_back_kernel,
        out_shape=(
            jax.ShapeDtypeStruct((rows, width), jnp.bfloat16),
            jax.ShapeDtypeStruct((rows, width), jnp.bfloat16),
        ),
        in_specs=[pl.BlockSpec(memory_space=pltpu.SMEM)]
        + [pl.BlockSpec(memory_space=pltpu.VMEM)] * 7,
        out_specs=[pl.BlockSpec(memory_space=pltpu.VMEM)] * 2,
        scratch_shapes=[pltpu.VMEM((rows, width), jnp.float32)] * 2,
        compiler_params=pltpu.CompilerParams(vmem_limit_bytes=56 << 20),
        cost_estimate=pl.CostEstimate(
            flops=16 * 2 * 4 * 512 * 512 * 256, bytes_accessed=20 << 20, transcendentals=16 * 512 * 512
        ),
        name="halo_back",
    )(meta, qh, gh, stats, k, v, part_k, part_v)


def time_embed(time_index, width):
    half_width = width // 2
    freqs = jnp.exp(-math.log(10000.0) * jnp.arange(half_width, dtype=jnp.float32) / half_width)
    angles = time_index.astype(jnp.float32)[:, None] * freqs[None, :]
    return jnp.concatenate([jnp.cos(angles), jnp.sin(angles)], axis=1)


def layer_norm(value):
    center = value - jnp.mean(value, axis=-1, keepdims=True)
    inverse = lax.rsqrt(jnp.mean(center * center, axis=-1, keepdims=True) + 1e-06)
    return (center * inverse, inverse)


def norm_back(normed, inverse, grad_normed):
    mean_grad = jnp.mean(grad_normed, axis=-1, keepdims=True)
    mean_cross = jnp.mean(grad_normed * normed, axis=-1, keepdims=True)
    return inverse * (grad_normed - mean_grad - normed * mean_cross)


def flat(value):
    return value.reshape(-1, value.shape[-1])


def by_unit(value):
    return value.reshape(-1, UNIT, value.shape[-1])


def chain(count, step):
    pairs = [(at, at + 1) for at in range(count - 1)]
    return pairs if step > 0 else [(b, a) for a, b in pairs]


def halo_candidates(own, shards):
    up, down = chain(shards, 1), chain(shards, -1)
    left = lax.ppermute(own, "shard", up)
    right = lax.ppermute(own, "shard", down)
    left_far = lax.ppermute(left[UNIT:], "shard", up)
    right_far = lax.ppermute(right[:UNIT], "shard", down)
    return jnp.concatenate([left_far, left, right, right_far], axis=0)


def image_layout(unit_segments, shard):
    units = unit_segments.shape[0]
    first = 2 * shard
    own = lax.dynamic_slice_in_dim(unit_segments, first, 2)
    same = unit_segments[None, :] == own[:, None]
    long = jnp.sum(same, axis=1) > 1
    before = jnp.sum(same[0] & (jnp.arange(units) < first))
    both = long[0] & (own[0] == own[1])
    mode = jnp.where(both, 2, jnp.where(long[0] | long[1], 1, 0))
    which = jnp.where(long[1], 1, 0)
    start = jnp.where(both, 3 - before, jnp.where(long[1], 3, 0))
    slot = start + jnp.arange(3)
    halo_units = jnp.clip(first - 3 + slot + jnp.where(slot >= 3, 2, 0), 0, units - 1)
    meta = jnp.stack([mode, which]).astype(jnp.int32)
    return (meta, start, own, unit_segments[halo_units])


def matmul(left, right):
    return jnp.dot(left, right, preferred_element_type=jnp.float32)


def contract_rows(left, right):
    return lax.dot_general(
        left, right, (((0,), (0,)), ((), ())), preferred_element_type=jnp.float32
    )


def contract_cols(left, right):
    return lax.dot_general(
        left, right, (((1,), (1,)), ((), ())), preferred_element_type=jnp.float32
    )


def gather_weight(local):
    wide = lax.all_gather(local, "shard", axis=1, tiled=True)
    return lax.all_gather(wide, "bin", axis=0, tiled=True)


def reduce_grad(grad):
    short = lax.psum_scatter(grad, "bin", scatter_dimension=0, tiled=True)
    return lax.psum_scatter(short, "shard", scatter_dimension=1, tiled=True).astype(jnp.float32)


def split_low(value):
    high = value.astype(jnp.bfloat16)
    return [high, (value - high.astype(jnp.float32)).astype(jnp.bfloat16)]


def per_device(
    block_input,
    label_embed,
    time_index,
    segment_ids,
    ada_weight,
    ada_bias,
    qkv_weight,
    qv_bias,
    proj_weight,
    proj_bias,
    up_weight,
    up_bias,
    down_weight,
    down_bias,
    bin_weight,
    out_cotangent,
):
    rows, width = block_input.shape
    slots = label_embed.shape[0]
    shards = lax.axis_size("shard")
    shard = lax.axis_index("shard")
    unit_segments = segment_ids.reshape(-1, UNIT)[:, 0]
    meta, halo_start, own_segments, halo_segments = image_layout(unit_segments, shard)
    candidates = halo_candidates(block_input, shards)
    halo_input = lax.dynamic_slice_in_dim(candidates, halo_start * UNIT, 3 * UNIT)

    qkv_full = gather_weight(qkv_weight)
    proj_full = gather_weight(proj_weight)
    up_full = gather_weight(up_weight)
    down_full = gather_weight(down_weight)

    cond = label_embed + time_embed(time_index, width)
    cond_low = jax.nn.silu(cond).astype(jnp.bfloat16)
    cond_all = lax.all_gather(cond_low, "bin", axis=0, tiled=True)
    modul = matmul(cond_low, ada_weight) + ada_bias
    own_mod = modul[own_segments].reshape(-1, 1, 6 * width)
    shift_a, scale_a, gate_a, shift_m, scale_m, gate_m = jnp.split(own_mod, 6, axis=2)
    halo_mod = modul[halo_segments][:, None, : 2 * width]

    tokens = by_unit(block_input.astype(jnp.float32))
    normed, inverse = layer_norm(tokens)
    attn_in = flat((normed * (1.0 + scale_a) + shift_a).astype(jnp.bfloat16))
    halo_normed = layer_norm(by_unit(halo_input.astype(jnp.float32)))[0]
    halo_in = flat(
        (halo_normed * (1.0 + halo_mod[:, :, width:]) + halo_mod[:, :, :width]).astype(jnp.bfloat16)
    )
    qkv_bias = jnp.concatenate([qv_bias[:width], jnp.zeros((width,), jnp.float32), qv_bias[width:]])
    qkv_low = (matmul(attn_in, qkv_full) + qkv_bias).astype(jnp.bfloat16)
    halo_low = (matmul(halo_in, qkv_full) + qkv_bias).astype(jnp.bfloat16)
    query, keys, values = jnp.split(qkv_low, 3, axis=1)
    halo_query, halo_keys, halo_values = jnp.split(halo_low, 3, axis=1)

    heads_low, log_total = attend(meta, query, keys, values, halo_keys, halo_values)
    attn_out = by_unit(matmul(heads_low, proj_full) + proj_bias)
    middle = tokens + gate_a * attn_out
    normed_mlp, inverse_mlp = layer_norm(middle)
    mlp_in = flat((normed_mlp * (1.0 + scale_m) + shift_m).astype(jnp.bfloat16))
    pre_act = matmul(mlp_in, up_full) + up_bias
    act_low = jax.nn.gelu(pre_act, approximate=True).astype(jnp.bfloat16)
    mlp_out = by_unit(matmul(act_low, down_full) + down_bias)
    result = flat(middle + gate_m * mlp_out)

    grad_out = by_unit(out_cotangent.astype(jnp.float32) * bin_weight[0])
    grad_mlp = flat((grad_out * gate_m).astype(jnp.bfloat16))
    grad_down_w = reduce_grad(contract_rows(act_low, grad_mlp).astype(jnp.bfloat16))
    grad_down_b = jnp.sum(grad_mlp.astype(jnp.float32), axis=0)
    grad_act = contract_cols(grad_mlp, down_full)
    gelu_back = jax.vjp(lambda value: jax.nn.gelu(value, approximate=True), pre_act)[1]
    grad_pre = gelu_back(grad_act)[0].astype(jnp.bfloat16)
    grad_up_w = reduce_grad(contract_rows(mlp_in, grad_pre).astype(jnp.bfloat16))
    grad_up_b = jnp.sum(grad_pre.astype(jnp.float32), axis=0)
    grad_in_mlp = by_unit(contract_cols(grad_pre, up_full))
    grad_mid = grad_out + norm_back(normed_mlp, inverse_mlp, grad_in_mlp * (1.0 + scale_m))
    grad_attn = flat((grad_mid * gate_a).astype(jnp.bfloat16))
    grad_proj_w = reduce_grad(contract_rows(heads_low, grad_attn).astype(jnp.bfloat16))
    grad_proj_b = jnp.sum(grad_attn.astype(jnp.float32), axis=0)
    grad_heads = contract_cols(grad_attn, proj_full).astype(jnp.bfloat16)

    own_head = jnp.arange(width)[:, None] // HEAD_DIM == jnp.arange(HEADS)[None, :]
    delta = jnp.dot(
        grad_heads.astype(jnp.float32) * heads_low.astype(jnp.float32),
        own_head.astype(jnp.float32),
        precision=lax.Precision.HIGHEST,
        preferred_element_type=jnp.float32,
    )
    own_stats = jnp.concatenate([log_total[:, :HEADS], delta], axis=1)
    spare = jnp.zeros((rows, 128 - 4 * HEADS), jnp.bfloat16)
    payload = jnp.concatenate([grad_heads] + split_low(own_stats) + [spare], axis=1)
    payload_all = halo_candidates(payload, shards)
    halo_payload = lax.dynamic_slice_in_dim(payload_all, halo_start * UNIT, 3 * UNIT)
    halo_stats = halo_payload[:, width : width + 2 * HEADS].astype(jnp.float32) + halo_payload[
        :, width + 2 * HEADS : width + 4 * HEADS
    ].astype(jnp.float32)
    grad_query, part_keys, part_values = own_back(
        meta, query, grad_heads, own_stats.T, keys, values, halo_keys, halo_values
    )
    grad_keys, grad_values = halo_back(
        meta,
        halo_query,
        halo_payload[:, :width],
        halo_stats.T,
        keys,
        values,
        part_keys,
        part_values,
    )
    grad_qkv = jnp.concatenate([grad_query, grad_keys, grad_values], axis=1)
    grad_qkv_w = reduce_grad(contract_rows(attn_in, grad_qkv).astype(jnp.bfloat16))
    grad_qv_b = jnp.concatenate(
        [
            jnp.sum(grad_query.astype(jnp.float32), axis=0),
            jnp.sum(grad_values.astype(jnp.float32), axis=0),
        ]
    )
    grad_in_attn = by_unit(contract_cols(grad_qkv, qkv_full))
    grad_input = flat(grad_mid + norm_back(normed, inverse, grad_in_attn * (1.0 + scale_a)))

    unit_mod = jnp.concatenate(
        [
            jnp.sum(value, axis=1)
            for value in (
                grad_in_attn,
                grad_in_attn * normed,
                grad_mid * attn_out,
                grad_in_mlp,
                grad_in_mlp * normed_mlp,
                grad_out * mlp_out,
            )
        ],
        axis=1,
    )
    picked = own_segments[:, None] == jnp.arange(slots)[None, :]
    mod_part = jnp.sum(jnp.where(picked[:, :, None], unit_mod[:, None, :], 0.0), axis=0)
    grad_mod = lax.psum(mod_part.astype(jnp.bfloat16), "shard")
    grad_cond_act = contract_cols(grad_mod, ada_weight)
    grad_label = jax.vjp(jax.nn.silu, cond)[1](grad_cond_act)[0]

    bins = lax.axis_size("bin")
    own_width = grad_mod.shape[1] // (bins * shards)
    mod_view = grad_mod.reshape(slots, bins, shards, own_width)
    mod_columns = lax.dynamic_index_in_dim(mod_view, shard, axis=2, keepdims=False)
    mod_columns = lax.all_to_all(mod_columns, "bin", split_axis=1, concat_axis=0, tiled=True)[:, 0]
    grad_ada_w = contract_rows(cond_all, mod_columns)
    grad_ada_b = jnp.sum(mod_columns.astype(jnp.float32), axis=0)

    early = lax.psum(
        jnp.concatenate([grad_proj_b, grad_up_b, grad_down_b]), ("bin", "shard")
    )
    grad_qv_b = lax.psum(grad_qv_b, ("bin", "shard"))
    hidden = up_bias.shape[0]
    return (
        result,
        grad_input,
        grad_label,
        grad_ada_w,
        grad_ada_b,
        grad_qkv_w,
        grad_qv_b,
        grad_proj_w,
        early[:width],
        grad_up_w,
        early[width : width + hidden],
        grad_down_w,
        early[width + hidden :],
    )


def solution(mesh):
    placed = (
        P(("bin", "shard"), None),
        P("bin", None),
        P("bin"),
        P("bin"),
        P(),
        P(),
        P("bin", "shard"),
        P(),
        P("bin", "shard"),
        P(),
        P("bin", "shard"),
        P(),
        P("bin", "shard"),
        P(),
        P("bin"),
        P(("bin", "shard"), None),
    )
    return jax.shard_map(
        per_device,
        mesh=mesh,
        in_specs=placed,
        out_specs=(
            P(("bin", "shard"), None),
            P(("bin", "shard"), None),
            P("bin", None),
            P(None, ("bin", "shard")),
            P(("bin", "shard")),
            P("bin", "shard"),
            P(),
            P("bin", "shard"),
            P(),
            P("bin", "shard"),
            P(),
            P("bin", "shard"),
            P(),
        ),
        check_vma=False,
    )
```

time: 2150 us -> 927 us (0.43)
  waiting for transfers between devices: 1260 us -> 473 us
  matrix products: 511 us -> 147 us
  other arithmetic: 134 us -> 38.4 us
  Pallas kernels: 0 us -> 42.5 us
  starting transfers between devices: 1.39 us -> 30.3 us
  blocking collectives: 128 us -> 103 us
  local copies, waits for them, and re-layouts: 84.5 us -> 60.6 us
    all_gather x16 -> x6, waiting for transfers between devices: 583 us -> 129 us  [the longest x4 102 us: gather_weight(): return lax.all_gather(wide, 'bin', axis=0, tiled=True)]
    reduce_scatter x7 -> x4, waiting for transfers between devices: 530 us -> 219 us  [reduce_grad(): short = lax.psum_scatter(grad, 'bin', scatter_dimension=0, tiled=True)]
    dot_general x34 -> x1, matrix products: 271 us -> 1.26 us  [per_device(): jnp.dot(grad_heads.astype(jnp.float32) * heads_low.astype(jnp.float32), o...]
    convert_element_type x15 -> x8, other arithmetic: 82.7 us -> 9.41 us  [the longest x1 2.51 us: per_device(): attn_in = flat((normed * (1.0 + scale_a) + shift_a).astype(jnp.bfloat16))]
    sub x4 -> x0, matrix products: 47.8 us -> none  [one_block(): expo = jnp.exp(scores - top)]
    pallas_call x0 -> x3, Pallas kernels: none -> 42.5 us  [the longest x1 22.2 us: own_back(): pl.pallas_call(own_back_kernel, out_shape=(jax.ShapeDtypeStruct((rows, wi...]
    dot_general x8 -> x6, matrix products: 89.2 us -> 58.4 us  [matmul(): return jnp.dot(left, right, preferred_element_type=jnp.float32)]
    all_gather x10 -> x3, local copies, waits for them, and re-layouts: 33.3 us -> 3.17 us  [gather_weight(): wide = lax.all_gather(local, 'shard', axis=1, tiled=True)]
  transfers between devices with their start and end apart: 28 -> 24, of which waited for: 22 -> 13; matrix products, arithmetic and copies ran while one was open for 33% -> 20% of each run, Pallas kernels for 0% -> 5%
where the time goes in v1:
time: 927 us; the launch traced here: 915 us
  waiting for transfers between devices  473 us (51%)
  matrix products  147 us (16%)
  blocking collectives  103 us (11%)
  local copies, waits for them, and re-layouts  60.6 us (7%)
  Pallas kernels  42.5 us (5%)
  other arithmetic  38.4 us (4%)
  starting transfers between devices  30.3 us (3%)
  between operations  21.2 us (2%)
    reduce_scatter x4, waiting for transfers between devices, reduce_grad(): short = lax.psum_scatter(grad, 'bin', scatter_dimension=0, tiled=True)  219 us
    all_gather x4, waiting for transfers between devices, gather_weight(): return lax.all_gather(wide, 'bin', axis=0, tiled=True)  102 us
    unnamed x19, waiting for transfers between devices  95.6 us
    dot_general x6, matrix products, matmul(): return jnp.dot(left, right, preferred_element_type=jnp.float32)  58.4 us
    all_gather x2, blocking collectives, gather_weight(): wide = lax.all_gather(local, 'shard', axis=1, tiled=True)  51.7 us
    dot_general x5, matrix products, contract_cols(): lax.dot_general(left, right, (((1,), (1,)), ((), ())), preferred_element_...  51.5 us
    psum x1, blocking collectives, per_device(): grad_qv_b = lax.psum(grad_qv_b, ('bin', 'shard'))  41.1 us
    dot_general x5, matrix products, contract_rows(): lax.dot_general(left, right, (((0,), (0,)), ((), ())), preferred_element_...  35.7 us
  transfers between devices with their start and end apart: 24, of which 13 were waited for; matrix products, arithmetic and copies ran while one was open for 20% of the time, Pallas kernels for 5%

profile of v1, /device:TPU:8, one launch (start us, length us, event | category | flops | bytes accessed | tf_op | source)
XLA Modules:
  0.0 915.3 jit_solution(4325036539661955768)
XLA Ops:
  8.7 32.6 %all-gather = bf16[4,864,144]{1,2,0:T(8,128)(2,1)S(1)} all-gather(bf16[1,864,144]{1,2,0:T(8,128)(2,1)} %bitcast.188), channel_id=1, replica_groups=mesh['bin'=8,'shard'=4] {'shard'}, dimensions={0}, use_global_device_ids=true | all-gather | bytes 1244160 | tf_op jit(solution)/shard_map/all_gather | solution.py:326
  41.7 1.7 reshape.390
  43.5 19.0 %all-gather.1 = bf16[4,288,144]{1,2,0:T(8,128)(2,1)S(1)} all-gather(bf16[1,288,144]{1,2,0:T(8,128)(2,1)S(1)} %bitcast.191), channel_id=1, replica_groups=mesh['bin'=8,'shard'=4] {'shard'}, dimensions={0}, use_global_device_ids=true | all-gather | bytes 414720 | tf_op jit(solution)/shard_map/all_gather | solution.py:326
  64.5 27.8 %all-gather.17.cloned.1.call-done = bf16[576,1152]{0,1:T(8,128)(2,1)} async-done(((bf16[576,288]{0,1:T(8,128)(2,1)}), bf16[576,1152]{0,1:T(8,128)(2,1)}) %all-gather.17.cloned.1.call-update) | async-done | bytes 1327120 | tf_op jit(solution)/shard_map/all_gather | solution.py:326
  92.3 2.6 copy.75
  95.0 3.2 collective-permute-start
  98.2 2.7 collective-permute-start.2
  109.9 7.7 convolution_add_fusion
  122.1 2.3 collective-permute-done
  125.2 3.4 collective-permute-start.1
  128.7 1.9 slice.101
  130.6 3.2 collective-permute-start.3
  135.3 2.5 fusion.16
  137.8 1.9 convert_reduce_fusion.2
  141.5 5.3 collective-permute-done.3
  146.8 2.5 convert_reduce_fusion.1
  149.9 2.1 fusion.12
  152.1 8.7 add_convert_fusion.1
  162.3 7.4 add_convert_fusion
  169.7 2.4 fusion.60
  172.2 14.1 %attend.1 = (bf16[512,1152]{1,0:T(8,128)(2,1)S(1)}, f32[512,128]{1,0:T(8,128)S(1)}) custom-call(s32[2]{0:T(128)S(1)} %pad_add_fusion.meta, bf16[512,1152]{1,0:T(8,128)(2,1)S(1)} %get-tuple-element.140.q, bf16[512,1152]{1,0:T(8,128)(2,1)S(1)} %get-tuple-element.139.k, bf16[512,1152]{1,0:T(8,128)(2,1)S(1)} %get-tuple-element.138.v, ...), custom_call_target="tpu_custom_call" | custom-call | flops 8589934592 | bytes 10485760 | tf_op jit(solution)/shard_map/attend/pallas_call | solution.py:95
  189.2 5.4 fusion.57
  196.0 1.7 fusion.20
  197.7 47.8 %all-gather.15.cloned.1.call-done = bf16[1152,4608]{1,0:T(8,128)(2,1)} async-done(((bf16[144,4608]{1,0:T(8,128)(2,1)}), bf16[1152,4608]{1,0:T(8,128)(2,1)}) %all-gather.15.cloned.1.call-update) | async-done | bytes 10616848 | tf_op jit(solution)/shard_map/all_gather | solution.py:327
  245.5 11.9 %fusion.66 = f32[512,4608]{1,0:T(8,128)} fusion(bf16[512,1152]{1,0:T(8,128)(2,1)} %fusion.20, bf16[1152,4608]{1,0:T(8,128)(2,1)} %all-gather.15.cloned.1.call-done), kind=kOutput, calls=%fused_computation.183 | convolution fusion | flops 5435817984 | bytes 21233664 | tf_op jit(solution)/shard_map/dot_general | solution.py:310
  257.3 53.7 %all-gather.19.cloned.1.call-done = bf16[4608,1152]{1,0:T(8,128)(2,1)} async-done(((bf16[576,1152]{1,0:T(8,128)(2,1)}), bf16[4608,1152]{1,0:T(8,128)(2,1)}) %all-gather.19.cloned.1.call-update) | async-done | bytes 10616848 | tf_op jit(solution)/shard_map/all_gather | solution.py:327
  311.1 17.5 %convert_reduce_fusion = (f32[4608]{0:T(1024)}, bf16[512,4608]{1,0:T(8,128)(2,1)}) fusion(f32[512,4608]{1,0:T(8,128)} %fusion.66, f32[4608]{0:T(1024)} %param.27, bf16[512,1152]{1,0:T(8,128)(2,1)S(1)} %copy-done.23, bf16[4608,1152]{1,0:T(8,128)(2,1)} %all-gather.19.cloned.1.call-done), kind=kOutput, calls=%fused_computation.16 | convolution fusion | flops 5490077184 | bytes 25989120 | tf_op jit(solution)/shard_map/dot_general | solution.py:320
  328.6 11.6 %fusion.28 = (f32[512]{0:T(512)S(1)}, f32[512]{0:T(512)S(1)}, f32[512,1152]{1,0:T(8,128)S(1)}) fusion(f32[2,1152]{1,0:T(2,128)S(1)} %copy-done.38, f32[512]{0:T(512)S(1)} %copy-done.52, f32[512,1152]{1,0:T(8,128)S(1)} %copy-done.8, f32[512]{0:T(512)S(1)} %broadcast_multiply_fusion.5, bf16[512,4608]{1,0:T(8,128)(2,1)} %get-tuple-element.125, ...), kind=kOutput, calls=%fused_computation.84 | convolution fusion | flops 5439355904 | bytes 20071424 | tf_op jit(solution)/shard_map/dot_general | solution.py:320
  340.4 17.4 %convert_reduce_fusion.3 = (f32[1152]{0:T(1024)}, bf16[512,1152]{1,0:T(8,128)(2,1)S(1)}, f32[512,1152]{1,0:T(8,128)}, f32[512,1152]{1,0:T(8,128)}, f32[512,1152]{1,0:T(8,128)}) fusion(f32[2,1152]{1,0:T(2,128)S(1)} %get-tuple-element.149, f32[512]{0:T(512)S(1)} %broadcast_multiply_fusion.3, f32[512,1152]{1,0:T(8,128)S(1)} %copy-done.8, ...), kind=kOutput, calls=%fused_computation.63 | convolution fusion | flops 5469436928 | bytes 34273284 | tf_op jit(solution)/shard_map/dot_general | solution.py:310
  357.8 1.7 convolution_convert_fusion.4
  362.9 3.4 collective-permute-start.4
  366.3 3.5 collective-permute-start.6
  371.2 4.6 convolution_convert_fusion.3
  375.9 20.1 %collective-permute-done.4 = bf16[512,1280]{0,1:T(8,128)(2,1)} collective-permute-done((bf16[512,1280]{0,1:T(8,128)(2,1)}, bf16[512,1280]{0,1:T(8,128)(2,1)}, u32[]{:S(2)}, u32[]{:S(2)}) %collective-permute-start.4) | collective-permute-done | bytes 1310752 | tf_op jit(solution)/shard_map/ppermute | solution.py:285
  397.1 3.4 collective-permute-start.5
  401.7 2.5 collective-permute-start.7
  404.2 22.2 %own_back.1 = (bf16[512,1152]{1,0:T(8,128)(2,1)}, f32[512,1152]{1,0:T(8,128)}, f32[512,1152]{1,0:T(8,128)}) custom-call(s32[2]{0:T(128)} %copy-done.5, bf16[512,1152]{1,0:T(8,128)(2,1)} %copy-done.2, bf16[512,1152]{1,0:T(8,128)(2,1)} %copy.79.g, f32[32,512]{1,0:T(8,128)} %get-tuple-element.143.stats, bf16[512,1152]{1,0:T(8,128)(2,1)} %copy-done.1, ...), custom_call_target="tpu_custom_call" | custom-call | flops 17179869184 | bytes 20971520 | tf_op jit(solution)/shard_map/own_back/pallas_call | solution.py:171
  426.4 2.4 constant_dynamic-update-slice_fusion.2
  428.8 2.5 fusion.31
  432.7 3.9 copy.80.gh
  437.2 6.2 halo_back.1
  443.4 1.6 constant_dynamic-update-slice_fusion.1
  445.2 1.8 copy-done.30
  447.1 6.7 convolution_convert_fusion.2
  455.1 10.2 %convolution_convert_fusion.1 = bf16[1152,4608]{1,0:T(8,128)(2,1)} fusion(bf16[512,1152]{1,0:T(8,128)(2,1)S(1)} %copy-done.27, bf16[512,4608]{1,0:T(8,128)(2,1)} %get-tuple-element.125), kind=kOutput, calls=%fused_computation.4 | convolution fusion | flops 5441126400 | bytes 16515072 | tf_op jit(solution)/shard_map/dot_general | solution.py:314
  466.5 12.9 %convolution_convert_fusion = bf16[4608,1152]{1,0:T(8,128)(2,1)} fusion(bf16[512,1152]{1,0:T(8,128)(2,1)S(1)} %copy-done.24, f32[512,4608]{1,0:T(8,128)} %fusion.66, f32[4608]{0:T(1024)S(1)} %copy-done.60), kind=kOutput, calls=%fused_computation.3 | convolution fusion | flops 5464719360 | bytes 21252096 | tf_op jit(solution)/shard_map/dot_general | solution.py:314
  480.4 10.2 %fusion.27 = (f32[512]{0:T(512)}, f32[512]{0:T(512)}, f32[512,1152]{1,0:T(8,128)S(1)}) fusion(f32[2,1152]{1,0:T(2,128)S(1)} %copy-done.43, f32[512]{0:T(512)S(1)} %copy-done.56, f32[512]{0:T(512)S(1)} %copy-done.46, bf16[512,1152]{1,0:T(8,128)(2,1)S(1)} %copy-done.6, bf16[512,3456]{1,0:T(8,128)(2,1)} %copy-done.30, ...), kind=kOutput, calls=%fused_computation.83 | convolution fusion | flops 4080991232 | bytes 15057920 | tf_op jit(solution)/shard_map/dot_general | solution.py:320
  490.6 3.0 fusion.22
  494.5 2.1 copy.87
  496.7 53.9 %reduce-scatter.17.cloned.1.call-done = bf16[144,3456]{1,0:T(8,128)(2,1)} async-done(((bf16[1152,3456]{1,0:T(8,128)(2,1)}), bf16[144,3456]{1,0:T(8,128)(2,1)}) %reduce-scatter.17.cloned.1.call-update) | async-done | bytes 995344 | tf_op jit(solution)/shard_map/reduce_scatter | solution.py:331
  550.7 2.6 copy.85
  553.3 83.1 %reduce-scatter.21.cloned.1.call-done = bf16[144,4608]{1,0:T(8,128)(2,1)} async-done(((bf16[1152,4608]{1,0:T(8,128)(2,1)}), bf16[144,4608]{1,0:T(8,128)(2,1)}) %reduce-scatter.21.cloned.1.call-update) | async-done | bytes 1327120 | tf_op jit(solution)/shard_map/reduce_scatter | solution.py:331
  636.4 3.8 copy.89
  640.3 81.7 %reduce-scatter.23.cloned.1.call-done = bf16[576,1152]{1,0:T(8,128)(2,1)} async-done(((bf16[4608,1152]{1,0:T(8,128)(2,1)}), bf16[576,1152]{1,0:T(8,128)(2,1)}) %reduce-scatter.23.cloned.1.call-update) | async-done | bytes 1327120 | tf_op jit(solution)/shard_map/reduce_scatter | solution.py:331
  722.0 2.6 copy.91
  724.6 10.2 %all_gather.35 = bf16[64,1152]{1,0:T(8,128)(2,1)} all-gather(bf16[8,1152]{1,0:T(8,128)(2,1)} %copy-done.32), channel_id=1, replica_groups=mesh['bin'=8,'shard'=4] {'bin'}, dimensions={0}, use_global_device_ids=true | all-gather | bytes 165888 | tf_op jit(solution)/shard_map/all_gather | solution.py:374
  736.1 1.5 convert_reduce_fusion.5
  739.7 41.1 %all-reduce = (f32[2304]{0:T(1024)}, f32[6912]{0:T(1024)}) all-reduce(f32[2304]{0:T(1024)} %pad_maximum_fusion.3, f32[6912]{0:T(1024)} %pad_maximum_fusion.1), channel_id=1, replica_groups=mesh['bin'=8,'shard'=4] {'bin','shard'}, use_global_device_ids=true, to_apply=%region_25.26 | all-reduce | flops 9216 | bytes 73728 | tf_op jit(solution)/shard_map/psum | solution.py:489
  783.5 3.8 multiply_add_fusion
  789.9 4.3 all-to-all-start
  794.3 10.5 %fusion.39 = f32[8,1152]{1,0:T(8,128)} fusion(f32[8,1152]{1,0:T(8,128)} %param.17, f32[8,576]{1,0:T(8,128)} %copy-done.34, f32[8,576]{1,0:T(8,128)} %copy-done.33, bf16[8,6912]{1,0:T(8,128)(2,1)} %all-reduce.3.cloned.1.call-done, bf16[1152,6912]{1,0:T(8,128)(2,1)} %param.20), kind=kOutput, calls=%fused_computation.103 | convolution fusion | flops 127503360 | bytes 16146432 | tf_op jit(solution)/shard_map/dot_general | solution.py:320
  808.4 13.8 %reduce-scatter.25.cloned.1.call-done = bf16[864,144]{1,0:T(8,128)(2,1)} async-done(((bf16[3456,144]{1,0:T(8,128)(2,1)}), bf16[864,144]{1,0:T(8,128)(2,1)}) %reduce-scatter.25.cloned.1.call-update) | async-done | bytes 248848
  824.2 47.1 %reduce-scatter.29.cloned.1.call-done = bf16[1152,144]{1,0:T(8,128)(2,1)} async-done(((bf16[4608,144]{1,0:T(8,128)(2,1)}), bf16[1152,144]{1,0:T(8,128)(2,1)}) %reduce-scatter.29.cloned.1.call-update) | async-done | bytes 331792
  873.5 32.6 %reduce-scatter.31.cloned.1.call-done = bf16[288,576]{1,0:T(8,128)(2,1)} async-done(((bf16[1152,576]{1,0:T(8,128)(2,1)}), bf16[288,576]{1,0:T(8,128)(2,1)}) %reduce-scatter.31.cloned.1.call-update) | async-done | bytes 331792
  (282 shorter events, 54.3 us)
Async XLA Ops:
  7.2 56.7 %all-gather.13.cloned.1.call-start = ((), (), s32[]{:S(2)}) async-start(), calls=%async_computation.11 | async-start | bytes 1658880 | tf_op jit(solution)/shard_map/all_gather | solution.py:326
  7.9 84.4 %all-gather.17.cloned.1.call-start = ((), (), s32[]{:S(2)}) async-start(), calls=%async_computation.13 | async-start | bytes 1843200 | tf_op jit(solution)/shard_map/all_gather | solution.py:326
  8.7 143.4 %all-gather.9.cloned.1.call-start = ((), (), s32[]{:S(2)}) async-start(), calls=%async_computation.9 | async-start | bytes 8957952 | tf_op jit(solution)/shard_map/all_gather | solution.py:327
  43.5 145.7 %all-gather.11.cloned.1.call-start = ((), (), s32[]{:S(2)}) async-start(), calls=%async_computation.10 | async-start | bytes 2985984 | tf_op jit(solution)/shard_map/all_gather | solution.py:327
  63.8 181.7 %all-gather.15.cloned.1.call-start = ((), (), s32[]{:S(2)}) async-start(), calls=%async_computation.12 | async-start | bytes 11943936 | tf_op jit(solution)/shard_map/all_gather | solution.py:327
  64.4 30.6 %copy-start.6 = (bf16[512,1152]{1,0:T(8,128)(2,1)S(1)}, bf16[512,1152]{1,0:T(8,128)(2,1)}, u32[]{:S(2)}) copy-start(bf16[512,1152]{1,0:T(8,128)(2,1)} %param.16) | copy-start | bytes 3538948
  64.4 36.5 %copy-start.68 = (s32[2048]{0:T(1024)S(1)}, s32[2048]{0:T(1024)}, u32[]{:S(2)}) copy-start(s32[2048]{0:T(1024)} %param.19) | copy-start | bytes 24580
  64.4 42.7 %copy-start.73 = (s32[8]{0:T(128)S(1)}, s32[8]{0:T(128)}, u32[]{:S(2)}) copy-start(s32[8]{0:T(128)} %param.18) | copy-start | bytes 100
  64.4 246.6 %all-gather.19.cloned.1.call-start = ((), (), s32[]{:S(2)}) async-start(), calls=%async_computation.14 | async-start | bytes 11943936 | tf_op jit(solution)/shard_map/all_gather | solution.py:327
  94.9 14.1 %copy-start.58 = (f32[2304]{0:T(1024)S(1)}, f32[2304]{0:T(1024)}, u32[]{:S(2)}) copy-start(f32[2304]{0:T(1024)} %param.23) | copy-start | bytes 27652
  94.9 14.9 %copy-start.35 = (f32[8,1152]{1,0:T(8,128)S(1)}, f32[8,1152]{1,0:T(8,128)}, u32[]{:S(2)}) copy-start(f32[8,1152]{1,0:T(8,128)} %param.17) | copy-start | bytes 110596
  94.9 15.0 %copy-start.57 = (f32[6912]{0:T(1024)S(1)}, f32[6912]{0:T(1024)}, u32[]{:S(2)}) copy-start(f32[6912]{0:T(1024)} %param.21) | copy-start | bytes 82948
  94.9 399.6 %reduce-scatter.19.cloned.1.call-start = ((), (), s32[]{:S(2)}) async-start(), calls=%async_computation.17 | async-start | bytes 2985984 | tf_op jit(solution)/shard_map/reduce_scatter | solution.py:331
  95.0 29.4 %collective-permute-start = (bf16[512,1152]{1,0:T(8,128)(2,1)S(1)}, bf16[512,1152]{1,0:T(8,128)(2,1)S(1)}, u32[]{:S(2)}, u32[]{:S(2)}) collective-permute-start(bf16[512,1152]{1,0:T(8,128)(2,1)S(1)} %copy-done.6), channel_id=1, source_target_pairs={{0,1},{1,2},{2,3},{4,5},{5,6},{6,7},{8,9},{9,10},{10,11},{12,13},{... | collective-permute-start | bytes 3538952 | tf_op jit(solution)/shard_map/ppermute | solution.py:285
  98.2 30.5 %collective-permute-start.2 = (bf16[512,1152]{1,0:T(8,128)(2,1)S(1)}, bf16[512,1152]{1,0:T(8,128)(2,1)}, u32[]{:S(2)}, u32[]{:S(2)}) collective-permute-start(bf16[512,1152]{1,0:T(8,128)(2,1)S(1)} %copy-done.6), channel_id=1, source_target_pairs={{1,0},{2,1},{3,2},{5,4},{6,5},{7,6},{9,8},{10,9},{11,10},{13,12},{... | collective-permute-start | bytes 3538952 | tf_op jit(solution)/shard_map/ppermute | solution.py:286
  101.2 5.9 copy-start.70
  109.8 7.9 copy-start.33
  109.8 7.9 copy-start.34
  109.9 7.7 copy-start.32
  122.1 15.7 %copy-start.9 = (bf16[512,1152]{1,0:T(8,128)(2,1)S(1)}, bf16[512,1152]{1,0:T(8,128)(2,1)}, u32[]{:S(2)}) copy-start(bf16[512,1152]{1,0:T(8,128)(2,1)} %param.31) | copy-start | bytes 3538948
  125.2 16.2 %collective-permute-start.1 = (bf16[256,1152]{1,0:T(8,128)(2,1)}, bf16[256,1152]{1,0:T(8,128)(2,1)}, u32[]{:S(2)}, u32[]{:S(2)}) collective-permute-start(bf16[256,1152]{1,0:T(8,128)(2,1)} %slice.100), channel_id=1, source_target_pairs={{0,1},{1,2},{2,3},{4,5},{5,6},{6,7},{8,9},{9,10},{10,11},{12,13},{... | collective-permute-start | bytes 1769480 | tf_op jit(solution)/shard_map/ppermute | solution.py:287
  130.6 16.2 %collective-permute-start.3 = (bf16[256,1152]{1,0:T(8,128)(2,1)}, bf16[256,1152]{1,0:T(8,128)(2,1)}, u32[]{:S(2)}, u32[]{:S(2)}) collective-permute-start(bf16[256,1152]{1,0:T(8,128)(2,1)} %slice.101), channel_id=1, source_target_pairs={{1,0},{2,1},{3,2},{5,4},{6,5},{7,6},{9,8},{10,9},{11,10},{13,12},{... | collective-permute-start | bytes 1769480 | tf_op jit(solution)/shard_map/ppermute | solution.py:288
  133.9 38.2 %copy-start.5 = (s32[2]{0:T(128)}, s32[2]{0:T(128)S(1)}, u32[]{:S(2)}) copy-start(s32[2]{0:T(128)S(1)} %pad_add_fusion.meta) | copy-start | bytes 28
  135.3 4.5 copy-start.55
  135.3 5.1 copy-start.36
  152.1 9.0 copy-start.72
  162.3 9.9 %copy-start = (bf16[512,1152]{1,0:T(8,128)(2,1)}, bf16[512,1152]{1,0:T(8,128)(2,1)S(1)}, u32[]{:S(2)}) copy-start(bf16[512,1152]{1,0:T(8,128)(2,1)S(1)} %get-tuple-element.138.v) | copy-start | bytes 3538948
  162.3 9.9 %copy-start.1 = (bf16[512,1152]{1,0:T(8,128)(2,1)}, bf16[512,1152]{1,0:T(8,128)(2,1)S(1)}, u32[]{:S(2)}) copy-start(bf16[512,1152]{1,0:T(8,128)(2,1)S(1)} %get-tuple-element.139.k) | copy-start | bytes 3538948
  162.3 9.9 %copy-start.2 = (bf16[512,1152]{1,0:T(8,128)(2,1)}, bf16[512,1152]{1,0:T(8,128)(2,1)S(1)}, u32[]{:S(2)}) copy-start(bf16[512,1152]{1,0:T(8,128)(2,1)S(1)} %get-tuple-element.140.q) | copy-start | bytes 3538948
  197.7 113.4 %copy-start.23 = (bf16[512,1152]{1,0:T(8,128)(2,1)S(1)}, bf16[512,1152]{1,0:T(8,128)(2,1)}, u32[]{:S(2)}) copy-start(bf16[512,1152]{1,0:T(8,128)(2,1)} %get-tuple-element.127) | copy-start | bytes 3538948
  311.1 17.5 %copy-start.8 = (f32[512,1152]{1,0:T(8,128)S(1)}, f32[512,1152]{1,0:T(8,128)}, u32[]{:S(2)}) copy-start(f32[512,1152]{1,0:T(8,128)} %copy-done.7) | copy-start | bytes 7077892
  311.1 17.5 %copy-start.38 = (f32[2,1152]{1,0:T(2,128)S(1)}, f32[2,1152]{1,0:T(2,128)}, u32[]{:S(2)}) copy-start(f32[2,1152]{1,0:T(2,128)} %get-tuple-element.146) | copy-start | bytes 27652
  311.1 17.5 %copy-start.52 = (f32[512]{0:T(512)S(1)}, f32[512]{0:T(512)}, u32[]{:S(2)}) copy-start(f32[512]{0:T(512)} %copy-done.51) | copy-start | bytes 6148
  328.6 11.7 %copy-start.10 = (bf16[512,1152]{1,0:T(8,128)(2,1)S(1)}, bf16[512,1152]{1,0:T(8,128)(2,1)}, u32[]{:S(2)}) copy-start(bf16[512,1152]{1,0:T(8,128)(2,1)} %param.31) | copy-start | bytes 3538948
  328.6 11.7 %copy-start.42 = (f32[2,1152]{1,0:T(2,128)S(1)}, f32[2,1152]{1,0:T(2,128)}, u32[]{:S(2)}) copy-start(f32[2,1152]{1,0:T(2,128)} %get-tuple-element.144) | copy-start | bytes 27652
  328.6 11.7 %copy-start.59 = (f32[4608]{0:T(1024)S(1)}, f32[4608]{0:T(1024)}, u32[]{:S(2)}) copy-start(f32[4608]{0:T(1024)} %param.27) | copy-start | bytes 55300
  328.6 11.7 %copy-start.67 = (f32[1152]{0:T(1024)S(1)}, f32[1152]{0:T(1024)}, u32[]{:S(2)}) copy-start(f32[1152]{0:T(1024)} %param.29) | copy-start | bytes 13828
  340.2 17.5 %copy-start.13 = (f32[512,1152]{1,0:T(8,128)}, f32[512,1152]{1,0:T(8,128)S(1)}, u32[]{:S(2)}) copy-start(f32[512,1152]{1,0:T(8,128)S(1)} %get-tuple-element.165) | copy-start | bytes 7077892
  340.3 17.5 %copy-start.61 = (f32[512]{0:T(512)}, f32[512]{0:T(512)S(1)}, u32[]{:S(2)}) copy-start(f32[512]{0:T(512)S(1)} %broadcast_multiply_fusion.3) | copy-start | bytes 6148
  340.3 17.5 %copy-start.63 = (f32[512]{0:T(512)}, f32[512]{0:T(512)S(1)}, u32[]{:S(2)}) copy-start(f32[512]{0:T(512)S(1)} %broadcast_multiply_fusion.4) | copy-start | bytes 6148
  340.3 17.4 %copy-start.20 = (bf16[1152,1152]{1,0:T(8,128)(2,1)S(1)}, bf16[1152,1152]{1,0:T(8,128)(2,1)}, u32[]{:S(2)}) copy-start(bf16[1152,1152]{1,0:T(8,128)(2,1)} %all-gather.11.cloned.1.call-done) | copy-start | bytes 7962628
  362.9 33.1 %collective-permute-start.4 = (bf16[512,1280]{0,1:T(8,128)(2,1)}, bf16[512,1280]{0,1:T(8,128)(2,1)}, u32[]{:S(2)}, u32[]{:S(2)}) collective-permute-start(bf16[512,1280]{0,1:T(8,128)(2,1)} %maximum_maximum_fusion), channel_id=1, source_target_pairs={{0,1},{1,2},{2,3},{4,5},{5,6},{6,7},{8,9},{9,10},{10,11},{12,13},{... | collective-permute-start | bytes 3932168 | tf_op jit(solution)/shard_map/ppermute | solution.py:285
  366.3 34.3 %collective-permute-start.6 = (bf16[512,1280]{0,1:T(8,128)(2,1)}, bf16[512,1280]{0,1:T(8,128)(2,1)}, u32[]{:S(2)}, u32[]{:S(2)}) collective-permute-start(bf16[512,1280]{0,1:T(8,128)(2,1)} %maximum_maximum_fusion), channel_id=1, source_target_pairs={{1,0},{2,1},{3,2},{5,4},{6,5},{7,6},{9,8},{10,9},{11,10},{13,12},{... | collective-permute-start | bytes 3932168 | tf_op jit(solution)/shard_map/ppermute | solution.py:286
  375.8 174.8 %reduce-scatter.17.cloned.1.call-start = ((), (), s32[]{:S(2)}) async-start(), calls=%async_computation.16 | async-start | bytes 8957952 | tf_op jit(solution)/shard_map/reduce_scatter | solution.py:331
  397.1 31.6 %collective-permute-start.5 = (bf16[256,1280]{0,1:T(8,128)(2,1)S(1)}, bf16[256,1280]{0,1:T(8,128)(2,1)S(1)}, u32[]{:S(2)}, u32[]{:S(2)}) collective-permute-start(bf16[256,1280]{0,1:T(8,128)(2,1)S(1)} %slice.106), channel_id=1, source_target_pairs={{0,1},{1,2},{2,3},{4,5},{5,6},{6,7},{8,9},{9,10},{10,11},{12,13},{... | collective-permute-start | bytes 1966088 | tf_op jit(solution)/shard_map/ppermute | solution.py:287
  401.7 27.1 %collective-permute-start.7 = (bf16[256,1280]{0,1:T(8,128)(2,1)S(1)}, bf16[256,1280]{0,1:T(8,128)(2,1)S(1)}, u32[]{:S(2)}, u32[]{:S(2)}) collective-permute-start(bf16[256,1280]{0,1:T(8,128)(2,1)S(1)} %slice.107), channel_id=1, source_target_pairs={{1,0},{2,1},{3,2},{5,4},{6,5},{7,6},{9,8},{10,9},{11,10},{13,12},{... | collective-permute-start | bytes 1966088 | tf_op jit(solution)/shard_map/ppermute | solution.py:288
  437.2 6.2 copy-start.29
  453.8 182.6 %reduce-scatter.21.cloned.1.call-start = ((), (), s32[]{:S(2)}) async-start(), calls=%async_computation.18 | async-start | bytes 11943936 | tf_op jit(solution)/shard_map/reduce_scatter | solution.py:331
  465.3 256.7 %reduce-scatter.23.cloned.1.call-start = ((), (), s32[]{:S(2)}) async-start(), calls=%async_computation.19 | async-start | bytes 11943936 | tf_op jit(solution)/shard_map/reduce_scatter | solution.py:331
  479.5 308.4 %all-reduce.3.cloned.1.call-start = ((), (), s32[]{:S(2)}) async-start(), calls=%async_computation.15 | async-start | bytes 221184 | tf_op jit(solution)/shard_map/psum | solution.py:474
  480.3 10.2 %copy-start.11 = (bf16[512,1152]{1,0:T(8,128)(2,1)S(1)}, bf16[512,1152]{1,0:T(8,128)(2,1)}, u32[]{:S(2)}) copy-start(bf16[512,1152]{1,0:T(8,128)(2,1)} %param.31) | copy-start | bytes 3538948
  480.3 10.2 %copy-start.14 = (f32[512,1152]{1,0:T(8,128)S(1)}, f32[512,1152]{1,0:T(8,128)}, u32[]{:S(2)}) copy-start(f32[512,1152]{1,0:T(8,128)} %copy-done.13) | copy-start | bytes 7077892
  480.3 10.2 %copy-start.15 = (f32[512,1152]{1,0:T(8,128)S(1)}, f32[512,1152]{1,0:T(8,128)}, u32[]{:S(2)}) copy-start(f32[512,1152]{1,0:T(8,128)} %get-tuple-element.166) | copy-start | bytes 7077892
  480.3 10.2 %copy-start.16 = (f32[512,1152]{1,0:T(8,128)S(1)}, f32[512,1152]{1,0:T(8,128)}, u32[]{:S(2)}) copy-start(f32[512,1152]{1,0:T(8,128)} %get-tuple-element.164) | copy-start | bytes 7077892
  480.4 10.2 %copy-start.39 = (f32[2,1152]{1,0:T(2,128)S(1)}, f32[2,1152]{1,0:T(2,128)}, u32[]{:S(2)}) copy-start(f32[2,1152]{1,0:T(2,128)} %get-tuple-element.146) | copy-start | bytes 27652
  494.5 312.2 %reduce-scatter.27.cloned.1.call-start = ((), (), s32[]{:S(2)}) async-start(), calls=%async_computation.21 | async-start | bytes 737280
  496.7 325.5 %reduce-scatter.25.cloned.1.call-start = ((), (), s32[]{:S(2)}) async-start(), calls=%async_computation.20 | async-start | bytes 2211840
  553.3 318.1 %reduce-scatter.29.cloned.1.call-start = ((), (), s32[]{:S(2)}) async-start(), calls=%async_computation.22 | async-start | bytes 2949120
  640.2 265.8 %reduce-scatter.31.cloned.1.call-start = ((), (), s32[]{:S(2)}) async-start(), calls=%async_computation.23 | async-start | bytes 1843200
  724.6 58.9 %copy-start.12 = (f32[512,1152]{1,0:T(8,128)S(1)}, f32[512,1152]{1,0:T(8,128)}, u32[]{:S(2)}) copy-start(f32[512,1152]{1,0:T(8,128)} %get-tuple-element.123) | copy-start | bytes 7077892
  724.6 58.9 %copy-start.44 = (f32[2,1152]{1,0:T(2,128)S(1)}, f32[2,1152]{1,0:T(2,128)}, u32[]{:S(2)}) copy-start(f32[2,1152]{1,0:T(2,128)} %get-tuple-element.148) | copy-start | bytes 27652
  724.6 58.9 %copy-start.47 = (f32[512]{0:T(512)S(1)}, f32[512]{0:T(512)}, u32[]{:S(2)}) copy-start(f32[512]{0:T(512)} %copy-done.45) | copy-start | bytes 6148
  789.9 14.8 %all-to-all-start = ((bf16[8,8,216]{2,0,1:T(8,128)(2,1)}), bf16[8,8,216]{2,0,1:T(8,128)(2,1)S(1)}, u32[]{:S(2)}, u32[]{:S(2)}) async-start(bf16[8,8,216]{2,0,1:T(8,128)(2,1)} %bitcast.175), calls=%async_computation | async-start | bytes 65536 | tf_op jit(solution)/shard_map/all_to_all | solution.py:482
  794.3 11.1 %copy-start.28 = (bf16[64,1152]{1,0:T(8,128)(2,1)S(1)}, bf16[64,1152]{1,0:T(8,128)(2,1)}, u32[]{:S(2)}) copy-start(bf16[64,1152]{1,0:T(8,128)(2,1)} %all_gather.35) | copy-start | bytes 442372
  (34 other events, 59.9 us)
Sparse Core Ops, SparseCore 0:
  9.6 47.2 all-gather.12
  58.4 33.8 all-gather.16
  94.8 52.4 all-gather.8
  149.6 30.2 all-gather.10
  181.6 63.8 all-gather.14
  247.2 63.8 all-gather.18
  375.9 43.7 reduce-scatter.18
  453.9 96.6 reduce-scatter.16
  554.2 82.1 reduce-scatter.20
  639.8 82.1 reduce-scatter.22
  724.9 34.3 all-reduce.2
  762.1 19.0 reduce-scatter.26
  783.7 38.5 reduce-scatter.24
  824.4 46.9 reduce-scatter.28
  873.5 32.5 reduce-scatter.30

commit v2 on v1

v2 whole, which is shorter than its diff:
```python
import functools
import math

import jax
import jax.numpy as jnp
from jax import lax
from jax.experimental import pallas as pl
from jax.experimental.pallas import tpu as pltpu
from jax.sharding import PartitionSpec as P

HEADS = 16
HEAD_DIM = 72
UNIT = 256
LOG2E = 1.0 / math.log(2.0)
SCALE2 = LOG2E / math.sqrt(HEAD_DIM)
WIN = 256


def dot_nt(a, b):
    return lax.dot_general(a, b, (((1,), (1,)), ((), ())), preferred_element_type=jnp.float32)


def dot_nn(a, b):
    return lax.dot_general(a, b, (((1,), (0,)), ((), ())), preferred_element_type=jnp.float32)


def dot_tn(a, b):
    return lax.dot_general(a, b, (((0,), (0,)), ((), ())), preferred_element_type=jnp.float32)


def head_window(head, width):
    first = jnp.minimum(lax.div(head * HEAD_DIM, 128), width // 128 - 2)
    return pl.multiple_of(first * 128, 128)


def head_mask(head, base, rows):
    lane = lax.broadcasted_iota(jnp.int32, (rows, WIN), 1) + base
    return (lane >= head * HEAD_DIM) & (lane < (head + 1) * HEAD_DIM)


def attend_kernel(meta, own, halo, out, lse):
    width = out.shape[1]
    lse[...] = jnp.zeros_like(lse)

    def one_head(head):
        base = head_window(head, width)
        win = pl.ds(base, WIN)
        key_win = pl.ds(pl.multiple_of(base + width, 128), WIN)
        value_win = pl.ds(pl.multiple_of(base + 2 * width, 128), WIN)

        def attend(row, count, parts):
            rows = pl.ds(row, count)
            mask = head_mask(head, base, count)
            query = jnp.where(mask, own[rows, win], jnp.zeros((), jnp.bfloat16))
            scores = [dot_nt(query, ref[pl.ds(at, n), key_win]) for ref, at, n in parts]
            top = functools.reduce(
                jnp.maximum, [jnp.max(s, axis=1, keepdims=True) for s in scores]
            )
            expo = [jnp.exp2((s - top) * SCALE2) for s in scores]
            total = sum(jnp.sum(e, axis=1, keepdims=True) for e in expo)
            summed = sum(
                dot_nn(e.astype(jnp.bfloat16), ref[pl.ds(at, n), value_win])
                for e, (ref, at, n) in zip(expo, parts)
            )
            value = (summed / total).astype(jnp.bfloat16)
            out[rows, win] = jnp.where(mask, value, out[rows, win])
            lane = lax.broadcasted_iota(jnp.int32, (count, 128), 1)
            here = (lane == head) | (lane == head + 2 * HEADS)
            lse[rows, :] = jnp.where(here, top * SCALE2 + jnp.log2(total), lse[rows, :])

        return attend

    def alone(attend, row):
        attend(row, UNIT, [(own, row, UNIT)])

    @pl.when(meta[0] == 0)
    def _():
        @pl.loop(0, HEADS, unroll=4)
        def _(head):
            alone(one_head(head), 0)
            alone(one_head(head), UNIT)

    @pl.when(meta[0] == 1)
    def _():
        first = pl.multiple_of(meta[1] * UNIT, UNIT)
        other = pl.multiple_of(UNIT - meta[1] * UNIT, UNIT)

        @pl.loop(0, HEADS, unroll=4)
        def _(head):
            attend = one_head(head)
            attend(first, UNIT, [(own, first, UNIT), (halo, 0, 3 * UNIT)])
            alone(attend, other)

    @pl.when(meta[0] == 2)
    def _():
        @pl.loop(0, HEADS, unroll=4)
        def _(head):
            attend = one_head(head)
            attend(0, UNIT, [(own, 0, 2 * UNIT), (halo, 0, 2 * UNIT)])
            attend(UNIT, UNIT, [(own, 0, 2 * UNIT), (halo, 0, 2 * UNIT)])


def attend(meta, own, halo):
    rows, width = own.shape[0], own.shape[1] // 3
    return pl.pallas_call(
        attend_kernel,
        out_shape=(
            jax.ShapeDtypeStruct((rows, width), jnp.bfloat16),
            jax.ShapeDtypeStruct((rows, 128), jnp.float32),
        ),
        in_specs=[pl.BlockSpec(memory_space=pltpu.SMEM)]
        + [pl.BlockSpec(memory_space=pltpu.VMEM)] * 2,
        out_specs=[pl.BlockSpec(memory_space=pltpu.VMEM)] * 2,
        compiler_params=pltpu.CompilerParams(vmem_limit_bytes=48 << 20),
        cost_estimate=pl.CostEstimate(
            flops=2 * 2 * 512 * 1024 * WIN * HEADS,
            bytes_accessed=10 << 20,
            transcendentals=HEADS * 512 * 1024,
        ),
        name="attend",
    )(meta, own, halo)


def own_back_kernel(meta, own, halo, g, stats, grad_q, grad_k, grad_v, turned):
    width = g.shape[1]
    grad_q[...] = jnp.zeros_like(grad_q)
    grad_k[...] = jnp.zeros_like(grad_k)
    grad_v[...] = jnp.zeros_like(grad_v)
    turned[...] = stats[...].T
    scale = 1.0 / math.sqrt(HEAD_DIM)

    def one_head(head):
        base = head_window(head, width)
        win = pl.ds(base, WIN)
        key_win = pl.ds(pl.multiple_of(base + width, 128), WIN)
        value_win = pl.ds(pl.multiple_of(base + 2 * width, 128), WIN)

        def back(row, count, parts):
            rows = pl.ds(row, count)
            mask = head_mask(head, base, count)
            zero = jnp.zeros((), jnp.bfloat16)
            query = jnp.where(mask, own[rows, win], zero)
            grad = jnp.where(mask, g[rows, win], zero)
            lse = turned[pl.ds(head, 1), rows]
            delta = turned[pl.ds(head + HEADS, 1), rows]
            total = jnp.zeros((count, WIN), jnp.float32)
            for ref, at, n, mine in parts:
                keys = ref[pl.ds(at, n), key_win]
                probs = jnp.exp2(dot_nt(keys, query) * SCALE2 - lse)
                grad_probs = dot_nt(ref[pl.ds(at, n), value_win], grad)
                grad_scores = (probs * (grad_probs - delta)).astype(jnp.bfloat16)
                total += dot_tn(grad_scores, keys)
                if mine:
                    grad_k[pl.ds(at, n), win] += dot_nn(grad_scores, query)
                    grad_v[pl.ds(at, n), win] += dot_nn(probs.astype(jnp.bfloat16), grad)
            grad_q[rows, win] = jnp.where(
                mask, (total * scale).astype(jnp.bfloat16), grad_q[rows, win]
            )

        return back

    def alone(back, row):
        back(row, UNIT, [(own, row, UNIT, True)])

    @pl.when(meta[0] == 0)
    def _():
        @pl.loop(0, HEADS, unroll=4)
        def _(head):
            back = one_head(head)
            alone(back, 0)
            alone(back, UNIT)

    @pl.when(meta[0] == 1)
    def _():
        first = pl.multiple_of(meta[1] * UNIT, UNIT)
        other = pl.multiple_of(UNIT - meta[1] * UNIT, UNIT)

        @pl.loop(0, HEADS, unroll=4)
        def _(head):
            back = one_head(head)
            back(first, UNIT, [(own, first, UNIT, True), (halo, 0, 3 * UNIT, False)])
            alone(back, other)

    @pl.when(meta[0] == 2)
    def _():
        @pl.loop(0, HEADS, unroll=4)
        def _(head):
            back = one_head(head)
            back(0, 2 * UNIT, [(own, 0, 2 * UNIT, True), (halo, 0, 2 * UNIT, False)])


def own_back(meta, own, halo, g, stats):
    rows, width = g.shape
    return pl.pallas_call(
        own_back_kernel,
        out_shape=(
            jax.ShapeDtypeStruct((rows, width), jnp.bfloat16),
            jax.ShapeDtypeStruct((rows, width), jnp.float32),
            jax.ShapeDtypeStruct((rows, width), jnp.float32),
        ),
        in_specs=[pl.BlockSpec(memory_space=pltpu.SMEM)]
        + [pl.BlockSpec(memory_space=pltpu.VMEM)] * 4,
        out_specs=[pl.BlockSpec(memory_space=pltpu.VMEM)] * 3,
        scratch_shapes=[pltpu.VMEM((128, rows), jnp.float32)],
        compiler_params=pltpu.CompilerParams(vmem_limit_bytes=56 << 20),
        cost_estimate=pl.CostEstimate(
            flops=2 * 4 * 512 * 1024 * WIN * HEADS,
            bytes_accessed=20 << 20,
            transcendentals=HEADS * 512 * 1024,
        ),
        name="own_back",
    )(meta, own, halo, g, stats)


def halo_back_kernel(
    meta, own, qh, far_left, left, right, far_right, grad_q, part_k, part_v, out, gh, turned, acc_k, acc_v
):
    width = part_k.shape[1]
    acc_k[...] = part_k[...]
    acc_v[...] = part_v[...]
    scale = 1.0 / math.sqrt(HEAD_DIM)
    units = [(far_left, 0), (left, 0), (left, UNIT), (right, 0), (right, UNIT), (far_right, 0)]

    def one_head(head):
        base = head_window(head, width)
        win = pl.ds(base, WIN)
        key_win = pl.ds(pl.multiple_of(base + width, 128), WIN)
        value_win = pl.ds(pl.multiple_of(base + 2 * width, 128), WIN)

        def back(count, row, own_count):
            mask = head_mask(head, base, count)
            zero = jnp.zeros((), jnp.bfloat16)
            query = jnp.where(mask, qh[0:count, win], zero)
            grad = jnp.where(mask, gh[0:count, win], zero)
            lse = turned[pl.ds(head, 1), 0:count]
            delta = turned[pl.ds(head + HEADS, 1), 0:count]
            rows = pl.ds(row, own_count)
            probs = jnp.exp2(dot_nt(own[rows, key_win], query) * SCALE2 - lse)
            grad_probs = dot_nt(own[rows, value_win], grad)
            grad_scores = (probs * (grad_probs - delta)).astype(jnp.bfloat16)
            acc_k[rows, win] += dot_nn(grad_scores, query)
            acc_v[rows, win] += dot_nn(probs.astype(jnp.bfloat16), grad)

        return back

    @pl.when(meta[0] != 0)
    def _():
        for at in range(3):
            for unit in range(at, at + 4):
                ref, row = units[unit]

                @pl.when(meta[2] + at == unit)
                def _(ref=ref, row=row, at=at):
                    gh[at * UNIT : (at + 1) * UNIT, :] = ref[row : row + UNIT, :]

        tail = gh[:, width:].astype(jnp.float32).T
        turned[...] = tail[: 2 * HEADS] + tail[2 * HEADS : 4 * HEADS]

    @pl.when(meta[0] == 1)
    def _():
        row = pl.multiple_of(meta[1] * UNIT, UNIT)

        @pl.loop(0, HEADS, unroll=4)
        def _(head):
            one_head(head)(3 * UNIT, row, UNIT)

    @pl.when(meta[0] == 2)
    def _():
        @pl.loop(0, HEADS, unroll=4)
        def _(head):
            one_head(head)(2 * UNIT, 0, 2 * UNIT)

    out[:, :width] = grad_q[...]
    out[:, width : 2 * width] = (acc_k[...] * scale).astype(jnp.bfloat16)
    out[:, 2 * width :] = acc_v[...].astype(jnp.bfloat16)


def halo_back(meta, own, halo, pieces, grad_q, part_k, part_v):
    rows, width = part_k.shape
    halo_rows = halo.shape[0]

    def whole(value):
        return pl.BlockSpec(value.shape, lambda step: (0, 0))

    return pl.pallas_call(
        halo_back_kernel,
        grid=(1,),
        out_shape=jax.ShapeDtypeStruct((rows, 3 * width), jnp.bfloat16),
        in_specs=[pl.BlockSpec(memory_space=pltpu.SMEM), whole(own)]
        + [pl.BlockSpec((halo_rows, width), lambda step: (0, 0))]
        + [whole(value) for value in (*pieces, grad_q, part_k, part_v)],
        out_specs=pl.BlockSpec((rows, 3 * width), lambda step: (0, 0)),
        scratch_shapes=[
            pltpu.VMEM((halo_rows, pieces[0].shape[1]), jnp.bfloat16),
            pltpu.VMEM((2 * HEADS, halo_rows), jnp.float32),
        ]
        + [pltpu.VMEM((rows, width), jnp.float32)] * 2,
        compiler_params=pltpu.CompilerParams(vmem_limit_bytes=60 << 20),
        cost_estimate=pl.CostEstimate(
            flops=2 * 4 * 512 * 512 * WIN * HEADS,
            bytes_accessed=20 << 20,
            transcendentals=HEADS * 512 * 512,
        ),
        name="halo_back",
    )(meta, own, halo, *pieces, grad_q, part_k, part_v)


def time_embed(time_index, width):
    half_width = width // 2
    freqs = jnp.exp(-math.log(10000.0) * jnp.arange(half_width, dtype=jnp.float32) / half_width)
    angles = time_index.astype(jnp.float32)[:, None] * freqs[None, :]
    return jnp.concatenate([jnp.cos(angles), jnp.sin(angles)], axis=1)


def layer_norm(value):
    center = value - jnp.mean(value, axis=-1, keepdims=True)
    inverse = lax.rsqrt(jnp.mean(center * center, axis=-1, keepdims=True) + 1e-06)
    return (center * inverse, inverse)


def norm_back(normed, inverse, grad_normed):
    mean_grad = jnp.mean(grad_normed, axis=-1, keepdims=True)
    mean_cross = jnp.mean(grad_normed * normed, axis=-1, keepdims=True)
    return inverse * (grad_normed - mean_grad - normed * mean_cross)


def by_unit(value):
    return value.reshape(-1, UNIT, value.shape[-1])


def per_token(rows):
    units, width = rows.shape
    return jnp.broadcast_to(rows[:, None, :], (units, UNIT, width)).reshape(units * UNIT, width)


def chain(count, step):
    return [(at, at + step) for at in range(count) if 0 <= at + step < count]


def send_halo(own, shards):
    left = lax.ppermute(own, "shard", chain(shards, 1))
    right = lax.ppermute(own, "shard", chain(shards, -1))
    return left, right


def send_far(left, right, shards, step):
    left_far = lax.ppermute(left, "shard", chain(shards, step))
    right_far = lax.ppermute(right, "shard", chain(shards, -step))
    return left_far, right_far


def image_layout(unit_segments, shard):
    units = unit_segments.shape[0]
    first = 2 * shard
    own = lax.dynamic_slice_in_dim(unit_segments, first, 2)
    same = unit_segments[None, :] == own[:, None]
    long = jnp.sum(same, axis=1) > 1
    before = jnp.sum(same[0] & (jnp.arange(units) < first))
    both = long[0] & (own[0] == own[1])
    mode = jnp.where(both, 2, jnp.where(long[0] | long[1], 1, 0))
    which = jnp.where(long[1], 1, 0)
    start = jnp.where(both, 3 - before, jnp.where(long[1], 3, 0))
    slot = start + jnp.arange(3)
    halo_units = jnp.clip(first - 3 + slot + jnp.where(slot >= 3, 2, 0), 0, units - 1)
    meta = jnp.stack([mode, which, start]).astype(jnp.int32)
    return (meta, start, own, unit_segments[halo_units])


def matmul(left, right):
    return jnp.dot(left, right, preferred_element_type=jnp.float32)


def contract_rows(left, right):
    return lax.dot_general(
        left, right, (((0,), (0,)), ((), ())), preferred_element_type=jnp.float32
    )


def contract_cols(left, right):
    return lax.dot_general(
        left, right, (((1,), (1,)), ((), ())), preferred_element_type=jnp.float32
    )


def flipped(mask):
    return [(at, at ^ mask) for at in range(8)]


def swap(value, mask):
    return lax.ppermute(value, "bin", flipped(mask))


def rotate(value, count, step):
    return lax.ppermute(value, "shard", [(at, (at + step) % count) for at in range(count)])


def place_kernel(spots, *refs):
    pieces, out, sems = refs[:-2], refs[-2], refs[-1]
    copies = []
    for at, piece in enumerate(pieces):
        start = pl.multiple_of(spots[at], 16)
        copies.append(
            pltpu.make_async_copy(piece, out.at[pl.ds(start, piece.shape[0])], sems.at[at])
        )
    for copy in copies:
        copy.start()
    for copy in copies:
        copy.wait()


def place_rows(spots, pieces):
    rows = sum(piece.shape[0] for piece in pieces)
    width = pieces[0].shape[1]
    return pl.pallas_call(
        place_kernel,
        out_shape=jax.ShapeDtypeStruct((rows, width), pieces[0].dtype),
        in_specs=[pl.BlockSpec(memory_space=pltpu.SMEM)]
        + [pl.BlockSpec(memory_space=pl.ANY)] * len(pieces),
        out_specs=pl.BlockSpec(memory_space=pl.ANY),
        scratch_shapes=[pltpu.SemaphoreType.DMA((len(pieces),))],
        compiler_params=pltpu.CompilerParams(vmem_limit_bytes=1 << 20),
        cost_estimate=pl.CostEstimate(
            flops=0, bytes_accessed=4 * rows * width, transcendentals=0
        ),
        name="place_rows",
    )(jnp.stack(spots).astype(jnp.int32), *pieces)


def after(value, *others):
    return lax.optimization_barrier((value,) + others)[0]


def together(values, *others):
    return lax.optimization_barrier(tuple(values) + others)[: len(values)]


def rotations(local):
    count = lax.axis_size("shard")
    return [rotate(local, count, step) for step in range(1, count)]


def in_order(local, others):
    count = len(others) + 1
    shard = lax.axis_index("shard")
    ring = jnp.stack(list(others[::-1]) + [local])
    twice = jnp.concatenate([ring, ring])
    return lax.dynamic_slice_in_dim(twice, count - 1 - shard, count)


def columns_of(local, others):
    return in_order(local, others).transpose(1, 0, 2).reshape(local.shape[0], -1)


def row_split(rows):
    return (rows // 2 + 15) // 16 * 16


def place_pieces(pieces, swapped):
    me = lax.axis_index("bin")
    rows = pieces[0].shape[0]
    half = row_split(rows)
    starts = [me, me ^ 2, me ^ 4, me ^ 6, me ^ 6]
    offsets = [0, 0, 0, 0, half]
    spots = [start * rows + offset for start, offset in zip(starts, offsets)]
    spots += [(start ^ 1) * rows + offset for start, offset in zip(starts, offsets)]
    return place_rows(spots, list(pieces) + list(swapped))


def column_parts(short):
    count = lax.axis_size("shard")
    shard = lax.axis_index("shard")
    parts = short.reshape(short.shape[0], count, -1)
    return [
        lax.dynamic_index_in_dim(parts, lax.rem(shard + step, count), 1, keepdims=False)
        for step in range(count)
    ]


def rotate_parts(parts):
    count = len(parts)
    return [rotate(part, count, step) for step, part in enumerate(parts) if step > 0]


def sum_wide(parts):
    return sum(part.astype(jnp.float32) for part in parts)


def scatter_columns(short):
    return lax.psum_scatter(short, "shard", scatter_dimension=1, tiled=True)


def stack_kernel(*refs):
    pieces, out = refs[:-1], refs[-1]
    width = out.shape[1]
    row = 0
    for piece in pieces:
        rows = piece.shape[0]
        for at in range(piece.shape[1] // width):
            out[row : row + rows, :] = piece[:, at * width : (at + 1) * width]
            row += rows


def stack_rows(pieces, width):
    rows = sum(piece.size for piece in pieces) // width
    return pl.pallas_call(
        stack_kernel,
        out_shape=jax.ShapeDtypeStruct((rows, width), pieces[0].dtype),
        in_specs=[pl.BlockSpec(memory_space=pltpu.VMEM)] * len(pieces),
        out_specs=pl.BlockSpec(memory_space=pltpu.VMEM),
        compiler_params=pltpu.CompilerParams(vmem_limit_bytes=8 << 20),
        cost_estimate=pl.CostEstimate(flops=0, bytes_accessed=8 * rows * width, transcendentals=0),
        name="stack_rows",
    )(*pieces)


def add_low(first, second):
    return (first.astype(jnp.float32) + second.astype(jnp.float32)).astype(jnp.bfloat16)


def half_blocks(left):
    me = lax.axis_index("bin")
    turned = lax.optimization_barrier(left.T)
    blocks = turned.reshape(8, turned.shape[0] // 8, -1)
    half = row_split(blocks.shape[1])
    result = []
    for flip in (1, 0):
        own, side, over, cross = [
            lax.dynamic_index_in_dim(blocks, me ^ flip ^ mask, 0, keepdims=False)
            for mask in (0, 2, 4, 6)
        ]
        upper = [part[:half] for part in (own, over, side, cross)]
        lower = [part[half:] for part in (own, side, over, cross)]
        result.append(jnp.concatenate(upper + lower))
    return result


def first_parts(total):
    half = row_split(total.shape[0] // 4)
    rest = total.shape[0] // 4 - half
    return total[2 * half : 4 * half], total[4 * half + 2 * rest :]


def second_parts(total, from_x, from_y):
    half = row_split(total.shape[0] // 4)
    rest = total.shape[0] // 4 - half
    low = 4 * half
    top = total[:half].astype(jnp.float32) + from_x[:half].astype(jnp.float32)
    bottom = total[low : low + rest].astype(jnp.float32) + from_y[:rest].astype(jnp.float32)
    return (
        add_low(total[half : 2 * half], from_x[half:]),
        add_low(total[low + rest : low + 2 * rest], from_y[rest:]),
        top,
        bottom,
    )


def last_rows(top, bottom, upper, lower):
    return jnp.concatenate(
        [top + upper.astype(jnp.float32), bottom + lower.astype(jnp.float32)]
    ).astype(jnp.bfloat16)


def split_low(value):
    high = value.astype(jnp.bfloat16)
    return [high, (value - high.astype(jnp.float32)).astype(jnp.bfloat16)]


def per_device(
    block_input,
    label_embed,
    time_index,
    segment_ids,
    ada_weight,
    ada_bias,
    qkv_weight,
    qv_bias,
    proj_weight,
    proj_bias,
    up_weight,
    up_bias,
    down_weight,
    down_bias,
    bin_weight,
    out_cotangent,
):
    rows, width = block_input.shape
    slots = label_embed.shape[0]
    shards = lax.axis_size("shard")
    bins = lax.axis_size("bin")
    shard = lax.axis_index("shard")
    fast = bins == 8
    unit_segments = segment_ids.reshape(-1, UNIT)[:, 0]
    meta, halo_start, own_segments, halo_segments = image_layout(unit_segments, shard)

    cond = label_embed + time_embed(time_index, width)
    cond_low = jax.nn.silu(cond).astype(jnp.bfloat16)
    modul = matmul(cond_low, ada_weight) + ada_bias
    own_mod = modul[own_segments]
    shift_a, scale_a, gate_a, shift_m, scale_m, gate_m = [
        per_token(part) for part in jnp.split(own_mod, 6, axis=1)
    ]
    halo_mod = modul[halo_segments][:, : 2 * width]
    halo_shift, halo_scale = per_token(halo_mod[:, :width]), per_token(halo_mod[:, width:])

    qkv_parts = rotations(qkv_weight)
    proj_parts = rotations(proj_weight)
    tokens = block_input.astype(jnp.float32)
    normed, inverse = layer_norm(tokens)
    attn_in = (normed * (1.0 + scale_a) + shift_a).astype(jnp.bfloat16)
    qkv_wide = columns_of(qkv_weight, together(qkv_parts, attn_in))
    qkv_full = lax.all_gather(qkv_wide, "bin", axis=0, tiled=True)
    proj_wide = columns_of(proj_weight, together(proj_parts, qkv_wide))
    left, right = send_halo(after(block_input, qkv_wide), shards)
    up_parts = rotations(after(up_weight, qkv_wide))
    if fast:
        proj_x, proj_y = swap(proj_wide, 2), swap(proj_wide, 4)
    else:
        proj_full = lax.all_gather(proj_wide, "bin", axis=0, tiled=True)
    left, right = together((left, right), proj_wide)
    far_left, far_right = together((left[UNIT:], right[:UNIT]))
    up_parts = together(up_parts, far_left, far_right)
    left_far, right_far = send_far(far_left, far_right, shards, 1)
    up_wide = columns_of(up_weight, up_parts)
    up_full = lax.all_gather(up_wide, "bin", axis=0, tiled=True)
    if fast:
        proj_x, proj_y = together((proj_x, proj_y), up_wide)
        half = row_split(proj_wide.shape[0])
        proj_cross = [swap(proj_y[:half], 2), swap(proj_x[half:], 4)]
        proj_core = [swap(piece, 1) for piece in (proj_wide, proj_x, proj_y)]
    qkv_bias = jnp.concatenate([qv_bias[:width], jnp.zeros((width,), jnp.float32), qv_bias[width:]])
    qkv_low = (matmul(after(attn_in, up_wide), qkv_full) + qkv_bias).astype(jnp.bfloat16)
    left_far, right_far = together((left_far, right_far), qkv_low)
    down_parts = rotations(after(down_weight, left_far))
    candidates = jnp.concatenate([left_far, left, right, right_far])
    halo_input = lax.dynamic_slice_in_dim(candidates, halo_start * UNIT, 3 * UNIT)
    halo_normed = layer_norm(halo_input.astype(jnp.float32))[0]
    halo_in = (halo_normed * (1.0 + halo_scale) + halo_shift).astype(jnp.bfloat16)
    halo_low = (matmul(halo_in, qkv_full) + qkv_bias).astype(jnp.bfloat16)
    if fast:
        proj_cross = together(proj_cross, halo_low)
        proj_core += [swap(piece, 1) for piece in proj_cross]
        halo_low = after(halo_low, *proj_cross)
    heads_low, log_total = attend(meta, qkv_low, halo_low)
    down_wide = columns_of(down_weight, together(down_parts, heads_low))
    if fast:
        down_x, down_y = swap(down_wide, 2), swap(down_wide, 4)
        proj_core = together(proj_core, down_wide)
        proj_full = place_pieces([proj_wide, proj_x, proj_y] + list(proj_cross), proj_core)
    else:
        down_full = lax.all_gather(down_wide, "bin", axis=0, tiled=True)
    attn_out = matmul(heads_low, proj_full) + proj_bias
    middle = tokens + gate_a * attn_out
    normed_mlp, inverse_mlp = layer_norm(middle)
    mlp_in = (normed_mlp * (1.0 + scale_m) + shift_m).astype(jnp.bfloat16)
    if fast:
        down_x, down_y = together((down_x, down_y), mlp_in)
        half = row_split(down_wide.shape[0])
        down_cross = together((down_y[:half], down_x[half:]))
        up_full = after(up_full, down_cross[0])
        down_cross = [swap(down_cross[0], 2), swap(down_cross[1], 4)]
        down_core = [swap(piece, 1) for piece in (down_wide, down_x, down_y)]
    pre_act = matmul(mlp_in, up_full) + up_bias
    act_low = lax.optimization_barrier(
        jax.nn.gelu(pre_act, approximate=True).astype(jnp.bfloat16)
    )

    slope = jax.vjp(lambda value: jax.nn.gelu(value, approximate=True), after(pre_act, act_low))[1](
        jnp.ones_like(pre_act)
    )[0]
    slope = lax.optimization_barrier(slope.astype(jnp.bfloat16))

    grad_out = out_cotangent.astype(jnp.float32) * bin_weight[0]
    grad_mlp = (grad_out * gate_m).astype(jnp.bfloat16)
    grad_down = contract_rows(act_low, grad_mlp).astype(jnp.bfloat16)
    if fast:
        down_cross = together(down_cross, grad_down, slope)
        down_core += [swap(piece, 1) for piece in down_cross]
        down_full = place_pieces([down_wide, down_x, down_y] + list(down_cross), down_core)
    grad_mlp = after(grad_mlp, grad_down)
    grad_down = lax.psum_scatter(grad_down, "bin", scatter_dimension=0, tiled=True)
    grad_down_b = jnp.sum(grad_mlp.astype(jnp.float32), axis=0)
    grad_act = contract_cols(grad_mlp, down_full)
    grad_pre = (grad_act * slope.astype(jnp.float32)).astype(jnp.bfloat16)
    grad_up_b = jnp.sum(grad_pre.astype(jnp.float32), axis=0)
    grad_up = contract_rows(mlp_in, grad_pre).astype(jnp.bfloat16)
    grad_in_mlp = contract_cols(after(grad_pre, grad_up), up_full)
    grad_up = lax.psum_scatter(grad_up, "bin", scatter_dimension=0, tiled=True)
    grad_mid = grad_out + norm_back(normed_mlp, inverse_mlp, grad_in_mlp * (1.0 + scale_m))
    grad_attn = (grad_mid * gate_a).astype(jnp.bfloat16)
    grad_proj_b = jnp.sum(grad_attn.astype(jnp.float32), axis=0)
    if fast:
        heads_other, heads_mine = half_blocks(heads_low)
        other_proj = matmul(heads_other, grad_attn).astype(jnp.bfloat16)
        grad_attn = after(grad_attn, other_proj)
        got_proj = swap(other_proj, 1)
    grad_heads = contract_cols(grad_attn, proj_full).astype(jnp.bfloat16)

    lane = jnp.arange(128)[None, :]
    own_head = jnp.arange(width)[:, None] // HEAD_DIM + HEADS == lane % (2 * HEADS)
    own_head &= lane < 4 * HEADS
    delta = jnp.dot(
        grad_heads.astype(jnp.float32) * heads_low.astype(jnp.float32),
        own_head.astype(jnp.float32),
        precision=lax.Precision.HIGHEST,
        preferred_element_type=jnp.float32,
    )
    own_stats = log_total + delta
    high, low = split_low(own_stats)
    payload = jnp.concatenate([grad_heads, jnp.where(lane < 2 * HEADS, high, low)], axis=1)
    left, right = send_halo(payload, shards)
    left_far, right_far = send_far(payload[UNIT:], payload[:UNIT], shards, 2)
    if fast:
        total_proj = matmul(after(heads_mine, payload), grad_attn) + got_proj.astype(jnp.float32)
        total_proj = total_proj.astype(jnp.bfloat16)
        proj_x, proj_y, total_proj = together((*first_parts(total_proj), total_proj))
        grad_heads = after(grad_heads, proj_x, proj_y)
        proj_x, proj_y = swap(proj_x, 2), swap(proj_y, 4)
    else:
        grad_proj = contract_rows(heads_low, grad_attn).astype(jnp.bfloat16)
        grad_proj = lax.psum_scatter(grad_proj, "bin", scatter_dimension=0, tiled=True)
    grad_query, part_keys, part_values = own_back(meta, qkv_low, halo_low, grad_heads, own_stats)
    left, right, left_far, right_far = together((left, right, left_far, right_far), grad_query)
    grad_qkv = halo_back(
        meta,
        qkv_low,
        halo_low,
        (left_far, left, right, right_far),
        grad_query,
        part_keys,
        part_values,
    )
    if fast:
        attn_other, attn_mine = half_blocks(attn_in)
        other_qkv = matmul(attn_other, grad_qkv).astype(jnp.bfloat16)
        got_qkv = swap(other_qkv, 1)
        grad_down_w = scatter_columns(after(grad_down, grad_up, other_qkv))
        grad_in_attn = contract_cols(after(grad_qkv, other_qkv), qkv_full)
        total_qkv = matmul(after(attn_mine, grad_in_attn), grad_qkv) + got_qkv.astype(jnp.float32)
        total_qkv = total_qkv.astype(jnp.bfloat16)
        qkv_x, qkv_y, total_qkv = together((*first_parts(total_qkv), total_qkv))
        qkv_x, qkv_y = swap(qkv_x, 2), swap(qkv_y, 4)
        proj_x, proj_y = together((proj_x, proj_y), total_qkv)
        proj_over, proj_side, *proj_kept = second_parts(total_proj, proj_x, proj_y)
        proj_upper, proj_lower = swap(proj_over, 4), swap(proj_side, 2)
        grad_in_attn = after(grad_in_attn, proj_over, proj_side)
    else:
        total_qkv = contract_rows(attn_in, grad_qkv).astype(jnp.bfloat16)
        grad_in_attn = contract_cols(grad_qkv, qkv_full)
    grad_qv_b = jnp.concatenate(
        [
            jnp.sum(grad_qkv[:, :width].astype(jnp.float32), axis=0),
            jnp.sum(grad_qkv[:, 2 * width :].astype(jnp.float32), axis=0),
        ]
    )
    mlp_out = matmul(after(act_low, grad_in_attn), down_full) + down_bias
    result = middle + gate_m * mlp_out
    if fast:
        grad_in_attn = after(grad_in_attn, mlp_out, grad_down_w)
    grad_input = grad_mid + norm_back(normed, inverse, grad_in_attn * (1.0 + scale_a))

    unit_mod = [
        jnp.sum(by_unit(value), axis=1)
        for value in (
            grad_in_attn,
            grad_in_attn * normed,
            grad_mid * attn_out,
            grad_in_mlp,
            grad_in_mlp * normed_mlp,
            grad_out * mlp_out,
        )
    ]
    biases = [part[None, :] for part in (grad_qv_b, grad_proj_b, grad_up_b, grad_down_b)]
    small = stack_rows(unit_mod + biases, width)
    if fast:
        qkv_x, qkv_y = together((qkv_x, qkv_y), small)
        qkv_over, qkv_side, *qkv_kept = second_parts(total_qkv, qkv_x, qkv_y)
        qkv_over, qkv_side = together((qkv_over, qkv_side))
        small = after(small, qkv_over)
        grad_up_w = scatter_columns(after(grad_up, qkv_over))
        qkv_upper, qkv_lower = swap(qkv_over, 4), swap(qkv_side, 2)
        proj_upper, proj_lower = together((proj_upper, proj_lower), qkv_over)
        grad_proj = last_rows(*proj_kept, proj_upper, proj_lower)
        proj_parts = together(column_parts(grad_proj))
        qkv_upper, qkv_lower = together((qkv_upper, qkv_lower), proj_parts[0])
        grad_qkv_w = last_rows(*qkv_kept, qkv_upper, qkv_lower)
        both_parts = together(
            [
                jnp.concatenate(pair, axis=1)
                for pair in zip(column_parts(grad_qkv_w), proj_parts)
            ]
        )
        both_moved = rotate_parts(both_parts)
        last_sent = both_parts[:1]
        both = sum_wide(list(both_parts[:1]) + both_moved)
        grad_up_w = after(grad_up_w, both)
        grad_qkv_w, grad_proj_w = jnp.split(both, [qkv_weight.shape[1]], axis=1)
    else:
        grad_qkv_w = lax.psum_scatter(total_qkv, "bin", scatter_dimension=0, tiled=True)
        grad_qkv_w, grad_proj_w, grad_up_w, grad_down_w = [
            scatter_columns(part) for part in (grad_qkv_w, grad_proj, grad_up, grad_down)
        ]
        last_sent = []
    moved = together(rotations(small), *last_sent)
    small = in_order(small, moved)
    all_units = small[:, :12].reshape(shards, 6, 2, width).transpose(0, 2, 1, 3)
    all_units = all_units.reshape(2 * shards, 6 * width)
    biases = jnp.sum(small[:, 12:], axis=0).reshape(-1)
    picked = unit_segments[None, :] == jnp.arange(slots)[:, None]
    grad_mod = jnp.sum(jnp.where(picked[:, :, None], all_units[None], 0.0), axis=1)
    grad_mod = grad_mod.astype(jnp.bfloat16)
    own_width = grad_mod.shape[1] // (bins * shards)
    mod_view = grad_mod.reshape(slots, bins, shards, own_width)
    mod_columns = lax.dynamic_index_in_dim(mod_view, shard, axis=2, keepdims=False)
    spread = jnp.concatenate(
        [cond_low] + [part.reshape(slots, -1) for part in split_low(biases)], axis=1
    )
    spread = jnp.broadcast_to(spread[:, None, :], (slots, bins, spread.shape[1]))
    traded = lax.all_to_all(
        jnp.concatenate([mod_columns, spread], axis=2),
        "bin",
        split_axis=1,
        concat_axis=0,
        tiled=True,
    )[:, 0]
    grad_cond_act = contract_cols(after(grad_mod, *last_sent), ada_weight)
    grad_label = jax.vjp(jax.nn.silu, cond)[1](grad_cond_act)[0]
    cond_all = traded[:, own_width : own_width + width]
    grad_ada_w = contract_rows(cond_all, traded[:, :own_width])
    grad_ada_b = jnp.sum(traded[:, :own_width].astype(jnp.float32), axis=0)
    high, lower = jnp.split(traded[:, own_width + width :].astype(jnp.float32), 2, axis=1)
    biases = jnp.sum((high + lower).reshape(bins, -1), axis=0)

    hidden = up_bias.shape[0]
    ends = [2 * width, 3 * width, 3 * width + hidden]
    grad_qv_b, grad_proj_b, grad_up_b, grad_down_b = jnp.split(biases, ends)
    return (
        result,
        grad_input,
        grad_label,
        grad_ada_w,
        grad_ada_b,
        grad_qkv_w.astype(jnp.float32),
        grad_qv_b,
        grad_proj_w.astype(jnp.float32),
        grad_proj_b,
        grad_up_w.astype(jnp.float32),
        grad_up_b,
        grad_down_w.astype(jnp.float32),
        grad_down_b,
    )


def solution(mesh):
    placed = (
        P(("bin", "shard"), None),
        P("bin", None),
        P("bin"),
        P("bin"),
        P(),
        P(),
        P("bin", "shard"),
        P(),
        P("bin", "shard"),
        P(),
        P("bin", "shard"),
        P(),
        P("bin", "shard"),
        P(),
        P("bin"),
        P(("bin", "shard"), None),
    )
    return jax.shard_map(
        per_device,
        mesh=mesh,
        in_specs=placed,
        out_specs=(
            P(("bin", "shard"), None),
            P(("bin", "shard"), None),
            P("bin", None),
            P(None, ("bin", "shard")),
            P(("bin", "shard")),
            P("bin", "shard"),
            P(),
            P("bin", "shard"),
            P(),
            P("bin", "shard"),
            P(),
            P("bin", "shard"),
            P(),
        ),
        check_vma=False,
    )
```

time: 927 us -> 587 us (0.63)
  waiting for transfers between devices: 473 us -> 155 us
  blocking collectives: 103 us -> 0 us
  starting transfers between devices: 30.3 us -> 91.8 us
  other arithmetic: 38.4 us -> 59.5 us
  matrix products: 147 us -> 133 us
    reduce_scatter x4 -> x2, waiting for transfers between devices: 219 us -> 0.04 us  [the longest x1 0.02 us: per_device(): lax.psum_scatter(grad_down, 'bin', scatter_dimension=0, tiled=True)]
    all_gather x6 -> x2, waiting for transfers between devices: 129 us -> 0.01 us  [the longest x1 0.01 us: per_device(): qkv_full = lax.all_gather(qkv_wide, 'bin', axis=0, tiled=True)]
    ppermute x8 -> x54, waiting for transfers between devices: 28.9 us -> 154 us  [the longest x18 56.1 us: rotate(): lax.ppermute(value, 'shard', [(at, (at + step) % count) for at in range(c...]
    unnamed x19 -> x8, waiting for transfers between devices: 95.6 us -> 0.12 us
    ppermute x8 -> x54, starting transfers between devices: 25.4 us -> 87.4 us  [the longest x28 36.9 us: swap(): return lax.ppermute(value, 'bin', flipped(mask))]
    all_gather x3 -> x0, blocking collectives: 61.8 us -> none  [the longest x2 51.7 us: gather_weight(): wide = lax.all_gather(local, 'shard', axis=1, tiled=True)]
    psum x1 -> x0, blocking collectives: 41.1 us -> none  [per_device(): grad_qv_b = lax.psum(grad_qv_b, ('bin', 'shard'))]
    convert_element_type x7 -> x11, other arithmetic: 8.77 us -> 26 us  [the longest x1 9.33 us: per_device(): slope = lax.optimization_barrier(slope.astype(jnp.bfloat16))]
  transfers between devices with their start and end apart: 24 -> 61, of which waited for: 13 -> 19; matrix products, arithmetic and copies ran while one was open for 20% -> 38% of each run, Pallas kernels for 5% -> 8%
where the time goes in v2:
time: 587 us; the launch traced here: 576 us
  waiting for transfers between devices  155 us (26%)
  matrix products  133 us (23%)
  starting transfers between devices  91.8 us (16%)
  local copies, waits for them, and re-layouts  69.6 us (12%)
  other arithmetic  59.5 us (10%)
  Pallas kernels  44.8 us (8%)
  between operations  22.3 us (4%)
    dot_general x10, matrix products, matmul(): return jnp.dot(left, right, preferred_element_type=jnp.float32)  62.2 us
    ppermute x18, waiting for transfers between devices, rotate(): lax.ppermute(value, 'shard', [(at, (at + step) % count) for at in range(c...  56.1 us
    dot_general x5, matrix products, contract_cols(): lax.dot_general(left, right, (((1,), (1,)), ((), ())), preferred_element_...  48.2 us
    ppermute x28, waiting for transfers between devices, swap(): return lax.ppermute(value, 'bin', flipped(mask))  38.9 us
    ppermute x28, starting transfers between devices, swap(): return lax.ppermute(value, 'bin', flipped(mask))  36.9 us
    unnamed x235, local copies, waits for them, and re-layouts  34.1 us
    ppermute x2, waiting for transfers between devices, send_halo(): right = lax.ppermute(own, 'shard', chain(shards, -1))  33.6 us
    ppermute x18, starting transfers between devices, rotate(): lax.ppermute(value, 'shard', [(at, (at + step) % count) for at in range(c...  24.6 us
  transfers between devices with their start and end apart: 61, of which 19 were waited for; matrix products, arithmetic and copies ran while one was open for 38% of the time, Pallas kernels for 8%

profile of v2, /device:TPU:8, one launch (start us, length us, event | category | flops | bytes accessed | tf_op | source)
XLA Modules:
  0.0 576.1 jit_solution(5112842768965056107)
XLA Ops:
  7.2 2.7 collective-permute-start.1
  9.9 2.0 collective-permute-start.2
  22.0 7.8 %convolution_add_fusion = f32[8,6912]{1,0:T(8,128)S(1)} fusion(bf16[8,1152]{1,0:T(8,128)(2,1)S(1)} %multiply_convert_fusion.1, bf16[1152,6912]{1,0:T(8,128)(2,1)} %param.20, f32[6912]{0:T(1024)} %param.21), kind=kOutput, calls=%fused_computation.27 | convolution fusion | flops 127457280 | bytes 16192512 | tf_op jit(solution)/shard_map/dot_general | solution.py:370
  35.1 2.8 reshape.341
  38.8 2.9 collective-permute-start.8
  41.7 2.8 collective-permute-start.5
  45.2 2.9 collective-permute-start.3
  48.1 14.9 %collective-permute-done.8 = bf16[144,288]{1,0:T(8,128)(2,1)S(1)} collective-permute-done((bf16[144,288]{1,0:T(8,128)(2,1)S(1)}, bf16[144,288]{1,0:T(8,128)(2,1)S(1)}, u32[]{:S(2)}, u32[]{:S(2)}) %collective-permute-start.8) | collective-permute-done | bytes 82976 | tf_op jit(solution)/shard_map/ppermute | solution.py:394
  64.9 4.5 collective-permute-start.6
  70.2 33.6 %collective-permute-done.7 = bf16[512,1152]{1,0:T(8,128)(2,1)} collective-permute-done((bf16[512,1152]{1,0:T(8,128)(2,1)S(1)}, bf16[512,1152]{1,0:T(8,128)(2,1)}, u32[]{:S(2)}, u32[]{:S(2)}) %collective-permute-start.7) | collective-permute-done | bytes 1179680 | tf_op jit(solution)/shard_map/ppermute | solution.py:342
  119.1 2.6 collective-permute-start.11
  121.7 3.2 collective-permute-start.12
  124.9 3.3 collective-permute-done.14.refs_2_
  128.3 3.6 collective-permute-done.13.refs_1_
  132.0 2.5 collective-permute-start.15
  134.6 8.4 %add_convert_fusion.2.own = bf16[512,3456]{1,0:T(8,128)(2,1)S(1)} fusion(bf16[512,1152]{1,0:T(8,128)(2,1)S(1)} %copy-done.29, bf16[1152,3456]{1,0:T(8,128)(2,1)} %all-gather.3.cloned.1.call-done, f32[3456]{0:T(1024)S(1)} %pad_maximum_fusion.7), kind=kOutput, calls=%fused_computation.29 | convolution fusion | flops 4080402432 | bytes 12695040 | tf_op jit(solution)/shard_map/dot_general | solution.py:370
  145.3 2.8 convert_reduce_fusion.1
  149.7 8.9 %add_convert_fusion.halo.qh = bf16[768,3456]{1,0:T(8,128)(2,1)} fusion(bf16[768,1152]{1,0:T(8,128)(2,1)S(1)} %fusion.20, bf16[1152,3456]{1,0:T(8,128)(2,1)S(1)} %copy-done.80, f32[3456]{0:T(1024)S(1)} %pad_maximum_fusion.7), kind=kOutput, calls=%fused_computation.8 | convolution fusion | flops 6120603648 | bytes 15054336 | tf_op jit(solution)/shard_map/dot_general | solution.py:370
  159.3 8.6 %attend.1 = (bf16[512,1152]{1,0:T(8,128)(2,1)S(1)}, f32[512,128]{1,0:T(8,128)S(1)}) custom-call(s32[3]{0:T(128)S(1)} %pad_add_fusion.meta, bf16[512,3456]{1,0:T(8,128)(2,1)S(1)} %add_convert_fusion.2.own, bf16[768,3456]{1,0:T(8,128)(2,1)} %add_convert_fusion.halo.qh), custom_call_target="tpu_custom_call" | custom-call | flops 8589934592 | bytes 10485760 | tf_op jit(solution)/shard_map/attend/pallas_call | solution.py:105
  173.5 2.0 collective-permute-start.26
  175.6 7.7 %collective-permute-start.25 = (bf16[576,1152]{1,0:T(8,128)(2,1)S(1)}, bf16[576,1152]{1,0:T(8,128)(2,1)}, u32[]{:S(2)}, u32[]{:S(2)}) collective-permute-start(bf16[576,1152]{1,0:T(8,128)(2,1)S(1)} %copy.102.refs_0_), channel_id=1, source_target_pairs={{0,8},{4,12},{8,0},{12,4},{16,24},{20,28},{24,16},{28,20},{1,9},{5... | collective-permute-start | bytes 3981320 | tf_op jit(solution)/shard_map/ppermute | solution.py:390
  187.5 2.6 fusion.34
  193.1 2.4 place_rows.2
  195.6 3.3 fusion.76
  201.3 6.1 %collective-permute-done.26.refs_2_ = bf16[576,1152]{1,0:T(8,128)(2,1)} collective-permute-done((bf16[576,1152]{1,0:T(8,128)(2,1)S(1)}, bf16[576,1152]{1,0:T(8,128)(2,1)}, u32[]{:S(2)}, u32[]{:S(2)}) %collective-permute-start.26) | collective-permute-done | bytes 1327136 | tf_op jit(solution)/shard_map/ppermute | solution.py:390
  211.5 13.1 %fusion.14 = (bf16[512,4608]{1,0:T(8,128)(2,1)S(1)}, f32[512,4608]{1,0:T(8,128)}) fusion(f32[4608]{0:T(1024)S(1)} %copy-done.82, bf16[512,1152]{1,0:T(8,128)(2,1)} %fusion.37, bf16[1152,4608]{1,0:T(8,128)(2,1)} %all-gather.5.cloned.1.call-done), kind=kOutput, calls=%fused_computation.23 | convolution fusion | flops 5459410944 | bytes 25970688 | tf_op jit(solution)/shard_map/dot_general | solution.py:370
  224.6 2.1 copy-done.27
  226.7 9.0 %convolution_convert_fusion.1 = bf16[4608,1152]{1,0:T(8,128)(2,1)} fusion(bf16[512,4608]{1,0:T(8,128)(2,1)S(1)} %get-tuple-element.167, bf16[512,1152]{1,0:T(8,128)(2,1)S(1)} %copy-done.28), kind=kOutput, calls=%fused_computation.4 | convolution fusion | flops 5441126400 | bytes 16515072 | tf_op jit(solution)/shard_map/dot_general | solution.py:374
  238.8 9.3 %fusion.6 = bf16[512,4608]{1,0:T(8,128)(2,1)} fusion(f32[512,4608]{1,0:T(8,128)} %get-tuple-element.143), kind=kLoop, calls=%fused_computation.15 | loop fusion | flops 42467328 | bytes 14155776 | tf_op jit(solution)/shard_map/convert_element_type | solution.py:670
  248.2 7.4 %collective-permute-done.28.refs_4_ = bf16[288,1152]{1,0:T(8,128)(2,1)} collective-permute-done((bf16[288,1152]{1,0:T(8,128)(2,1)}, bf16[288,1152]{1,0:T(8,128)(2,1)}, u32[]{:S(2)}, u32[]{:S(2)}) %collective-permute-start.28) | collective-permute-done | bytes 663584 | tf_op jit(solution)/shard_map/ppermute | solution.py:390
  256.2 2.5 collective-permute-done.32.refs_8_
  259.0 4.2 place_rows.3
  263.2 13.5 %convert_reduce_fusion = (f32[4608]{0:T(1024)}, bf16[512,4608]{1,0:T(8,128)(2,1)}) fusion(bf16[512,4608]{1,0:T(8,128)(2,1)} %fusion.6, bf16[512,1152]{1,0:T(8,128)(2,1)} %fusion.34, bf16[4608,1152]{1,0:T(8,128)(2,1)S(1)} %place_rows.3), kind=kOutput, calls=%fused_computation.24 | convolution fusion | flops 5447609856 | bytes 21252096 | tf_op jit(solution)/shard_map/dot_general | solution.py:380
  276.8 10.6 %convolution_convert_fusion = bf16[1152,4608]{1,0:T(8,128)(2,1)} fusion(bf16[512,1152]{1,0:T(8,128)(2,1)S(1)} %copy-done.37, bf16[512,4608]{1,0:T(8,128)(2,1)} %get-tuple-element.146), kind=kOutput, calls=%fused_computation.3 | convolution fusion | flops 5441126400 | bytes 16515072 | tf_op jit(solution)/shard_map/dot_general | solution.py:374
  302.1 11.6 %fusion.44 = (f32[512]{0:T(512)S(1)}, f32[512]{0:T(512)S(1)}, f32[512,1152]{1,0:T(8,128)S(1)}) fusion(f32[2,1152]{1,0:T(2,128)S(1)} %copy-done.58, f32[512]{0:T(512)S(1)} %copy-done.66, f32[512,1152]{1,0:T(8,128)S(1)} %copy-done.16, f32[512]{0:T(512)S(1)} %broadcast_multiply_fusion.5, bf16[512,4608]{1,0:T(8,128)(2,1)} %get-tuple-element.146, ...), kind=kOutput, calls=%fused_computation.100 | convolution fusion | flops 5439355904 | bytes 20071424 | tf_op jit(solution)/shard_map/dot_general | solution.py:380
  313.7 2.9 convert_reduce_fusion.4
  320.3 2.1 fusion.59
  322.5 2.4 collective-permute-start.35
  325.0 3.4 collective-permute-start.34
  329.8 6.3 %collective-permute-start.36 = (bf16[256,1280]{1,0:T(8,128)(2,1)S(1)}, bf16[256,1280]{1,0:T(8,128)(2,1)}, u32[]{:S(2)}, u32[]{:S(2)}) collective-permute-start(bf16[256,1280]{1,0:T(8,128)(2,1)S(1)} %get-tuple-element.287), channel_id=1, source_target_pairs={{0,2},{1,3},{4,6},{5,7},{8,10},{9,11},{12,14},{13,15},{16,18},{17,... | collective-permute-start | bytes 1966088 | tf_op jit(solution)/shard_map/ppermute | solution.py:347
  338.3 20.2 %own_back.1 = (bf16[512,1152]{1,0:T(8,128)(2,1)}, f32[512,1152]{1,0:T(8,128)}, f32[512,1152]{1,0:T(8,128)}) custom-call(s32[3]{0:T(128)} %copy-done.11, bf16[512,3456]{1,0:T(8,128)(2,1)} %copy-done.12, bf16[768,3456]{1,0:T(8,128)(2,1)} %add_convert_fusion.halo.qh, bf16[512,1152]{1,0:T(8,128)(2,1)} %copy-done.21, f32[512,128]{1,0:T(8,128)} %get-tuple-element.349.stats), custom_call_target="tpu_custom_call" | custom-call | flops 17179869184 | bytes 20971520 | tf_op jit(solution)/shard_map/own_back/pallas_call | solution.py:194
  358.5 11.6 %collective-permute-done.37.far_right = bf16[256,1280]{1,0:T(8,128)(2,1)S(1)} collective-permute-done((bf16[256,1280]{1,0:T(8,128)(2,1)S(1)}, bf16[256,1280]{1,0:T(8,128)(2,1)S(1)}, u32[]{:S(2)}, u32[]{:S(2)}) %collective-permute-start.37) | collective-permute-done | bytes 655392 | tf_op jit(solution)/shard_map/ppermute | solution.py:348
  370.2 14.2 %collective-permute-done.36.far_left = bf16[256,1280]{1,0:T(8,128)(2,1)} collective-permute-done((bf16[256,1280]{1,0:T(8,128)(2,1)S(1)}, bf16[256,1280]{1,0:T(8,128)(2,1)}, u32[]{:S(2)}, u32[]{:S(2)}) %collective-permute-start.36) | collective-permute-done | bytes 655392 | tf_op jit(solution)/shard_map/ppermute | solution.py:347
  384.4 9.3 %halo_back.1 = bf16[512,3456]{1,0:T(8,128)(2,1)} custom-call(s32[3]{0:T(128)} %copy-done.11, bf16[512,3456]{1,0:T(8,128)(2,1)} %copy-done.12, bf16[768,3456]{1,0:T(8,128)(2,1)} %add_convert_fusion.halo.qh, bf16[256,1280]{1,0:T(8,128)(2,1)} %collective-permute-done.36.far_left, bf16[512,1280]{1,0:T(8,128)(2,1)} %collective-permute-done.34.left, ...), custom_call_target="tpu_custom_call" | custom-call | flops 8589934592 | bytes 20971520 | tf_op jit(solution)/shard_map/halo_back/pallas_call | solution.py:285
  393.7 6.3 %convolution_convert_fusion.2 = bf16[576,3456]{1,0:T(8,128)(2,1)} fusion(bf16[576,512]{1,0:T(8,128)(2,1)S(1)} %copy-done.74, bf16[512,3456]{1,0:T(8,128)(2,1)} %halo_back.1), kind=kOutput, calls=%fused_computation.30 | convolution fusion | flops 2040422400 | bytes 8110080 | tf_op jit(solution)/shard_map/dot_general | solution.py:370
  400.0 9.1 %collective-permute-start.41 = (bf16[576,3456]{1,0:T(8,128)(2,1)}, bf16[576,3456]{1,0:T(8,128)(2,1)}, u32[]{:S(2)}, u32[]{:S(2)}) collective-permute-start(bf16[576,3456]{1,0:T(8,128)(2,1)} %convolution_convert_fusion.2), channel_id=1, source_target_pairs={{0,4},{4,0},{8,12},{12,8},{16,20},{20,16},{24,28},{28,24},{1,5},{5... | collective-permute-start | bytes 11943944 | tf_op jit(solution)/shard_map/ppermute | solution.py:390
  411.2 2.3 bitcast_reduce_fusion.1
  413.7 2.0 collective-permute-start.39
  416.1 2.6 copy.119
  419.0 10.8 %fusion.84 = f32[512,1152]{1,0:T(8,128)} fusion(bf16[512,3456]{1,0:T(8,128)(2,1)} %halo_back.1, bf16[1152,3456]{1,0:T(8,128)(2,1)} %all-gather.3.cloned.1.call-done), kind=kOutput, calls=%fused_computation.327 | convolution fusion | flops 4076863488 | bytes 13860864 | tf_op jit(solution)/shard_map/dot_general | solution.py:380
  429.9 4.7 add_convert_fusion.1
  436.6 2.9 add_convert_fusion.11
  445.3 7.8 %fusion.35 = (f32[512,1152]{1,0:T(8,128)}, f32[512,1152]{1,0:T(8,128)S(1)}) fusion(f32[512,1152]{1,0:T(8,128)S(1)} %copy-done.16, f32[2,1152]{1,0:T(2,128)S(1)} %get-tuple-element.326, f32[1152]{0:T(1024)S(1)} %copy-done.75, bf16[512,4608]{1,0:T(8,128)(2,1)S(1)} %bitcast.384, bf16[4608,1152]{1,0:T(8,128)(2,1)S(1)} %bitcast.377), kind=kOutput, calls=%fused_computation.73 | convolution fusion | flops 5437587456 | bytes 22427136 | tf_op jit(solution)/shard_map/dot_general | solution.py:370
  454.7 2.6 fusion.43
  459.1 2.5 fusion.78
  461.9 6.8 %collective-permute-done.43 = bf16[128,3456]{1,0:T(8,128)(2,1)} collective-permute-done((bf16[128,3456]{1,0:T(8,128)(2,1)}, bf16[128,3456]{1,0:T(8,128)(2,1)}, u32[]{:S(2)}, u32[]{:S(2)}) %collective-permute-start.43) | collective-permute-done | bytes 884768 | tf_op jit(solution)/shard_map/ppermute | solution.py:390
  469.5 2.1 add_convert_fusion.5
  471.6 2.0 add_convert_fusion.7
  483.0 2.4 copy.121
  485.4 6.7 %collective-permute-done.48 = bf16[64,3456]{1,0:T(8,128)(2,1)} collective-permute-done((bf16[64,3456]{1,0:T(8,128)(2,1)}, bf16[64,3456]{1,0:T(8,128)(2,1)}, u32[]{:S(2)}, u32[]{:S(2)}) %collective-permute-start.48) | collective-permute-done | bytes 442400 | tf_op jit(solution)/shard_map/ppermute | solution.py:390
  503.9 10.4 %fusion.63 = f32[8,1152]{1,0:T(8,128)} fusion(f32[8,1152]{1,0:T(8,128)S(1)} %copy-done.54, f32[8,576]{1,0:T(8,128)S(1)} %copy-done.51, f32[8,576]{1,0:T(8,128)S(1)} %copy-done.49, bf16[8,6912]{1,0:T(8,128)(2,1)S(1)} %select_reduce_fusion, bf16[1152,6912]{1,0:T(8,128)(2,1)} %param.20), kind=kOutput, calls=%fused_computation.260 | convolution fusion | flops 127503360 | bytes 16146432 | tf_op jit(solution)/shard_map/dot_general | solution.py:380
  515.4 3.5 all-to-all-start
  518.9 14.5 %collective-permute-done.51 = bf16[144,1152]{1,0:T(8,128)(2,1)S(1)} collective-permute-done((bf16[144,1152]{1,0:T(8,128)(2,1)S(1)}, bf16[144,1152]{1,0:T(8,128)(2,1)S(1)}, u32[]{:S(2)}, u32[]{:S(2)}) %collective-permute-start.51) | collective-permute-done | bytes 331808 | tf_op jit(solution)/shard_map/ppermute | solution.py:394
  533.4 25.6 %collective-permute-done.52 = bf16[144,1152]{1,0:T(8,128)(2,1)S(1)} collective-permute-done((bf16[144,1152]{1,0:T(8,128)(2,1)S(1)}, bf16[144,1152]{1,0:T(8,128)(2,1)S(1)}, u32[]{:S(2)}, u32[]{:S(2)}) %collective-permute-start.52) | collective-permute-done | bytes 331808 | tf_op jit(solution)/shard_map/ppermute | solution.py:394
  (466 shorter events, 125.0 us)
Async XLA Ops:
  7.2 127.4 %all-gather.3.cloned.1.call-start = ((), (), s32[]{:S(2)}) async-start(), calls=%async_computation.5 | async-start | bytes 8957952 | tf_op jit(solution)/shard_map/all_gather | solution.py:611
  7.2 26.1 %collective-permute-start.1 = (bf16[144,864]{1,0:T(8,128)(2,1)}, bf16[144,864]{1,0:T(8,128)(2,1)S(1)}, u32[]{:S(2)}, u32[]{:S(2)}) collective-permute-start(bf16[144,864]{1,0:T(8,128)(2,1)} %param.22), channel_id=1, source_target_pairs={{0,2},{1,3},{2,0},{3,1},{4,6},{5,7},{6,4},{7,5},{8,10},{9,11},{10,... | collective-permute-start | bytes 746504 | tf_op jit(solution)/shard_map/ppermute | solution.py:394
  9.9 23.4 %collective-permute-start = (bf16[144,864]{1,0:T(8,128)(2,1)}, bf16[144,864]{1,0:T(8,128)(2,1)S(1)}, u32[]{:S(2)}, u32[]{:S(2)}) collective-permute-start(bf16[144,864]{1,0:T(8,128)(2,1)} %param.22), channel_id=1, source_target_pairs={{0,1},{1,2},{2,3},{3,0},{4,5},{5,6},{6,7},{7,4},{8,9},{9,10},{10,1... | collective-permute-start | bytes 746504 | tf_op jit(solution)/shard_map/ppermute | solution.py:394
  9.9 23.4 %collective-permute-start.2 = (bf16[144,864]{1,0:T(8,128)(2,1)}, bf16[144,864]{1,0:T(8,128)(2,1)S(1)}, u32[]{:S(2)}, u32[]{:S(2)}) collective-permute-start(bf16[144,864]{1,0:T(8,128)(2,1)} %param.22), channel_id=1, source_target_pairs={{0,3},{1,0},{2,1},{3,2},{4,7},{5,4},{6,5},{7,6},{8,11},{9,8},{10,9... | collective-permute-start | bytes 746504 | tf_op jit(solution)/shard_map/ppermute | solution.py:394
  31.1 164.5 %copy-start.55 = (f32[2,1152]{1,0:T(2,128)}, f32[2,1152]{1,0:T(2,128)S(1)}, u32[]{:S(2)}) copy-start(f32[2,1152]{1,0:T(2,128)S(1)} %get-tuple-element.330) | copy-start | bytes 27652
  31.1 168.2 %copy-start.57 = (f32[2,1152]{1,0:T(2,128)}, f32[2,1152]{1,0:T(2,128)S(1)}, u32[]{:S(2)}) copy-start(f32[2,1152]{1,0:T(2,128)S(1)} %get-tuple-element.327) | copy-start | bytes 27652
  37.9 173.6 %all-gather.5.cloned.1.call-start = ((), (), s32[]{:S(2)}) async-start(), calls=%async_computation.6 | async-start | bytes 11943936 | tf_op jit(solution)/shard_map/all_gather | solution.py:624
  37.9 7.3 %collective-permute-start.9 = (bf16[144,288]{1,0:T(8,128)(2,1)S(1)}, bf16[144,288]{1,0:T(8,128)(2,1)S(1)}, u32[]{:S(2)}, u32[]{:S(2)}) collective-permute-start(bf16[144,288]{1,0:T(8,128)(2,1)S(1)} %copy-done.39), channel_id=1, source_target_pairs={{0,2},{1,3},{2,0},{3,1},{4,6},{5,7},{6,4},{7,5},{8,10},{9,11},{10,... | collective-permute-start | bytes 248840 | tf_op jit(solution)/shard_map/ppermute | solution.py:394
  38.8 24.2 %collective-permute-start.8 = (bf16[144,288]{1,0:T(8,128)(2,1)S(1)}, bf16[144,288]{1,0:T(8,128)(2,1)S(1)}, u32[]{:S(2)}, u32[]{:S(2)}) collective-permute-start(bf16[144,288]{1,0:T(8,128)(2,1)S(1)} %copy-done.39), channel_id=1, source_target_pairs={{0,1},{1,2},{2,3},{3,0},{4,5},{5,6},{6,7},{7,4},{8,9},{9,10},{10,1... | collective-permute-start | bytes 248840 | tf_op jit(solution)/shard_map/ppermute | solution.py:394
  41.7 23.2 %collective-permute-start.10 = (bf16[144,288]{1,0:T(8,128)(2,1)S(1)}, bf16[144,288]{1,0:T(8,128)(2,1)S(1)}, u32[]{:S(2)}, u32[]{:S(2)}) collective-permute-start(bf16[144,288]{1,0:T(8,128)(2,1)S(1)} %copy-done.39), channel_id=1, source_target_pairs={{0,3},{1,0},{2,1},{3,2},{4,7},{5,4},{6,5},{7,6},{8,11},{9,8},{10,9... | collective-permute-start | bytes 248840 | tf_op jit(solution)/shard_map/ppermute | solution.py:394
  41.7 65.9 %collective-permute-start.5 = (bf16[144,1152]{1,0:T(8,128)(2,1)S(1)}, bf16[144,1152]{1,0:T(8,128)(2,1)S(1)}, u32[]{:S(2)}, u32[]{:S(2)}) collective-permute-start(bf16[144,1152]{1,0:T(8,128)(2,1)S(1)} %copy-done.36), channel_id=1, source_target_pairs={{0,3},{1,0},{2,1},{3,2},{4,7},{5,4},{6,5},{7,6},{8,11},{9,8},{10,9... | collective-permute-start | bytes 995336 | tf_op jit(solution)/shard_map/ppermute | solution.py:394
  44.5 63.1 %collective-permute-start.4 = (bf16[144,1152]{1,0:T(8,128)(2,1)S(1)}, bf16[144,1152]{1,0:T(8,128)(2,1)}, u32[]{:S(2)}, u32[]{:S(2)}) collective-permute-start(bf16[144,1152]{1,0:T(8,128)(2,1)S(1)} %copy-done.36), channel_id=1, source_target_pairs={{0,2},{1,3},{2,0},{3,1},{4,6},{5,7},{6,4},{7,5},{8,10},{9,11},{10,... | collective-permute-start | bytes 995336 | tf_op jit(solution)/shard_map/ppermute | solution.py:394
  45.2 62.4 %collective-permute-start.3 = (bf16[144,1152]{1,0:T(8,128)(2,1)S(1)}, bf16[144,1152]{1,0:T(8,128)(2,1)}, u32[]{:S(2)}, u32[]{:S(2)}) collective-permute-start(bf16[144,1152]{1,0:T(8,128)(2,1)S(1)} %copy-done.36), channel_id=1, source_target_pairs={{0,1},{1,2},{2,3},{3,0},{4,5},{5,6},{6,7},{7,4},{8,9},{9,10},{10,1... | collective-permute-start | bytes 995336 | tf_op jit(solution)/shard_map/ppermute | solution.py:394
  63.0 40.8 %collective-permute-start.7 = (bf16[512,1152]{1,0:T(8,128)(2,1)S(1)}, bf16[512,1152]{1,0:T(8,128)(2,1)}, u32[]{:S(2)}, u32[]{:S(2)}) collective-permute-start(bf16[512,1152]{1,0:T(8,128)(2,1)S(1)} %copy-done.17), channel_id=1, source_target_pairs={{1,0},{2,1},{3,2},{5,4},{6,5},{7,6},{9,8},{10,9},{11,10},{13,12},{... | collective-permute-start | bytes 3538952 | tf_op jit(solution)/shard_map/ppermute | solution.py:342
  64.9 38.9 %collective-permute-start.6 = (bf16[512,1152]{1,0:T(8,128)(2,1)S(1)}, bf16[512,1152]{1,0:T(8,128)(2,1)}, u32[]{:S(2)}, u32[]{:S(2)}) collective-permute-start(bf16[512,1152]{1,0:T(8,128)(2,1)S(1)} %copy-done.17), channel_id=1, source_target_pairs={{0,1},{1,2},{2,3},{4,5},{5,6},{6,7},{8,9},{9,10},{10,11},{12,13},{... | collective-permute-start | bytes 3538952 | tf_op jit(solution)/shard_map/ppermute | solution.py:341
  113.2 302.9 %reduce-scatter.9.cloned.1.call-start = ((), (), s32[]{:S(2)}) async-start(), calls=%async_computation.7 | async-start | bytes 11943936 | tf_op jit(solution)/shard_map/reduce_scatter | solution.py:680
  115.9 43.3 %copy-start.11 = (s32[3]{0:T(128)}, s32[3]{0:T(128)S(1)}, u32[]{:S(2)}) copy-start(s32[3]{0:T(128)S(1)} %pad_add_fusion.meta) | copy-start | bytes 40
  116.0 12.3 %collective-permute-start.14 = (bf16[144,1152]{1,0:T(8,128)(2,1)S(1)}, bf16[144,1152]{1,0:T(8,128)(2,1)S(1)}, u32[]{:S(2)}, u32[]{:S(2)}) collective-permute-start(bf16[144,1152]{1,0:T(8,128)(2,1)S(1)} %reshape.342.refs_0_), channel_id=1, source_target_pairs={{0,16},{4,20},{8,24},{12,28},{16,0},{20,4},{24,8},{28,12},{1,17},{... | collective-permute-start | bytes 995336 | tf_op jit(solution)/shard_map/ppermute | solution.py:390
  117.6 14.4 %collective-permute-start.13 = (bf16[144,1152]{1,0:T(8,128)(2,1)S(1)}, bf16[144,1152]{1,0:T(8,128)(2,1)S(1)}, u32[]{:S(2)}, u32[]{:S(2)}) collective-permute-start(bf16[144,1152]{1,0:T(8,128)(2,1)S(1)} %reshape.342.refs_0_), channel_id=1, source_target_pairs={{0,8},{4,12},{8,0},{12,4},{16,24},{20,28},{24,16},{28,20},{1,9},{5... | collective-permute-start | bytes 995336 | tf_op jit(solution)/shard_map/ppermute | solution.py:390
  119.1 24.0 %collective-permute-start.11 = (bf16[256,1152]{1,0:T(8,128)(2,1)}, bf16[256,1152]{1,0:T(8,128)(2,1)S(1)}, u32[]{:S(2)}, u32[]{:S(2)}) collective-permute-start(bf16[256,1152]{1,0:T(8,128)(2,1)} %slice.342), channel_id=1, source_target_pairs={{0,1},{1,2},{2,3},{4,5},{5,6},{6,7},{8,9},{9,10},{10,11},{12,13},{... | collective-permute-start | bytes 1769480 | tf_op jit(solution)/shard_map/ppermute | solution.py:347
  121.7 21.3 %collective-permute-start.12 = (bf16[256,1152]{1,0:T(8,128)(2,1)}, bf16[256,1152]{1,0:T(8,128)(2,1)}, u32[]{:S(2)}, u32[]{:S(2)}) collective-permute-start(bf16[256,1152]{1,0:T(8,128)(2,1)} %slice.343), channel_id=1, source_target_pairs={{1,0},{2,1},{3,2},{5,4},{6,5},{7,6},{9,8},{10,9},{11,10},{13,12},{... | collective-permute-start | bytes 1769480 | tf_op jit(solution)/shard_map/ppermute | solution.py:348
  131.9 26.7 %collective-permute-start.16 = (bf16[64,1152]{1,0:T(8,128)(2,1)S(1)}, bf16[64,1152]{1,0:T(8,128)(2,1)S(1)}, u32[]{:S(2)}, u32[]{:S(2)}) collective-permute-start(bf16[64,1152]{1,0:T(8,128)(2,1)S(1)} %slice.349), channel_id=1, source_target_pairs={{0,16},{4,20},{8,24},{12,28},{16,0},{20,4},{24,8},{28,12},{1,17},{... | collective-permute-start | bytes 442376 | tf_op jit(solution)/shard_map/ppermute | solution.py:390
  132.0 27.2 %collective-permute-start.15 = (bf16[80,1152]{1,0:T(8,128)(2,1)S(1)}, bf16[80,1152]{1,0:T(8,128)(2,1)}, u32[]{:S(2)}, u32[]{:S(2)}) collective-permute-start(bf16[80,1152]{1,0:T(8,128)(2,1)S(1)} %slice.348), channel_id=1, source_target_pairs={{0,8},{4,12},{8,0},{12,4},{16,24},{20,28},{24,16},{28,20},{1,9},{5... | collective-permute-start | bytes 552968 | tf_op jit(solution)/shard_map/ppermute | solution.py:390
  143.0 24.8 %collective-permute-start.24 = (bf16[576,288]{0,1:T(8,128)(2,1)}, bf16[576,288]{0,1:T(8,128)(2,1)S(1)}, u32[]{:S(2)}, u32[]{:S(2)}) collective-permute-start(bf16[576,288]{0,1:T(8,128)(2,1)} %param.28), channel_id=1, source_target_pairs={{0,3},{1,0},{2,1},{3,2},{4,7},{5,4},{6,5},{7,6},{8,11},{9,8},{10,9... | collective-permute-start | bytes 995336 | tf_op jit(solution)/shard_map/ppermute | solution.py:394
  143.1 24.8 %collective-permute-start.23 = (bf16[576,288]{0,1:T(8,128)(2,1)}, bf16[576,288]{0,1:T(8,128)(2,1)S(1)}, u32[]{:S(2)}, u32[]{:S(2)}) collective-permute-start(bf16[576,288]{0,1:T(8,128)(2,1)} %param.28), channel_id=1, source_target_pairs={{0,2},{1,3},{2,0},{3,1},{4,6},{5,7},{6,4},{7,5},{8,10},{9,11},{10,... | collective-permute-start | bytes 995336 | tf_op jit(solution)/shard_map/ppermute | solution.py:394
  144.5 23.5 %collective-permute-start.22 = (bf16[576,288]{0,1:T(8,128)(2,1)}, bf16[576,288]{0,1:T(8,128)(2,1)S(1)}, u32[]{:S(2)}, u32[]{:S(2)}) collective-permute-start(bf16[576,288]{0,1:T(8,128)(2,1)} %param.28), channel_id=1, source_target_pairs={{0,1},{1,2},{2,3},{3,0},{4,5},{5,6},{6,7},{7,4},{8,9},{9,10},{10,1... | collective-permute-start | bytes 995336 | tf_op jit(solution)/shard_map/ppermute | solution.py:394
  173.5 33.9 %collective-permute-start.26 = (bf16[576,1152]{1,0:T(8,128)(2,1)S(1)}, bf16[576,1152]{1,0:T(8,128)(2,1)}, u32[]{:S(2)}, u32[]{:S(2)}) collective-permute-start(bf16[576,1152]{1,0:T(8,128)(2,1)S(1)} %copy.102.refs_0_), channel_id=1, source_target_pairs={{0,16},{4,20},{8,24},{12,28},{16,0},{20,4},{24,8},{28,12},{1,17},{... | collective-permute-start | bytes 3981320 | tf_op jit(solution)/shard_map/ppermute | solution.py:390
  175.6 32.0 %collective-permute-start.25 = (bf16[576,1152]{1,0:T(8,128)(2,1)S(1)}, bf16[576,1152]{1,0:T(8,128)(2,1)}, u32[]{:S(2)}, u32[]{:S(2)}) collective-permute-start(bf16[576,1152]{1,0:T(8,128)(2,1)S(1)} %copy.102.refs_0_), channel_id=1, source_target_pairs={{0,8},{4,12},{8,0},{12,4},{16,24},{20,28},{24,16},{28,20},{1,9},{5... | collective-permute-start | bytes 3981320 | tf_op jit(solution)/shard_map/ppermute | solution.py:390
  183.2 1.6 collective-permute-start.17
  183.2 2.5 collective-permute-start.19
  183.7 6.5 %collective-permute-start.18 = (bf16[144,1152]{1,0:T(8,128)(2,1)S(1)}, bf16[144,1152]{1,0:T(8,128)(2,1)}, u32[]{:S(2)}, u32[]{:S(2)}) collective-permute-start(bf16[144,1152]{1,0:T(8,128)(2,1)S(1)} %collective-permute-done.13.refs_1_), channel_id=1, source_target_pairs={{0,4},{4,0},{8,12},{12,8},{16,20},{20,16},{24,28},{28,24},{1,5},{5... | collective-permute-start | bytes 995336 | tf_op jit(solution)/shard_map/ppermute | solution.py:390
  185.6 4.6 collective-permute-start.20
  186.5 3.7 collective-permute-start.21
  235.7 180.4 %reduce-scatter.11.cloned.1.call-start = ((), (), s32[]{:S(2)}) async-start(), calls=%async_computation.8 | async-start | bytes 11943936 | tf_op jit(solution)/shard_map/reduce_scatter | solution.py:687
  236.2 20.0 %collective-permute-start.29 = (bf16[576,1152]{1,0:T(8,128)(2,1)S(1)}, bf16[576,1152]{1,0:T(8,128)(2,1)}, u32[]{:S(2)}, u32[]{:S(2)}) collective-permute-start(bf16[576,1152]{1,0:T(8,128)(2,1)S(1)} %copy.102.refs_0_), channel_id=1, source_target_pairs={{0,4},{4,0},{8,12},{12,8},{16,20},{20,16},{24,28},{28,24},{1,5},{5... | collective-permute-start | bytes 3981320 | tf_op jit(solution)/shard_map/ppermute | solution.py:390
  236.3 19.2 %collective-permute-start.27 = (bf16[288,1152]{1,0:T(8,128)(2,1)}, bf16[288,1152]{1,0:T(8,128)(2,1)S(1)}, u32[]{:S(2)}, u32[]{:S(2)}) collective-permute-start(bf16[288,1152]{1,0:T(8,128)(2,1)} %slice.350), channel_id=1, source_target_pairs={{0,8},{4,12},{8,0},{12,4},{16,24},{20,28},{24,16},{28,20},{1,9},{5... | collective-permute-start | bytes 1990664 | tf_op jit(solution)/shard_map/ppermute | solution.py:390
  237.8 18.4 %collective-permute-start.31 = (bf16[576,1152]{1,0:T(8,128)(2,1)}, bf16[576,1152]{1,0:T(8,128)(2,1)}, u32[]{:S(2)}, u32[]{:S(2)}) collective-permute-start(bf16[576,1152]{1,0:T(8,128)(2,1)} %collective-permute-done.26.refs_2_), channel_id=1, source_target_pairs={{0,4},{4,0},{8,12},{12,8},{16,20},{20,16},{24,28},{28,24},{1,5},{5... | collective-permute-start | bytes 3981320 | tf_op jit(solution)/shard_map/ppermute | solution.py:390
  237.9 18.3 %collective-permute-start.30 = (bf16[576,1152]{1,0:T(8,128)(2,1)}, bf16[576,1152]{1,0:T(8,128)(2,1)}, u32[]{:S(2)}, u32[]{:S(2)}) collective-permute-start(bf16[576,1152]{1,0:T(8,128)(2,1)} %collective-permute-done.25.refs_1_), channel_id=1, source_target_pairs={{0,4},{4,0},{8,12},{12,8},{16,20},{20,16},{24,28},{28,24},{1,5},{5... | collective-permute-start | bytes 3981320 | tf_op jit(solution)/shard_map/ppermute | solution.py:390
  238.3 17.3 %collective-permute-start.28 = (bf16[288,1152]{1,0:T(8,128)(2,1)}, bf16[288,1152]{1,0:T(8,128)(2,1)}, u32[]{:S(2)}, u32[]{:S(2)}) collective-permute-start(bf16[288,1152]{1,0:T(8,128)(2,1)} %slice.351), channel_id=1, source_target_pairs={{0,16},{4,20},{8,24},{12,28},{16,0},{20,4},{24,8},{28,12},{1,17},{... | collective-permute-start | bytes 1990664 | tf_op jit(solution)/shard_map/ppermute | solution.py:390
  255.6 3.2 collective-permute-start.32
  255.6 3.4 collective-permute-start.33
  287.4 166.1 %reduce-scatter.13.cloned.1.call-start = ((), (), s32[]{:S(2)}) async-start(), calls=%async_computation.9 | async-start | bytes 1843200
  317.6 18.6 %collective-permute-start.38 = (bf16[576,1152]{1,0:T(8,128)(2,1)S(1)}, bf16[576,1152]{1,0:T(8,128)(2,1)S(1)}, u32[]{:S(2)}, u32[]{:S(2)}) collective-permute-start(bf16[576,1152]{1,0:T(8,128)(2,1)S(1)} %convolution_convert_fusion.3), channel_id=1, source_target_pairs={{0,4},{4,0},{8,12},{12,8},{16,20},{20,16},{24,28},{28,24},{1,5},{5... | collective-permute-start | bytes 3981320 | tf_op jit(solution)/shard_map/ppermute | solution.py:390
  322.5 61.9 %collective-permute-start.35 = (bf16[512,1280]{1,0:T(8,128)(2,1)S(1)}, bf16[512,1280]{1,0:T(8,128)(2,1)}, u32[]{:S(2)}, u32[]{:S(2)}) collective-permute-start(bf16[512,1280]{1,0:T(8,128)(2,1)S(1)} %pad_maximum_fusion), channel_id=1, source_target_pairs={{1,0},{2,1},{3,2},{5,4},{6,5},{7,6},{9,8},{10,9},{11,10},{13,12},{... | collective-permute-start | bytes 3932168 | tf_op jit(solution)/shard_map/ppermute | solution.py:342
  325.0 59.4 %collective-permute-start.34 = (bf16[512,1280]{1,0:T(8,128)(2,1)S(1)}, bf16[512,1280]{1,0:T(8,128)(2,1)}, u32[]{:S(2)}, u32[]{:S(2)}) collective-permute-start(bf16[512,1280]{1,0:T(8,128)(2,1)S(1)} %pad_maximum_fusion), channel_id=1, source_target_pairs={{0,1},{1,2},{2,3},{4,5},{5,6},{6,7},{8,9},{9,10},{10,11},{12,13},{... | collective-permute-start | bytes 3932168 | tf_op jit(solution)/shard_map/ppermute | solution.py:341
  328.5 41.7 %collective-permute-start.37 = (bf16[256,1280]{1,0:T(8,128)(2,1)S(1)}, bf16[256,1280]{1,0:T(8,128)(2,1)S(1)}, u32[]{:S(2)}, u32[]{:S(2)}) collective-permute-start(bf16[256,1280]{1,0:T(8,128)(2,1)S(1)} %get-tuple-element.286), channel_id=1, source_target_pairs={{2,0},{3,1},{6,4},{7,5},{10,8},{11,9},{14,12},{15,13},{18,16},{19,... | collective-permute-start | bytes 1966088 | tf_op jit(solution)/shard_map/ppermute | solution.py:348
  329.8 54.6 %collective-permute-start.36 = (bf16[256,1280]{1,0:T(8,128)(2,1)S(1)}, bf16[256,1280]{1,0:T(8,128)(2,1)}, u32[]{:S(2)}, u32[]{:S(2)}) collective-permute-start(bf16[256,1280]{1,0:T(8,128)(2,1)S(1)} %get-tuple-element.287), channel_id=1, source_target_pairs={{0,2},{1,3},{4,6},{5,7},{8,10},{9,11},{12,14},{13,15},{16,18},{17,... | collective-permute-start | bytes 1966088 | tf_op jit(solution)/shard_map/ppermute | solution.py:347
  400.0 29.8 %collective-permute-start.41 = (bf16[576,3456]{1,0:T(8,128)(2,1)}, bf16[576,3456]{1,0:T(8,128)(2,1)}, u32[]{:S(2)}, u32[]{:S(2)}) collective-permute-start(bf16[576,3456]{1,0:T(8,128)(2,1)} %convolution_convert_fusion.2), channel_id=1, source_target_pairs={{0,4},{4,0},{8,12},{12,8},{16,20},{20,16},{24,28},{28,24},{1,5},{5... | collective-permute-start | bytes 11943944 | tf_op jit(solution)/shard_map/ppermute | solution.py:390
  413.6 23.0 %collective-permute-start.40 = (bf16[128,1152]{1,0:T(8,128)(2,1)}, bf16[128,1152]{1,0:T(8,128)(2,1)}, u32[]{:S(2)}, u32[]{:S(2)}) collective-permute-start(bf16[128,1152]{1,0:T(8,128)(2,1)} %slice.459), channel_id=1, source_target_pairs={{0,16},{4,20},{8,24},{12,28},{16,0},{20,4},{24,8},{28,12},{1,17},{... | collective-permute-start | bytes 884744 | tf_op jit(solution)/shard_map/ppermute | solution.py:390
  413.7 23.0 %collective-permute-start.39 = (bf16[160,1152]{1,0:T(8,128)(2,1)S(1)}, bf16[160,1152]{1,0:T(8,128)(2,1)S(1)}, u32[]{:S(2)}, u32[]{:S(2)}) collective-permute-start(bf16[160,1152]{1,0:T(8,128)(2,1)S(1)} %slice.458), channel_id=1, source_target_pairs={{0,8},{4,12},{8,0},{12,4},{16,24},{20,28},{24,16},{28,20},{1,9},{5... | collective-permute-start | bytes 1105928 | tf_op jit(solution)/shard_map/ppermute | solution.py:390
  418.8 148.0 %reduce-scatter.15.cloned.1.call-start = ((), (), s32[]{:S(2)}) async-start(), calls=%async_computation.10 | async-start | bytes 2949120
  439.5 37.9 %collective-permute-start.50 = (bf16[64,1152]{1,0:T(8,128)(2,1)}, bf16[64,1152]{1,0:T(8,128)(2,1)}, u32[]{:S(2)}, u32[]{:S(2)}) collective-permute-start(bf16[64,1152]{1,0:T(8,128)(2,1)} %add_convert_fusion.11), channel_id=1, source_target_pairs={{0,8},{4,12},{8,0},{12,4},{16,24},{20,28},{24,16},{28,20},{1,9},{5... | collective-permute-start | bytes 442376 | tf_op jit(solution)/shard_map/ppermute | solution.py:390
  439.7 29.8 %collective-permute-start.42 = (bf16[160,3456]{1,0:T(8,128)(2,1)}, bf16[160,3456]{1,0:T(8,128)(2,1)}, u32[]{:S(2)}, u32[]{:S(2)}) collective-permute-start(bf16[160,3456]{1,0:T(8,128)(2,1)} %slice.460), channel_id=1, source_target_pairs={{0,8},{4,12},{8,0},{12,4},{16,24},{20,28},{24,16},{28,20},{1,9},{5... | collective-permute-start | bytes 3317768 | tf_op jit(solution)/shard_map/ppermute | solution.py:390
  443.2 35.8 %collective-permute-start.49 = (bf16[80,1152]{1,0:T(8,128)(2,1)}, bf16[80,1152]{1,0:T(8,128)(2,1)}, u32[]{:S(2)}, u32[]{:S(2)}) collective-permute-start(bf16[80,1152]{1,0:T(8,128)(2,1)} %add_convert_fusion.9), channel_id=1, source_target_pairs={{0,16},{4,20},{8,24},{12,28},{16,0},{20,4},{24,8},{28,12},{1,17},{... | collective-permute-start | bytes 552968 | tf_op jit(solution)/shard_map/ppermute | solution.py:390
  445.2 23.5 %collective-permute-start.43 = (bf16[128,3456]{1,0:T(8,128)(2,1)}, bf16[128,3456]{1,0:T(8,128)(2,1)}, u32[]{:S(2)}, u32[]{:S(2)}) collective-permute-start(bf16[128,3456]{1,0:T(8,128)(2,1)} %slice.461), channel_id=1, source_target_pairs={{0,16},{4,20},{8,24},{12,28},{16,0},{20,4},{24,8},{28,12},{1,17},{... | collective-permute-start | bytes 2654216 | tf_op jit(solution)/shard_map/ppermute | solution.py:390
  474.7 22.7 %collective-permute-start.46 = (f32[20,1152]{1,0:T(8,128)S(1)}, f32[20,1152]{1,0:T(8,128)S(1)}, u32[]{:S(2)}, u32[]{:S(2)}) collective-permute-start(f32[20,1152]{1,0:T(8,128)S(1)} %stack_rows.1), channel_id=1, source_target_pairs={{0,3},{1,0},{2,1},{3,2},{4,7},{5,4},{6,5},{7,6},{8,11},{9,8},{10,9... | collective-permute-start | bytes 276488 | tf_op jit(solution)/shard_map/ppermute | solution.py:394
  475.9 21.5 %collective-permute-start.45 = (f32[20,1152]{1,0:T(8,128)S(1)}, f32[20,1152]{1,0:T(8,128)S(1)}, u32[]{:S(2)}, u32[]{:S(2)}) collective-permute-start(f32[20,1152]{1,0:T(8,128)S(1)} %stack_rows.1), channel_id=1, source_target_pairs={{0,2},{1,3},{2,0},{3,1},{4,6},{5,7},{6,4},{7,5},{8,10},{9,11},{10,... | collective-permute-start | bytes 276488 | tf_op jit(solution)/shard_map/ppermute | solution.py:394
  475.9 21.5 %collective-permute-start.44 = (f32[20,1152]{1,0:T(8,128)S(1)}, f32[20,1152]{1,0:T(8,128)S(1)}, u32[]{:S(2)}, u32[]{:S(2)}) collective-permute-start(f32[20,1152]{1,0:T(8,128)S(1)} %stack_rows.1), channel_id=1, source_target_pairs={{0,1},{1,2},{2,3},{3,0},{4,5},{5,6},{6,7},{7,4},{8,9},{9,10},{10,1... | collective-permute-start | bytes 276488 | tf_op jit(solution)/shard_map/ppermute | solution.py:394
  477.4 14.7 %collective-permute-start.47 = (bf16[80,3456]{1,0:T(8,128)(2,1)}, bf16[80,3456]{1,0:T(8,128)(2,1)S(1)}, u32[]{:S(2)}, u32[]{:S(2)}) collective-permute-start(bf16[80,3456]{1,0:T(8,128)(2,1)} %add_convert_fusion.5), channel_id=1, source_target_pairs={{0,16},{4,20},{8,24},{12,28},{16,0},{20,4},{24,8},{28,12},{1,17},{... | collective-permute-start | bytes 1658888 | tf_op jit(solution)/shard_map/ppermute | solution.py:390
  481.5 10.6 %collective-permute-start.48 = (bf16[64,3456]{1,0:T(8,128)(2,1)}, bf16[64,3456]{1,0:T(8,128)(2,1)}, u32[]{:S(2)}, u32[]{:S(2)}) collective-permute-start(bf16[64,3456]{1,0:T(8,128)(2,1)} %add_convert_fusion.7), channel_id=1, source_target_pairs={{0,8},{4,12},{8,0},{12,4},{16,24},{20,28},{24,16},{28,20},{1,9},{5... | collective-permute-start | bytes 1327112 | tf_op jit(solution)/shard_map/ppermute | solution.py:390
  498.9 34.5 %collective-permute-start.51 = (bf16[144,1152]{1,0:T(8,128)(2,1)S(1)}, bf16[144,1152]{1,0:T(8,128)(2,1)S(1)}, u32[]{:S(2)}, u32[]{:S(2)}) collective-permute-start(bf16[144,1152]{1,0:T(8,128)(2,1)S(1)} %pad_maximum_fusion.3), channel_id=1, source_target_pairs={{0,1},{1,2},{2,3},{3,0},{4,5},{5,6},{6,7},{7,4},{8,9},{9,10},{10,1... | collective-permute-start | bytes 995336 | tf_op jit(solution)/shard_map/ppermute | solution.py:394
  500.6 58.4 %collective-permute-start.52 = (bf16[144,1152]{1,0:T(8,128)(2,1)S(1)}, bf16[144,1152]{1,0:T(8,128)(2,1)S(1)}, u32[]{:S(2)}, u32[]{:S(2)}) collective-permute-start(bf16[144,1152]{1,0:T(8,128)(2,1)S(1)} %pad_maximum_fusion.4), channel_id=1, source_target_pairs={{0,2},{1,3},{2,0},{3,1},{4,6},{5,7},{6,4},{7,5},{8,10},{9,11},{10,... | collective-permute-start | bytes 995336 | tf_op jit(solution)/shard_map/ppermute | solution.py:394
  502.0 58.0 %collective-permute-start.53 = (bf16[144,1152]{1,0:T(8,128)(2,1)S(1)}, bf16[144,1152]{1,0:T(8,128)(2,1)}, u32[]{:S(2)}, u32[]{:S(2)}) collective-permute-start(bf16[144,1152]{1,0:T(8,128)(2,1)S(1)} %pad_maximum_fusion.5), channel_id=1, source_target_pairs={{0,3},{1,0},{2,1},{3,2},{4,7},{5,4},{6,5},{7,6},{8,11},{9,8},{10,9... | collective-permute-start | bytes 995336 | tf_op jit(solution)/shard_map/ppermute | solution.py:394
  515.4 47.3 %all-to-all-start = ((bf16[8,8,3672]{2,0,1:T(8,128)(2,1)}), bf16[8,8,3672]{2,0,1:T(8,128)(2,1)S(1)}, u32[]{:S(2)}, u32[]{:S(2)}) async-start(bf16[8,8,3672]{2,0,1:T(8,128)(2,1)} %pad_maximum_fusion.1), calls=%async_computation.2 | async-start | bytes 950272 | tf_op jit(solution)/shard_map/all_to_all | solution.py:818
  (85 other events, 569.7 us)
Sparse Core Ops, SparseCore 0:
  38.0 52.4 all-gather.2
  113.3 69.6 all-gather.4
  235.8 82.6 reduce-scatter.8
  321.9 82.2 reduce-scatter.10
  418.9 30.5 reduce-scatter.12
  485.5 76.5 reduce-scatter.14

commit v3 on v2

--- a/solution.py
+++ b/solution.py
@@ -734,6 +734,7 @@
         other_qkv = matmul(attn_other, grad_qkv).astype(jnp.bfloat16)
         got_qkv = swap(other_qkv, 1)
         grad_down_w = scatter_columns(after(grad_down, grad_up, other_qkv))
+        grad_up_w = scatter_columns(after(grad_up, other_qkv))
         grad_in_attn = contract_cols(after(grad_qkv, other_qkv), qkv_full)
         total_qkv = matmul(after(attn_mine, grad_in_attn), grad_qkv) + got_qkv.astype(jnp.float32)
         total_qkv = total_qkv.astype(jnp.bfloat16)
@@ -776,7 +777,6 @@
         qkv_over, qkv_side, *qkv_kept = second_parts(total_qkv, qkv_x, qkv_y)
         qkv_over, qkv_side = together((qkv_over, qkv_side))
         small = after(small, qkv_over)
-        grad_up_w = scatter_columns(after(grad_up, qkv_over))
         qkv_upper, qkv_lower = swap(qkv_over, 4), swap(qkv_side, 2)
         proj_upper, proj_lower = together((proj_upper, proj_lower), qkv_over)
         grad_proj = last_rows(*proj_kept, proj_upper, proj_lower)
@@ -790,7 +790,6 @@
             ]
         )
         both_moved = rotate_parts(both_parts)
-        last_sent = both_parts[:1]
         both = sum_wide(list(both_parts[:1]) + both_moved)
         grad_up_w = after(grad_up_w, both)
         grad_qkv_w, grad_proj_w = jnp.split(both, [qkv_weight.shape[1]], axis=1)
@@ -799,8 +798,7 @@
         grad_qkv_w, grad_proj_w, grad_up_w, grad_down_w = [
             scatter_columns(part) for part in (grad_qkv_w, grad_proj, grad_up, grad_down)
         ]
-        last_sent = []
-    moved = together(rotations(small), *last_sent)
+    moved = rotations(small)
     small = in_order(small, moved)
     all_units = small[:, :12].reshape(shards, 6, 2, width).transpose(0, 2, 1, 3)
     all_units = all_units.reshape(2 * shards, 6 * width)
@@ -822,7 +820,7 @@
         concat_axis=0,
         tiled=True,
     )[:, 0]
-    grad_cond_act = contract_cols(after(grad_mod, *last_sent), ada_weight)
+    grad_cond_act = contract_cols(grad_mod, ada_weight)
     grad_label = jax.vjp(jax.nn.silu, cond)[1](grad_cond_act)[0]
     cond_all = traded[:, own_width : own_width + width]
     grad_ada_w = contract_rows(cond_all, traded[:, :own_width])

time: 587 us -> 596 us (1.015)
  waiting for transfers between devices: 155 us -> 161 us
    unnamed x8, waiting for transfers between devices: 0.12 us -> 34.9 us
    ppermute x28, waiting for transfers between devices: 38.9 us -> 24.3 us  [swap(): return lax.ppermute(value, 'bin', flipped(mask))]
    ppermute x18, waiting for transfers between devices: 56.1 us -> 41.8 us  [rotate(): lax.ppermute(value, 'shard', [(at, (at + step) % count) for at in range(c...]
    unnamed x235 -> x231, local copies, waits for them, and re-layouts: 34.1 us -> 36.2 us
  transfers between devices with their start and end apart: 61 -> 61, of which waited for: 19 -> 18; matrix products, arithmetic and copies ran while one was open for 38% -> 37% of each run, Pallas kernels for 8% -> 8%
where the time goes in v3:
time: 596 us; the launch traced here: 585 us
  waiting for transfers between devices  161 us (27%)
  matrix products  134 us (22%)
  starting transfers between devices  93.1 us (16%)
  local copies, waits for them, and re-layouts  71 us (12%)
  other arithmetic  59.2 us (10%)
  Pallas kernels  44.8 us (8%)
  between operations  22.3 us (4%)
    dot_general x10, matrix products, matmul(): return jnp.dot(left, right, preferred_element_type=jnp.float32)  62.6 us
    dot_general x5, matrix products, contract_cols(): lax.dot_general(left, right, (((1,), (1,)), ((), ())), preferred_element_...  48.1 us
    ppermute x18, waiting for transfers between devices, rotate(): lax.ppermute(value, 'shard', [(at, (at + step) % count) for at in range(c...  41.8 us
    ppermute x28, starting transfers between devices, swap(): return lax.ppermute(value, 'bin', flipped(mask))  39.9 us
    unnamed x231, local copies, waits for them, and re-layouts  36.2 us
    unnamed x8, waiting for transfers between devices  34.9 us
    ppermute x2, waiting for transfers between devices, send_halo(): right = lax.ppermute(own, 'shard', chain(shards, -1))  33.6 us
    ppermute x28, waiting for transfers between devices, swap(): return lax.ppermute(value, 'bin', flipped(mask))  24.3 us
  transfers between devices with their start and end apart: 61, of which 18 were waited for; matrix products, arithmetic and copies ran while one was open for 37% of the time, Pallas kernels for 8%

profile of v3, /device:TPU:8, one launch (start us, length us, event | category | flops | bytes accessed | tf_op | source)
XLA Modules:
  0.0 584.6 jit_solution(13156846519389376359)
XLA Ops:
  7.2 2.7 collective-permute-start.1
  9.9 2.0 collective-permute-start.2
  22.0 7.8 %convolution_add_fusion = f32[8,6912]{1,0:T(8,128)S(1)} fusion(bf16[8,1152]{1,0:T(8,128)(2,1)S(1)} %multiply_convert_fusion.1, bf16[1152,6912]{1,0:T(8,128)(2,1)} %param.20, f32[6912]{0:T(1024)} %param.21), kind=kOutput, calls=%fused_computation.27 | convolution fusion | flops 127457280 | bytes 16192512 | tf_op jit(solution)/shard_map/dot_general | solution.py:370
  35.1 2.8 reshape.341
  38.8 2.9 collective-permute-start.8
  41.7 2.8 collective-permute-start.5
  45.2 2.9 collective-permute-start.3
  48.1 14.9 %collective-permute-done.8 = bf16[144,288]{1,0:T(8,128)(2,1)S(1)} collective-permute-done((bf16[144,288]{1,0:T(8,128)(2,1)S(1)}, bf16[144,288]{1,0:T(8,128)(2,1)S(1)}, u32[]{:S(2)}, u32[]{:S(2)}) %collective-permute-start.8) | collective-permute-done | bytes 82976 | tf_op jit(solution)/shard_map/ppermute | solution.py:394
  64.9 4.5 collective-permute-start.6
  70.2 33.6 %collective-permute-done.7 = bf16[512,1152]{1,0:T(8,128)(2,1)} collective-permute-done((bf16[512,1152]{1,0:T(8,128)(2,1)S(1)}, bf16[512,1152]{1,0:T(8,128)(2,1)}, u32[]{:S(2)}, u32[]{:S(2)}) %collective-permute-start.7) | collective-permute-done | bytes 1179680 | tf_op jit(solution)/shard_map/ppermute | solution.py:342
  119.0 2.6 collective-permute-start.11
  121.7 3.2 collective-permute-start.12
  124.9 3.4 collective-permute-done.14.refs_2_
  128.3 3.6 collective-permute-done.13.refs_1_
  132.0 2.5 collective-permute-start.15
  134.6 8.4 %add_convert_fusion.2.own = bf16[512,3456]{1,0:T(8,128)(2,1)S(1)} fusion(bf16[512,1152]{1,0:T(8,128)(2,1)S(1)} %copy-done.29, bf16[1152,3456]{1,0:T(8,128)(2,1)} %all-gather.3.cloned.1.call-done, f32[3456]{0:T(1024)S(1)} %pad_maximum_fusion.7), kind=kOutput, calls=%fused_computation.29 | convolution fusion | flops 4080402432 | bytes 12695040 | tf_op jit(solution)/shard_map/dot_general | solution.py:370
  145.2 2.8 convert_reduce_fusion.1
  149.6 8.9 %add_convert_fusion.halo.qh = bf16[768,3456]{1,0:T(8,128)(2,1)} fusion(bf16[768,1152]{1,0:T(8,128)(2,1)S(1)} %fusion.20, bf16[1152,3456]{1,0:T(8,128)(2,1)S(1)} %copy-done.78, f32[3456]{0:T(1024)S(1)} %pad_maximum_fusion.7), kind=kOutput, calls=%fused_computation.8 | convolution fusion | flops 6120603648 | bytes 15054336 | tf_op jit(solution)/shard_map/dot_general | solution.py:370
  159.2 8.6 %attend.1 = (bf16[512,1152]{1,0:T(8,128)(2,1)S(1)}, f32[512,128]{1,0:T(8,128)S(1)}) custom-call(s32[3]{0:T(128)S(1)} %pad_add_fusion.meta, bf16[512,3456]{1,0:T(8,128)(2,1)S(1)} %add_convert_fusion.2.own, bf16[768,3456]{1,0:T(8,128)(2,1)} %add_convert_fusion.halo.qh), custom_call_target="tpu_custom_call" | custom-call | flops 8589934592 | bytes 10485760 | tf_op jit(solution)/shard_map/attend/pallas_call | solution.py:105
  173.5 11.4 %collective-permute-start.26 = (bf16[576,1152]{1,0:T(8,128)(2,1)S(1)}, bf16[576,1152]{1,0:T(8,128)(2,1)}, u32[]{:S(2)}, u32[]{:S(2)}) collective-permute-start(bf16[576,1152]{1,0:T(8,128)(2,1)S(1)} %copy.102.refs_0_), channel_id=1, source_target_pairs={{0,16},{4,20},{8,24},{12,28},{16,0},{20,4},{24,8},{28,12},{1,17},{... | collective-permute-start | bytes 3981320 | tf_op jit(solution)/shard_map/ppermute | solution.py:390
  189.2 2.6 fusion.34
  194.8 2.4 place_rows.2
  197.3 3.3 fusion.76
  203.0 4.5 collective-permute-done.26.refs_2_
  207.5 2.0 slice.350
  211.5 13.1 %fusion.14 = (bf16[512,4608]{1,0:T(8,128)(2,1)S(1)}, f32[512,4608]{1,0:T(8,128)}) fusion(f32[4608]{0:T(1024)S(1)} %copy-done.80, bf16[512,1152]{1,0:T(8,128)(2,1)} %fusion.37, bf16[1152,4608]{1,0:T(8,128)(2,1)} %all-gather.5.cloned.1.call-done), kind=kOutput, calls=%fused_computation.23 | convolution fusion | flops 5459410944 | bytes 25970688 | tf_op jit(solution)/shard_map/dot_general | solution.py:370
  224.6 2.1 copy-done.27
  226.7 9.0 %convolution_convert_fusion.1 = bf16[4608,1152]{1,0:T(8,128)(2,1)} fusion(bf16[512,4608]{1,0:T(8,128)(2,1)S(1)} %get-tuple-element.163, bf16[512,1152]{1,0:T(8,128)(2,1)S(1)} %copy-done.28), kind=kOutput, calls=%fused_computation.4 | convolution fusion | flops 5441126400 | bytes 16515072 | tf_op jit(solution)/shard_map/dot_general | solution.py:374
  238.9 9.3 %fusion.6 = bf16[512,4608]{1,0:T(8,128)(2,1)} fusion(f32[512,4608]{1,0:T(8,128)} %get-tuple-element.139), kind=kLoop, calls=%fused_computation.15 | loop fusion | flops 42467328 | bytes 14155776 | tf_op jit(solution)/shard_map/convert_element_type | solution.py:670
  248.2 7.4 %collective-permute-done.28.refs_4_ = bf16[288,1152]{1,0:T(8,128)(2,1)} collective-permute-done((bf16[288,1152]{1,0:T(8,128)(2,1)}, bf16[288,1152]{1,0:T(8,128)(2,1)}, u32[]{:S(2)}, u32[]{:S(2)}) %collective-permute-start.28) | collective-permute-done | bytes 663584 | tf_op jit(solution)/shard_map/ppermute | solution.py:390
  256.2 2.5 collective-permute-done.32.refs_8_
  258.9 4.2 place_rows.3
  263.2 13.5 %convert_reduce_fusion = (f32[4608]{0:T(1024)}, bf16[512,4608]{1,0:T(8,128)(2,1)}) fusion(bf16[512,4608]{1,0:T(8,128)(2,1)} %fusion.6, bf16[512,1152]{1,0:T(8,128)(2,1)} %fusion.34, bf16[4608,1152]{1,0:T(8,128)(2,1)S(1)} %place_rows.3), kind=kOutput, calls=%fused_computation.24 | convolution fusion | flops 5447609856 | bytes 21252096 | tf_op jit(solution)/shard_map/dot_general | solution.py:380
  276.7 10.6 %convolution_convert_fusion = bf16[1152,4608]{1,0:T(8,128)(2,1)} fusion(bf16[512,1152]{1,0:T(8,128)(2,1)S(1)} %copy-done.36, bf16[512,4608]{1,0:T(8,128)(2,1)} %get-tuple-element.142), kind=kOutput, calls=%fused_computation.3 | convolution fusion | flops 5441126400 | bytes 16515072 | tf_op jit(solution)/shard_map/dot_general | solution.py:374
  302.0 11.6 %fusion.44 = (f32[512]{0:T(512)S(1)}, f32[512]{0:T(512)S(1)}, f32[512,1152]{1,0:T(8,128)S(1)}) fusion(f32[2,1152]{1,0:T(2,128)S(1)} %copy-done.57, f32[512]{0:T(512)S(1)} %copy-done.65, f32[512,1152]{1,0:T(8,128)S(1)} %copy-done.16, f32[512]{0:T(512)S(1)} %broadcast_multiply_fusion.5, bf16[512,4608]{1,0:T(8,128)(2,1)} %get-tuple-element.142, ...), kind=kOutput, calls=%fused_computation.100 | convolution fusion | flops 5439355904 | bytes 20071424 | tf_op jit(solution)/shard_map/dot_general | solution.py:380
  313.7 2.9 convert_reduce_fusion.4
  320.3 2.1 fusion.59
  322.5 2.5 collective-permute-start.35
  325.0 3.4 collective-permute-start.34
  329.8 6.3 %collective-permute-start.36 = (bf16[256,1280]{1,0:T(8,128)(2,1)S(1)}, bf16[256,1280]{1,0:T(8,128)(2,1)}, u32[]{:S(2)}, u32[]{:S(2)}) collective-permute-start(bf16[256,1280]{1,0:T(8,128)(2,1)S(1)} %get-tuple-element.279), channel_id=1, source_target_pairs={{0,2},{1,3},{4,6},{5,7},{8,10},{9,11},{12,14},{13,15},{16,18},{17,... | collective-permute-start | bytes 1966088 | tf_op jit(solution)/shard_map/ppermute | solution.py:347
  338.2 20.2 %own_back.1 = (bf16[512,1152]{1,0:T(8,128)(2,1)}, f32[512,1152]{1,0:T(8,128)}, f32[512,1152]{1,0:T(8,128)}) custom-call(s32[3]{0:T(128)} %copy-done.11, bf16[512,3456]{1,0:T(8,128)(2,1)} %copy-done.12, bf16[768,3456]{1,0:T(8,128)(2,1)} %add_convert_fusion.halo.qh, bf16[512,1152]{1,0:T(8,128)(2,1)} %copy-done.21, f32[512,128]{1,0:T(8,128)} %get-tuple-element.341.stats), custom_call_target="tpu_custom_call" | custom-call | flops 17179869184 | bytes 20971520 | tf_op jit(solution)/shard_map/own_back/pallas_call | solution.py:194
  358.4 11.7 %collective-permute-done.37.far_right = bf16[256,1280]{1,0:T(8,128)(2,1)S(1)} collective-permute-done((bf16[256,1280]{1,0:T(8,128)(2,1)S(1)}, bf16[256,1280]{1,0:T(8,128)(2,1)S(1)}, u32[]{:S(2)}, u32[]{:S(2)}) %collective-permute-start.37) | collective-permute-done | bytes 655392 | tf_op jit(solution)/shard_map/ppermute | solution.py:348
  370.1 14.2 %collective-permute-done.36.far_left = bf16[256,1280]{1,0:T(8,128)(2,1)} collective-permute-done((bf16[256,1280]{1,0:T(8,128)(2,1)S(1)}, bf16[256,1280]{1,0:T(8,128)(2,1)}, u32[]{:S(2)}, u32[]{:S(2)}) %collective-permute-start.36) | collective-permute-done | bytes 655392 | tf_op jit(solution)/shard_map/ppermute | solution.py:347
  384.3 9.2 %halo_back.1 = bf16[512,3456]{1,0:T(8,128)(2,1)} custom-call(s32[3]{0:T(128)} %copy-done.11, bf16[512,3456]{1,0:T(8,128)(2,1)} %copy-done.12, bf16[768,3456]{1,0:T(8,128)(2,1)} %add_convert_fusion.halo.qh, bf16[256,1280]{1,0:T(8,128)(2,1)} %collective-permute-done.36.far_left, bf16[512,1280]{1,0:T(8,128)(2,1)} %collective-permute-done.34.left, ...), custom_call_target="tpu_custom_call" | custom-call | flops 8589934592 | bytes 20971520 | tf_op jit(solution)/shard_map/halo_back/pallas_call | solution.py:285
  393.6 6.5 %convolution_convert_fusion.2 = bf16[576,3456]{1,0:T(8,128)(2,1)} fusion(bf16[576,512]{1,0:T(8,128)(2,1)} %copy-done.72, bf16[512,3456]{1,0:T(8,128)(2,1)} %halo_back.1), kind=kOutput, calls=%fused_computation.30 | convolution fusion | flops 2040422400 | bytes 8110080 | tf_op jit(solution)/shard_map/dot_general | solution.py:370
  400.0 9.1 %collective-permute-start.41 = (bf16[576,3456]{1,0:T(8,128)(2,1)}, bf16[576,3456]{1,0:T(8,128)(2,1)}, u32[]{:S(2)}, u32[]{:S(2)}) collective-permute-start(bf16[576,3456]{1,0:T(8,128)(2,1)} %convolution_convert_fusion.2), channel_id=1, source_target_pairs={{0,4},{4,0},{8,12},{12,8},{16,20},{20,16},{24,28},{28,24},{1,5},{5... | collective-permute-start | bytes 11943944 | tf_op jit(solution)/shard_map/ppermute | solution.py:390
  411.2 2.3 bitcast_reduce_fusion.1
  413.6 2.1 collective-permute-start.40
  416.3 2.6 copy.119
  419.2 10.8 %fusion.84 = f32[512,1152]{1,0:T(8,128)} fusion(bf16[512,3456]{1,0:T(8,128)(2,1)} %halo_back.1, bf16[1152,3456]{1,0:T(8,128)(2,1)} %all-gather.3.cloned.1.call-done), kind=kOutput, calls=%fused_computation.327 | convolution fusion | flops 4076863488 | bytes 13860864 | tf_op jit(solution)/shard_map/dot_general | solution.py:380
  430.1 4.7 add_convert_fusion.1
  436.9 2.9 add_convert_fusion.11
  445.5 8.0 %fusion.35 = (f32[512,1152]{1,0:T(8,128)}, f32[512,1152]{1,0:T(8,128)}) fusion(f32[512,1152]{1,0:T(8,128)S(1)} %copy-done.16, f32[2,1152]{1,0:T(2,128)S(1)} %get-tuple-element.318, f32[1152]{0:T(1024)S(1)} %copy-done.73, bf16[512,4608]{1,0:T(8,128)(2,1)S(1)} %bitcast.384, bf16[4608,1152]{1,0:T(8,128)(2,1)S(1)} %bitcast.377), kind=kOutput, calls=%fused_computation.73 | convolution fusion | flops 5437587456 | bytes 22427136 | tf_op jit(solution)/shard_map/dot_general | solution.py:370
  453.5 3.9 copy.121
  457.4 2.1 bitcast_reduce_fusion.refs_5_
  460.8 2.8 fusion.43
  465.5 2.3 fusion.78
  470.9 2.1 add_convert_fusion.7
  474.0 3.5 collective-permute-start.45
  477.8 34.8 %reduce-scatter.15.cloned.1.call-done = bf16[1152,144]{1,0:T(8,128)(2,1)} async-done(((bf16[4608,144]{1,0:T(8,128)(2,1)}), bf16[1152,144]{1,0:T(8,128)(2,1)}) %reduce-scatter.15.cloned.1.call-update) | async-done | bytes 331792
  523.1 3.5 all-to-all-start
  526.6 10.4 %fusion.63 = f32[8,1152]{1,0:T(8,128)} fusion(f32[8,1152]{1,0:T(8,128)S(1)} %copy-done.53, f32[8,576]{1,0:T(8,128)S(1)} %copy-done.50, f32[8,576]{1,0:T(8,128)S(1)} %copy-done.48, bf16[8,6912]{1,0:T(8,128)(2,1)S(1)} %select_reduce_fusion, bf16[1152,6912]{1,0:T(8,128)(2,1)} %param.20), kind=kOutput, calls=%fused_computation.260 | convolution fusion | flops 127503360 | bytes 16146432 | tf_op jit(solution)/shard_map/dot_general | solution.py:380
  548.1 6.6 %collective-permute-done.51 = bf16[144,1152]{1,0:T(8,128)(2,1)S(1)} collective-permute-done((bf16[144,1152]{1,0:T(8,128)(2,1)S(1)}, bf16[144,1152]{1,0:T(8,128)(2,1)S(1)}, u32[]{:S(2)}, u32[]{:S(2)}) %collective-permute-start.51) | collective-permute-done | bytes 331808 | tf_op jit(solution)/shard_map/ppermute | solution.py:394
  554.6 18.8 %collective-permute-done.52 = bf16[144,1152]{1,0:T(8,128)(2,1)S(1)} collective-permute-done((bf16[144,1152]{1,0:T(8,128)(2,1)S(1)}, bf16[144,1152]{1,0:T(8,128)(2,1)S(1)}, u32[]{:S(2)}, u32[]{:S(2)}) %collective-permute-start.52) | collective-permute-done | bytes 331808 | tf_op jit(solution)/shard_map/ppermute | solution.py:394
  (462 shorter events, 119.4 us)
Async XLA Ops:
  7.2 127.4 %all-gather.3.cloned.1.call-start = ((), (), s32[]{:S(2)}) async-start(), calls=%async_computation.5 | async-start | bytes 8957952 | tf_op jit(solution)/shard_map/all_gather | solution.py:611
  7.2 26.1 %collective-permute-start.1 = (bf16[144,864]{1,0:T(8,128)(2,1)}, bf16[144,864]{1,0:T(8,128)(2,1)S(1)}, u32[]{:S(2)}, u32[]{:S(2)}) collective-permute-start(bf16[144,864]{1,0:T(8,128)(2,1)} %param.22), channel_id=1, source_target_pairs={{0,2},{1,3},{2,0},{3,1},{4,6},{5,7},{6,4},{7,5},{8,10},{9,11},{10,... | collective-permute-start | bytes 746504 | tf_op jit(solution)/shard_map/ppermute | solution.py:394
  9.9 23.4 %collective-permute-start = (bf16[144,864]{1,0:T(8,128)(2,1)}, bf16[144,864]{1,0:T(8,128)(2,1)S(1)}, u32[]{:S(2)}, u32[]{:S(2)}) collective-permute-start(bf16[144,864]{1,0:T(8,128)(2,1)} %param.22), channel_id=1, source_target_pairs={{0,1},{1,2},{2,3},{3,0},{4,5},{5,6},{6,7},{7,4},{8,9},{9,10},{10,1... | collective-permute-start | bytes 746504 | tf_op jit(solution)/shard_map/ppermute | solution.py:394
  9.9 23.4 %collective-permute-start.2 = (bf16[144,864]{1,0:T(8,128)(2,1)}, bf16[144,864]{1,0:T(8,128)(2,1)S(1)}, u32[]{:S(2)}, u32[]{:S(2)}) collective-permute-start(bf16[144,864]{1,0:T(8,128)(2,1)} %param.22), channel_id=1, source_target_pairs={{0,3},{1,0},{2,1},{3,2},{4,7},{5,4},{6,5},{7,6},{8,11},{9,8},{10,9... | collective-permute-start | bytes 746504 | tf_op jit(solution)/shard_map/ppermute | solution.py:394
  31.1 166.2 %copy-start.54 = (f32[2,1152]{1,0:T(2,128)}, f32[2,1152]{1,0:T(2,128)S(1)}, u32[]{:S(2)}) copy-start(f32[2,1152]{1,0:T(2,128)S(1)} %get-tuple-element.322) | copy-start | bytes 27652
  31.1 170.0 %copy-start.56 = (f32[2,1152]{1,0:T(2,128)}, f32[2,1152]{1,0:T(2,128)S(1)}, u32[]{:S(2)}) copy-start(f32[2,1152]{1,0:T(2,128)S(1)} %get-tuple-element.319) | copy-start | bytes 27652
  37.9 173.6 %all-gather.5.cloned.1.call-start = ((), (), s32[]{:S(2)}) async-start(), calls=%async_computation.6 | async-start | bytes 11943936 | tf_op jit(solution)/shard_map/all_gather | solution.py:624
  37.9 7.3 %collective-permute-start.9 = (bf16[144,288]{1,0:T(8,128)(2,1)S(1)}, bf16[144,288]{1,0:T(8,128)(2,1)S(1)}, u32[]{:S(2)}, u32[]{:S(2)}) collective-permute-start(bf16[144,288]{1,0:T(8,128)(2,1)S(1)} %copy-done.38), channel_id=1, source_target_pairs={{0,2},{1,3},{2,0},{3,1},{4,6},{5,7},{6,4},{7,5},{8,10},{9,11},{10,... | collective-permute-start | bytes 248840 | tf_op jit(solution)/shard_map/ppermute | solution.py:394
  38.8 24.2 %collective-permute-start.8 = (bf16[144,288]{1,0:T(8,128)(2,1)S(1)}, bf16[144,288]{1,0:T(8,128)(2,1)S(1)}, u32[]{:S(2)}, u32[]{:S(2)}) collective-permute-start(bf16[144,288]{1,0:T(8,128)(2,1)S(1)} %copy-done.38), channel_id=1, source_target_pairs={{0,1},{1,2},{2,3},{3,0},{4,5},{5,6},{6,7},{7,4},{8,9},{9,10},{10,1... | collective-permute-start | bytes 248840 | tf_op jit(solution)/shard_map/ppermute | solution.py:394
  41.7 23.2 %collective-permute-start.10 = (bf16[144,288]{1,0:T(8,128)(2,1)S(1)}, bf16[144,288]{1,0:T(8,128)(2,1)S(1)}, u32[]{:S(2)}, u32[]{:S(2)}) collective-permute-start(bf16[144,288]{1,0:T(8,128)(2,1)S(1)} %copy-done.38), channel_id=1, source_target_pairs={{0,3},{1,0},{2,1},{3,2},{4,7},{5,4},{6,5},{7,6},{8,11},{9,8},{10,9... | collective-permute-start | bytes 248840 | tf_op jit(solution)/shard_map/ppermute | solution.py:394
  41.7 65.9 %collective-permute-start.5 = (bf16[144,1152]{1,0:T(8,128)(2,1)S(1)}, bf16[144,1152]{1,0:T(8,128)(2,1)S(1)}, u32[]{:S(2)}, u32[]{:S(2)}) collective-permute-start(bf16[144,1152]{1,0:T(8,128)(2,1)S(1)} %copy-done.35), channel_id=1, source_target_pairs={{0,3},{1,0},{2,1},{3,2},{4,7},{5,4},{6,5},{7,6},{8,11},{9,8},{10,9... | collective-permute-start | bytes 995336 | tf_op jit(solution)/shard_map/ppermute | solution.py:394
  44.5 63.1 %collective-permute-start.4 = (bf16[144,1152]{1,0:T(8,128)(2,1)S(1)}, bf16[144,1152]{1,0:T(8,128)(2,1)}, u32[]{:S(2)}, u32[]{:S(2)}) collective-permute-start(bf16[144,1152]{1,0:T(8,128)(2,1)S(1)} %copy-done.35), channel_id=1, source_target_pairs={{0,2},{1,3},{2,0},{3,1},{4,6},{5,7},{6,4},{7,5},{8,10},{9,11},{10,... | collective-permute-start | bytes 995336 | tf_op jit(solution)/shard_map/ppermute | solution.py:394
  45.2 62.4 %collective-permute-start.3 = (bf16[144,1152]{1,0:T(8,128)(2,1)S(1)}, bf16[144,1152]{1,0:T(8,128)(2,1)}, u32[]{:S(2)}, u32[]{:S(2)}) collective-permute-start(bf16[144,1152]{1,0:T(8,128)(2,1)S(1)} %copy-done.35), channel_id=1, source_target_pairs={{0,1},{1,2},{2,3},{3,0},{4,5},{5,6},{6,7},{7,4},{8,9},{9,10},{10,1... | collective-permute-start | bytes 995336 | tf_op jit(solution)/shard_map/ppermute | solution.py:394
  63.0 40.8 %collective-permute-start.7 = (bf16[512,1152]{1,0:T(8,128)(2,1)S(1)}, bf16[512,1152]{1,0:T(8,128)(2,1)}, u32[]{:S(2)}, u32[]{:S(2)}) collective-permute-start(bf16[512,1152]{1,0:T(8,128)(2,1)S(1)} %copy-done.17), channel_id=1, source_target_pairs={{1,0},{2,1},{3,2},{5,4},{6,5},{7,6},{9,8},{10,9},{11,10},{13,12},{... | collective-permute-start | bytes 3538952 | tf_op jit(solution)/shard_map/ppermute | solution.py:342
  64.9 38.9 %collective-permute-start.6 = (bf16[512,1152]{1,0:T(8,128)(2,1)S(1)}, bf16[512,1152]{1,0:T(8,128)(2,1)}, u32[]{:S(2)}, u32[]{:S(2)}) collective-permute-start(bf16[512,1152]{1,0:T(8,128)(2,1)S(1)} %copy-done.17), channel_id=1, source_target_pairs={{0,1},{1,2},{2,3},{4,5},{5,6},{6,7},{8,9},{9,10},{10,11},{12,13},{... | collective-permute-start | bytes 3538952 | tf_op jit(solution)/shard_map/ppermute | solution.py:341
  113.2 303.1 %reduce-scatter.9.cloned.1.call-start = ((), (), s32[]{:S(2)}) async-start(), calls=%async_computation.7 | async-start | bytes 11943936 | tf_op jit(solution)/shard_map/reduce_scatter | solution.py:680
  115.9 12.3 %collective-permute-start.14 = (bf16[144,1152]{1,0:T(8,128)(2,1)S(1)}, bf16[144,1152]{1,0:T(8,128)(2,1)S(1)}, u32[]{:S(2)}, u32[]{:S(2)}) collective-permute-start(bf16[144,1152]{1,0:T(8,128)(2,1)S(1)} %reshape.342.refs_0_), channel_id=1, source_target_pairs={{0,16},{4,20},{8,24},{12,28},{16,0},{20,4},{24,8},{28,12},{1,17},{... | collective-permute-start | bytes 995336 | tf_op jit(solution)/shard_map/ppermute | solution.py:390
  117.5 14.4 %collective-permute-start.13 = (bf16[144,1152]{1,0:T(8,128)(2,1)S(1)}, bf16[144,1152]{1,0:T(8,128)(2,1)S(1)}, u32[]{:S(2)}, u32[]{:S(2)}) collective-permute-start(bf16[144,1152]{1,0:T(8,128)(2,1)S(1)} %reshape.342.refs_0_), channel_id=1, source_target_pairs={{0,8},{4,12},{8,0},{12,4},{16,24},{20,28},{24,16},{28,20},{1,9},{5... | collective-permute-start | bytes 995336 | tf_op jit(solution)/shard_map/ppermute | solution.py:390
  119.0 24.0 %collective-permute-start.11 = (bf16[256,1152]{1,0:T(8,128)(2,1)}, bf16[256,1152]{1,0:T(8,128)(2,1)S(1)}, u32[]{:S(2)}, u32[]{:S(2)}) collective-permute-start(bf16[256,1152]{1,0:T(8,128)(2,1)} %slice.342), channel_id=1, source_target_pairs={{0,1},{1,2},{2,3},{4,5},{5,6},{6,7},{8,9},{9,10},{10,11},{12,13},{... | collective-permute-start | bytes 1769480 | tf_op jit(solution)/shard_map/ppermute | solution.py:347
  121.7 21.3 %collective-permute-start.12 = (bf16[256,1152]{1,0:T(8,128)(2,1)}, bf16[256,1152]{1,0:T(8,128)(2,1)}, u32[]{:S(2)}, u32[]{:S(2)}) collective-permute-start(bf16[256,1152]{1,0:T(8,128)(2,1)} %slice.343), channel_id=1, source_target_pairs={{1,0},{2,1},{3,2},{5,4},{6,5},{7,6},{9,8},{10,9},{11,10},{13,12},{... | collective-permute-start | bytes 1769480 | tf_op jit(solution)/shard_map/ppermute | solution.py:348
  131.9 26.7 %collective-permute-start.16 = (bf16[64,1152]{1,0:T(8,128)(2,1)S(1)}, bf16[64,1152]{1,0:T(8,128)(2,1)S(1)}, u32[]{:S(2)}, u32[]{:S(2)}) collective-permute-start(bf16[64,1152]{1,0:T(8,128)(2,1)S(1)} %slice.349), channel_id=1, source_target_pairs={{0,16},{4,20},{8,24},{12,28},{16,0},{20,4},{24,8},{28,12},{1,17},{... | collective-permute-start | bytes 442376 | tf_op jit(solution)/shard_map/ppermute | solution.py:390
  132.0 27.2 %collective-permute-start.15 = (bf16[80,1152]{1,0:T(8,128)(2,1)S(1)}, bf16[80,1152]{1,0:T(8,128)(2,1)}, u32[]{:S(2)}, u32[]{:S(2)}) collective-permute-start(bf16[80,1152]{1,0:T(8,128)(2,1)S(1)} %slice.348), channel_id=1, source_target_pairs={{0,8},{4,12},{8,0},{12,4},{16,24},{20,28},{24,16},{28,20},{1,9},{5... | collective-permute-start | bytes 552968 | tf_op jit(solution)/shard_map/ppermute | solution.py:390
  143.0 24.8 %collective-permute-start.24 = (bf16[576,288]{0,1:T(8,128)(2,1)}, bf16[576,288]{0,1:T(8,128)(2,1)S(1)}, u32[]{:S(2)}, u32[]{:S(2)}) collective-permute-start(bf16[576,288]{0,1:T(8,128)(2,1)} %param.28), channel_id=1, source_target_pairs={{0,3},{1,0},{2,1},{3,2},{4,7},{5,4},{6,5},{7,6},{8,11},{9,8},{10,9... | collective-permute-start | bytes 995336 | tf_op jit(solution)/shard_map/ppermute | solution.py:394
  143.1 24.8 %collective-permute-start.23 = (bf16[576,288]{0,1:T(8,128)(2,1)}, bf16[576,288]{0,1:T(8,128)(2,1)S(1)}, u32[]{:S(2)}, u32[]{:S(2)}) collective-permute-start(bf16[576,288]{0,1:T(8,128)(2,1)} %param.28), channel_id=1, source_target_pairs={{0,2},{1,3},{2,0},{3,1},{4,6},{5,7},{6,4},{7,5},{8,10},{9,11},{10,... | collective-permute-start | bytes 995336 | tf_op jit(solution)/shard_map/ppermute | solution.py:394
  144.5 23.5 %collective-permute-start.22 = (bf16[576,288]{0,1:T(8,128)(2,1)}, bf16[576,288]{0,1:T(8,128)(2,1)S(1)}, u32[]{:S(2)}, u32[]{:S(2)}) collective-permute-start(bf16[576,288]{0,1:T(8,128)(2,1)} %param.28), channel_id=1, source_target_pairs={{0,1},{1,2},{2,3},{3,0},{4,5},{5,6},{6,7},{7,4},{8,9},{9,10},{10,1... | collective-permute-start | bytes 995336 | tf_op jit(solution)/shard_map/ppermute | solution.py:394
  173.5 34.0 %collective-permute-start.26 = (bf16[576,1152]{1,0:T(8,128)(2,1)S(1)}, bf16[576,1152]{1,0:T(8,128)(2,1)}, u32[]{:S(2)}, u32[]{:S(2)}) collective-permute-start(bf16[576,1152]{1,0:T(8,128)(2,1)S(1)} %copy.102.refs_0_), channel_id=1, source_target_pairs={{0,16},{4,20},{8,24},{12,28},{16,0},{20,4},{24,8},{28,12},{1,17},{... | collective-permute-start | bytes 3981320 | tf_op jit(solution)/shard_map/ppermute | solution.py:390
  184.9 22.6 %collective-permute-start.25 = (bf16[576,1152]{1,0:T(8,128)(2,1)S(1)}, bf16[576,1152]{1,0:T(8,128)(2,1)}, u32[]{:S(2)}, u32[]{:S(2)}) collective-permute-start(bf16[576,1152]{1,0:T(8,128)(2,1)S(1)} %copy.102.refs_0_), channel_id=1, source_target_pairs={{0,8},{4,12},{8,0},{12,4},{16,24},{20,28},{24,16},{28,20},{1,9},{5... | collective-permute-start | bytes 3981320 | tf_op jit(solution)/shard_map/ppermute | solution.py:390
  184.9 1.6 collective-permute-start.17
  184.9 2.5 collective-permute-start.19
  185.4 6.5 %collective-permute-start.18 = (bf16[144,1152]{1,0:T(8,128)(2,1)S(1)}, bf16[144,1152]{1,0:T(8,128)(2,1)}, u32[]{:S(2)}, u32[]{:S(2)}) collective-permute-start(bf16[144,1152]{1,0:T(8,128)(2,1)S(1)} %collective-permute-done.13.refs_1_), channel_id=1, source_target_pairs={{0,4},{4,0},{8,12},{12,8},{16,20},{20,16},{24,28},{28,24},{1,5},{5... | collective-permute-start | bytes 995336 | tf_op jit(solution)/shard_map/ppermute | solution.py:390
  187.3 4.6 collective-permute-start.20
  188.2 3.8 collective-permute-start.21
  235.7 180.6 %reduce-scatter.11.cloned.1.call-start = ((), (), s32[]{:S(2)}) async-start(), calls=%async_computation.8 | async-start | bytes 11943936 | tf_op jit(solution)/shard_map/reduce_scatter | solution.py:687
  236.2 20.0 %collective-permute-start.29 = (bf16[576,1152]{1,0:T(8,128)(2,1)S(1)}, bf16[576,1152]{1,0:T(8,128)(2,1)}, u32[]{:S(2)}, u32[]{:S(2)}) collective-permute-start(bf16[576,1152]{1,0:T(8,128)(2,1)S(1)} %copy.102.refs_0_), channel_id=1, source_target_pairs={{0,4},{4,0},{8,12},{12,8},{16,20},{20,16},{24,28},{28,24},{1,5},{5... | collective-permute-start | bytes 3981320 | tf_op jit(solution)/shard_map/ppermute | solution.py:390
  236.2 19.3 %collective-permute-start.27 = (bf16[288,1152]{1,0:T(8,128)(2,1)}, bf16[288,1152]{1,0:T(8,128)(2,1)S(1)}, u32[]{:S(2)}, u32[]{:S(2)}) collective-permute-start(bf16[288,1152]{1,0:T(8,128)(2,1)} %slice.350), channel_id=1, source_target_pairs={{0,8},{4,12},{8,0},{12,4},{16,24},{20,28},{24,16},{28,20},{1,9},{5... | collective-permute-start | bytes 1990664 | tf_op jit(solution)/shard_map/ppermute | solution.py:390
  237.7 18.4 %collective-permute-start.31 = (bf16[576,1152]{1,0:T(8,128)(2,1)}, bf16[576,1152]{1,0:T(8,128)(2,1)}, u32[]{:S(2)}, u32[]{:S(2)}) collective-permute-start(bf16[576,1152]{1,0:T(8,128)(2,1)} %collective-permute-done.26.refs_2_), channel_id=1, source_target_pairs={{0,4},{4,0},{8,12},{12,8},{16,20},{20,16},{24,28},{28,24},{1,5},{5... | collective-permute-start | bytes 3981320 | tf_op jit(solution)/shard_map/ppermute | solution.py:390
  237.9 18.3 %collective-permute-start.30 = (bf16[576,1152]{1,0:T(8,128)(2,1)}, bf16[576,1152]{1,0:T(8,128)(2,1)}, u32[]{:S(2)}, u32[]{:S(2)}) collective-permute-start(bf16[576,1152]{1,0:T(8,128)(2,1)} %collective-permute-done.25.refs_1_), channel_id=1, source_target_pairs={{0,4},{4,0},{8,12},{12,8},{16,20},{20,16},{24,28},{28,24},{1,5},{5... | collective-permute-start | bytes 3981320 | tf_op jit(solution)/shard_map/ppermute | solution.py:390
  238.3 17.3 %collective-permute-start.28 = (bf16[288,1152]{1,0:T(8,128)(2,1)}, bf16[288,1152]{1,0:T(8,128)(2,1)}, u32[]{:S(2)}, u32[]{:S(2)}) collective-permute-start(bf16[288,1152]{1,0:T(8,128)(2,1)} %slice.351), channel_id=1, source_target_pairs={{0,16},{4,20},{8,24},{12,28},{16,0},{20,4},{24,8},{28,12},{1,17},{... | collective-permute-start | bytes 1990664 | tf_op jit(solution)/shard_map/ppermute | solution.py:390
  255.5 3.2 collective-permute-start.32
  255.5 3.4 collective-permute-start.33
  287.4 172.2 %reduce-scatter.13.cloned.1.call-start = ((), (), s32[]{:S(2)}) async-start(), calls=%async_computation.9 | async-start | bytes 1843200
  317.5 18.6 %collective-permute-start.38 = (bf16[576,1152]{1,0:T(8,128)(2,1)S(1)}, bf16[576,1152]{1,0:T(8,128)(2,1)S(1)}, u32[]{:S(2)}, u32[]{:S(2)}) collective-permute-start(bf16[576,1152]{1,0:T(8,128)(2,1)S(1)} %convolution_convert_fusion.3), channel_id=1, source_target_pairs={{0,4},{4,0},{8,12},{12,8},{16,20},{20,16},{24,28},{28,24},{1,5},{5... | collective-permute-start | bytes 3981320 | tf_op jit(solution)/shard_map/ppermute | solution.py:390
  322.5 61.8 %collective-permute-start.35 = (bf16[512,1280]{1,0:T(8,128)(2,1)S(1)}, bf16[512,1280]{1,0:T(8,128)(2,1)}, u32[]{:S(2)}, u32[]{:S(2)}) collective-permute-start(bf16[512,1280]{1,0:T(8,128)(2,1)S(1)} %pad_maximum_fusion), channel_id=1, source_target_pairs={{1,0},{2,1},{3,2},{5,4},{6,5},{7,6},{9,8},{10,9},{11,10},{13,12},{... | collective-permute-start | bytes 3932168 | tf_op jit(solution)/shard_map/ppermute | solution.py:342
  325.0 59.4 %collective-permute-start.34 = (bf16[512,1280]{1,0:T(8,128)(2,1)S(1)}, bf16[512,1280]{1,0:T(8,128)(2,1)}, u32[]{:S(2)}, u32[]{:S(2)}) collective-permute-start(bf16[512,1280]{1,0:T(8,128)(2,1)S(1)} %pad_maximum_fusion), channel_id=1, source_target_pairs={{0,1},{1,2},{2,3},{4,5},{5,6},{6,7},{8,9},{9,10},{10,11},{12,13},{... | collective-permute-start | bytes 3932168 | tf_op jit(solution)/shard_map/ppermute | solution.py:341
  328.5 41.7 %collective-permute-start.37 = (bf16[256,1280]{1,0:T(8,128)(2,1)S(1)}, bf16[256,1280]{1,0:T(8,128)(2,1)S(1)}, u32[]{:S(2)}, u32[]{:S(2)}) collective-permute-start(bf16[256,1280]{1,0:T(8,128)(2,1)S(1)} %get-tuple-element.278), channel_id=1, source_target_pairs={{2,0},{3,1},{6,4},{7,5},{10,8},{11,9},{14,12},{15,13},{18,16},{19,... | collective-permute-start | bytes 1966088 | tf_op jit(solution)/shard_map/ppermute | solution.py:348
  329.8 54.6 %collective-permute-start.36 = (bf16[256,1280]{1,0:T(8,128)(2,1)S(1)}, bf16[256,1280]{1,0:T(8,128)(2,1)}, u32[]{:S(2)}, u32[]{:S(2)}) collective-permute-start(bf16[256,1280]{1,0:T(8,128)(2,1)S(1)} %get-tuple-element.279), channel_id=1, source_target_pairs={{0,2},{1,3},{4,6},{5,7},{8,10},{9,11},{12,14},{13,15},{16,18},{17,... | collective-permute-start | bytes 1966088 | tf_op jit(solution)/shard_map/ppermute | solution.py:347
  400.0 30.0 %collective-permute-start.41 = (bf16[576,3456]{1,0:T(8,128)(2,1)}, bf16[576,3456]{1,0:T(8,128)(2,1)}, u32[]{:S(2)}, u32[]{:S(2)}) collective-permute-start(bf16[576,3456]{1,0:T(8,128)(2,1)} %convolution_convert_fusion.2), channel_id=1, source_target_pairs={{0,4},{4,0},{8,12},{12,8},{16,20},{20,16},{24,28},{28,24},{1,5},{5... | collective-permute-start | bytes 11943944 | tf_op jit(solution)/shard_map/ppermute | solution.py:390
  413.6 23.2 %collective-permute-start.40 = (bf16[128,1152]{1,0:T(8,128)(2,1)S(1)}, bf16[128,1152]{1,0:T(8,128)(2,1)}, u32[]{:S(2)}, u32[]{:S(2)}) collective-permute-start(bf16[128,1152]{1,0:T(8,128)(2,1)S(1)} %slice.459), channel_id=1, source_target_pairs={{0,16},{4,20},{8,24},{12,28},{16,0},{20,4},{24,8},{28,12},{1,17},{... | collective-permute-start | bytes 884744 | tf_op jit(solution)/shard_map/ppermute | solution.py:390
  415.7 21.2 %collective-permute-start.39 = (bf16[160,1152]{1,0:T(8,128)(2,1)S(1)}, bf16[160,1152]{1,0:T(8,128)(2,1)S(1)}, u32[]{:S(2)}, u32[]{:S(2)}) collective-permute-start(bf16[160,1152]{1,0:T(8,128)(2,1)S(1)} %slice.458), channel_id=1, source_target_pairs={{0,8},{4,12},{8,0},{12,4},{16,24},{20,28},{24,16},{28,20},{1,9},{5... | collective-permute-start | bytes 1105928 | tf_op jit(solution)/shard_map/ppermute | solution.py:390
  419.0 93.6 %reduce-scatter.15.cloned.1.call-start = ((), (), s32[]{:S(2)}) async-start(), calls=%async_computation.10 | async-start | bytes 2949120
  439.7 74.1 %collective-permute-start.50 = (bf16[64,1152]{1,0:T(8,128)(2,1)}, bf16[64,1152]{1,0:T(8,128)(2,1)}, u32[]{:S(2)}, u32[]{:S(2)}) collective-permute-start(bf16[64,1152]{1,0:T(8,128)(2,1)} %add_convert_fusion.11), channel_id=1, source_target_pairs={{0,8},{4,12},{8,0},{12,4},{16,24},{20,28},{24,16},{28,20},{1,9},{5... | collective-permute-start | bytes 442376 | tf_op jit(solution)/shard_map/ppermute | solution.py:390
  441.6 27.9 %collective-permute-start.42 = (bf16[160,3456]{1,0:T(8,128)(2,1)}, bf16[160,3456]{1,0:T(8,128)(2,1)}, u32[]{:S(2)}, u32[]{:S(2)}) collective-permute-start(bf16[160,3456]{1,0:T(8,128)(2,1)} %slice.460), channel_id=1, source_target_pairs={{0,8},{4,12},{8,0},{12,4},{16,24},{20,28},{24,16},{28,20},{1,9},{5... | collective-permute-start | bytes 3317768 | tf_op jit(solution)/shard_map/ppermute | solution.py:390
  443.4 72.0 %collective-permute-start.49 = (bf16[80,1152]{1,0:T(8,128)(2,1)}, bf16[80,1152]{1,0:T(8,128)(2,1)}, u32[]{:S(2)}, u32[]{:S(2)}) collective-permute-start(bf16[80,1152]{1,0:T(8,128)(2,1)} %add_convert_fusion.9), channel_id=1, source_target_pairs={{0,16},{4,20},{8,24},{12,28},{16,0},{20,4},{24,8},{28,12},{1,17},{... | collective-permute-start | bytes 552968 | tf_op jit(solution)/shard_map/ppermute | solution.py:390
  443.5 25.2 %collective-permute-start.43 = (bf16[128,3456]{1,0:T(8,128)(2,1)}, bf16[128,3456]{1,0:T(8,128)(2,1)}, u32[]{:S(2)}, u32[]{:S(2)}) collective-permute-start(bf16[128,3456]{1,0:T(8,128)(2,1)} %slice.461), channel_id=1, source_target_pairs={{0,16},{4,20},{8,24},{12,28},{16,0},{20,4},{24,8},{28,12},{1,17},{... | collective-permute-start | bytes 2654216 | tf_op jit(solution)/shard_map/ppermute | solution.py:390
  470.9 45.7 %copy-start.44 = (bf16[160,1152]{1,0:T(8,128)(2,1)S(1)}, bf16[160,1152]{1,0:T(8,128)(2,1)}, u32[]{:S(2)}) copy-start(bf16[160,1152]{1,0:T(8,128)(2,1)} %copy-done.43) | copy-start | bytes 1105924
  474.0 46.5 %collective-permute-start.46 = (f32[20,1152]{1,0:T(8,128)S(1)}, f32[20,1152]{1,0:T(8,128)S(1)}, u32[]{:S(2)}, u32[]{:S(2)}) collective-permute-start(f32[20,1152]{1,0:T(8,128)S(1)} %stack_rows.1), channel_id=1, source_target_pairs={{0,1},{1,2},{2,3},{3,0},{4,5},{5,6},{6,7},{7,4},{8,9},{9,10},{10,1... | collective-permute-start | bytes 276488 | tf_op jit(solution)/shard_map/ppermute | solution.py:394
  474.0 46.5 %collective-permute-start.45 = (f32[20,1152]{1,0:T(8,128)S(1)}, f32[20,1152]{1,0:T(8,128)S(1)}, u32[]{:S(2)}, u32[]{:S(2)}) collective-permute-start(f32[20,1152]{1,0:T(8,128)S(1)} %stack_rows.1), channel_id=1, source_target_pairs={{0,2},{1,3},{2,0},{3,1},{4,6},{5,7},{6,4},{7,5},{8,10},{9,11},{10,... | collective-permute-start | bytes 276488 | tf_op jit(solution)/shard_map/ppermute | solution.py:394
  477.6 42.9 %collective-permute-start.44 = (f32[20,1152]{1,0:T(8,128)S(1)}, f32[20,1152]{1,0:T(8,128)S(1)}, u32[]{:S(2)}, u32[]{:S(2)}) collective-permute-start(f32[20,1152]{1,0:T(8,128)S(1)} %stack_rows.1), channel_id=1, source_target_pairs={{0,3},{1,0},{2,1},{3,2},{4,7},{5,4},{6,5},{7,6},{8,11},{9,8},{10,9... | collective-permute-start | bytes 276488 | tf_op jit(solution)/shard_map/ppermute | solution.py:394
  513.9 25.2 %collective-permute-start.47 = (bf16[80,3456]{1,0:T(8,128)(2,1)S(1)}, bf16[80,3456]{1,0:T(8,128)(2,1)S(1)}, u32[]{:S(2)}, u32[]{:S(2)}) collective-permute-start(bf16[80,3456]{1,0:T(8,128)(2,1)S(1)} %add_convert_fusion.5), channel_id=1, source_target_pairs={{0,16},{4,20},{8,24},{12,28},{16,0},{20,4},{24,8},{28,12},{1,17},{... | collective-permute-start | bytes 1658888 | tf_op jit(solution)/shard_map/ppermute | solution.py:390
  519.0 20.1 %collective-permute-start.48 = (bf16[64,3456]{1,0:T(8,128)(2,1)}, bf16[64,3456]{1,0:T(8,128)(2,1)S(1)}, u32[]{:S(2)}, u32[]{:S(2)}) collective-permute-start(bf16[64,3456]{1,0:T(8,128)(2,1)} %add_convert_fusion.7), channel_id=1, source_target_pairs={{0,8},{4,12},{8,0},{12,4},{16,24},{20,28},{24,16},{28,20},{1,9},{5... | collective-permute-start | bytes 1327112 | tf_op jit(solution)/shard_map/ppermute | solution.py:390
  523.1 13.9 %all-to-all-start = ((bf16[8,8,3672]{2,0,1:T(8,128)(2,1)}), bf16[8,8,3672]{2,0,1:T(8,128)(2,1)S(1)}, u32[]{:S(2)}, u32[]{:S(2)}) async-start(bf16[8,8,3672]{2,0,1:T(8,128)(2,1)} %pad_maximum_fusion.1), calls=%async_computation.2 | async-start | bytes 950272 | tf_op jit(solution)/shard_map/all_to_all | solution.py:816
  544.0 10.7 %collective-permute-start.51 = (bf16[144,1152]{1,0:T(8,128)(2,1)S(1)}, bf16[144,1152]{1,0:T(8,128)(2,1)S(1)}, u32[]{:S(2)}, u32[]{:S(2)}) collective-permute-start(bf16[144,1152]{1,0:T(8,128)(2,1)S(1)} %pad_maximum_fusion.3), channel_id=1, source_target_pairs={{0,1},{1,2},{2,3},{3,0},{4,5},{5,6},{6,7},{7,4},{8,9},{9,10},{10,1... | collective-permute-start | bytes 995336 | tf_op jit(solution)/shard_map/ppermute | solution.py:394
  544.6 28.9 %collective-permute-start.52 = (bf16[144,1152]{1,0:T(8,128)(2,1)S(1)}, bf16[144,1152]{1,0:T(8,128)(2,1)S(1)}, u32[]{:S(2)}, u32[]{:S(2)}) collective-permute-start(bf16[144,1152]{1,0:T(8,128)(2,1)S(1)} %pad_maximum_fusion.4), channel_id=1, source_target_pairs={{0,2},{1,3},{2,0},{3,1},{4,6},{5,7},{6,4},{7,5},{8,10},{9,11},{10,... | collective-permute-start | bytes 995336 | tf_op jit(solution)/shard_map/ppermute | solution.py:394
  545.4 29.4 %collective-permute-start.53 = (bf16[144,1152]{1,0:T(8,128)(2,1)S(1)}, bf16[144,1152]{1,0:T(8,128)(2,1)S(1)}, u32[]{:S(2)}, u32[]{:S(2)}) collective-permute-start(bf16[144,1152]{1,0:T(8,128)(2,1)S(1)} %pad_maximum_fusion.5), channel_id=1, source_target_pairs={{0,3},{1,0},{2,1},{3,2},{4,7},{5,4},{6,5},{7,6},{8,11},{9,8},{10,9... | collective-permute-start | bytes 995336 | tf_op jit(solution)/shard_map/ppermute | solution.py:394
  (83 other events, 573.9 us)
Sparse Core Ops, SparseCore 0:
  38.0 52.4 all-gather.2
  113.3 68.6 all-gather.4
  235.8 82.6 reduce-scatter.8
  321.9 82.1 reduce-scatter.10
  419.1 30.4 reduce-scatter.12
  457.5 55.0 reduce-scatter.14
